TPU v7x, 32 devices: a whole 2x2x4 slice. The times are simulated.
32 devices in a mesh: wide: 16 (over z, x, core), narrow: 2 (over y).
Axes of the slice: x: 2, y: 2, z: 4, core: 2. Of those that a mesh axis runs over, the one named last changes fastest.
Arguments:
- three_index: bfloat16 [16, 3072, 1024], P('wide', None, 'narrow'), may hold values from -0.59765625 to 0.59765625
- orbital_map: int32 [16], replicated, may hold values from 0 to 15, each once
- occ_energy: float32 [16], replicated, may hold values from -2 to -0.3
- vir_energy: float32 [1024], replicated, may hold values from 0.2 to 3
- pair_kept: int32 [6, 16], P(None, 'wide'), may hold values 0 or 1
Outputs:
- density: float32 [16, 3072, 1024], P('wide', None, 'narrow')
Inputs may be any that keep to these rules, and one draw needn't show every extreme that they name: `orbital_map`: each of the 16 orbitals once.
All inputs are finite; a program needn't handle non-finite values. No bound on the sum of `pair_kept` on one device may be relied on, other than what follows from the above.
Results may differ from a plain program's by a relative error of at most 0.0015.
Values may be sent and summed in bfloat16 or wider, within the bound.
No kernel may reach another device: no remote copies, remote signals or barrier semaphores. Data moves between devices by JAX's collectives and lax.ppermute only.
A program may use at most 192 MiB of HBM per device.

v0:
```python
import jax
import jax.numpy as jnp
from jax import lax
from jax.sharding import PartitionSpec as P

ROUNDS = 5


def passed_along(array, axis, by):
    length = lax.axis_size(axis)
    return lax.ppermute(array, axis, [(i, (i + by) % length) for i in range(length)])


def block_energy(orbital_map, occ_energy, block_id, occ_count):
    orbits = lax.dynamic_slice_in_dim(orbital_map, block_id * occ_count, occ_count)
    labels = jnp.arange(occ_energy.shape[0], dtype=jnp.int32)
    chosen = orbits[:, None] == labels[None, :]
    return jnp.sum(jnp.where(chosen, occ_energy[None, :], 0.0), axis=1)


def amplitudes(gathered, visiting, left_energy, right_energy, vir_all, vir_local, weight):
    coulomb = jnp.einsum("ipa,jpb->ijab", gathered, visiting, preferred_element_type=jnp.float32)
    denominator = (vir_all[:, None] + vir_local[None, :])[None, None] - (
        left_energy[:, None] + right_energy[None, :]
    )[:, :, None, None]
    return (weight * coulomb / denominator).astype(jnp.bfloat16)


def per_device(three_index, orbital_map, occ_energy, vir_energy, pair_kept):
    occ_count = three_index.shape[0]
    vir_count = three_index.shape[2]
    blocks = lax.axis_size("wide")
    own_block = lax.axis_index("wide")
    vir_local = lax.dynamic_slice_in_dim(
        vir_energy, lax.axis_index("narrow") * vir_count, vir_count
    )
    own_energy = block_energy(orbital_map, occ_energy, own_block, occ_count)
    weights = pair_kept.astype(jnp.float32)
    gathered = lax.all_gather(three_index, "narrow", axis=2, tiled=True)
    amplitude = amplitudes(
        gathered, three_index, own_energy, own_energy, vir_energy, vir_local, weights[0, 0]
    )
    forward = jnp.einsum(
        "ijab,jpb->ipa", amplitude, three_index, preferred_element_type=jnp.float32
    )
    visiting = three_index
    stored_amps = []
    for round_index in range(1, ROUNDS + 1):
        visiting = passed_along(visiting, "wide", 1)
        partner = (own_block - round_index) % blocks
        partner_energy = block_energy(orbital_map, occ_energy, partner, occ_count)
        amplitude = amplitudes(
            gathered,
            visiting,
            own_energy,
            partner_energy,
            vir_energy,
            vir_local,
            weights[round_index, 0],
        )
        forward = forward + jnp.einsum(
            "ijab,jpb->ipa", amplitude, visiting, preferred_element_type=jnp.float32
        )
        stored_amps.append(amplitude)
    carried = None
    for round_index in range(1, ROUNDS + 1):
        backward = jnp.einsum(
            "ijab,ipa->jpb",
            stored_amps[round_index - 1],
            gathered,
            preferred_element_type=jnp.float32,
        )
        if round_index > 1:
            carried = passed_along(carried, "wide", 1) + backward
        else:
            carried = backward
    returned = passed_along(carried, "wide", -ROUNDS)
    scattered = lax.psum_scatter(forward, "narrow", scatter_dimension=2, tiled=True)
    return scattered + returned


def solution(mesh):
    placed = (P("wide", None, "narrow"), P(), P(), P(), P(None, "wide"))
    return jax.shard_map(
        per_device, mesh=mesh, in_specs=placed, out_specs=P("wide", None, "narrow"), check_vma=False
    )
```

profile of v0, /device:TPU:3, one launch (start us, length us, event | category | flops | bytes accessed | tf_op | source)
XLA Modules:
  0.0 705.9 jit_solution(2828249982948608496)
XLA Ops:
  6.5 0.0 all-gather.2.cloned.1.call-start
  6.6 1.9 collective-permute-start
  8.5 0.0 all-gather.2.cloned.1.call-update
  8.5 0.0 reduce-scatter.2.cloned.1.call-start
  8.5 34.5 %collective-permute-done = bf16[1,3072,512]{2,1,0:T(8,128)(2,1)} collective-permute-done((bf16[1,3072,512]{2,1,0:T(8,128)(2,1)}, bf16[1,3072,512]{2,1,0:T(8,128)(2,1)}, u32[]{:S(2)}, u32[]{:S(2)}) %collective-permute-start) | collective-permute-done | bytes 3145760 | tf_op jit(solution)/shard_map/ppermute | solution.py:11
  43.0 3.4 collective-permute-start.1
  46.4 0.7 fusion.125
  47.1 4.4 fusion.123
  52.6 0.1 dynamic_slice.21
  52.7 0.7 fusion.124
  53.3 27.6 %collective-permute-done.1 = bf16[1,3072,512]{2,1,0:T(8,128)(2,1)} collective-permute-done((bf16[1,3072,512]{2,1,0:T(8,128)(2,1)}, bf16[1,3072,512]{2,1,0:T(8,128)(2,1)}, u32[]{:S(2)}, u32[]{:S(2)}) %collective-permute-start.1) | collective-permute-done | bytes 3145760 | tf_op jit(solution)/shard_map/ppermute | solution.py:11
  80.9 3.4 collective-permute-start.2
  84.3 6.3 all-gather.2.cloned.1.call-done
  90.6 8.1 %fusion.100 = bf16[1024,512]{0,1:T(8,128)(2,1)S(1)} fusion(bf16[1,3072,1024]{2,1,0:T(8,128)(2,1)} %all-gather.2.cloned.1.call-done, bf16[1,3072,512]{2,1,0:T(8,128)(2,1)} %collective-permute-done, f32[]{:T(128)S(6)} %add.194, f32[]{:T(128)} %bitcast.7, f32[512]{0:T(512)S(1)} %dynamic_slice.21, f32[1024]{0:T(1024)S(1)} %copy-done.2), kind=kOutput, calls=%fused_computation.67 | convolution fusion | flops 3223846912 | bytes 10491912 | tf_op jit(solution)/shard_map/ipa,jpb->ijab/dot_general | solution.py:22
  98.7 5.4 fusion.22
  104.1 1.8 collective-permute-start.5
  111.6 8.5 %fusion.38 = f32[1024,3072]{1,0:T(8,128)} fusion(bf16[1024,512]{0,1:T(8,128)(2,1)S(1)} %fusion.100, bf16[1,3072,512]{2,1,0:T(8,128)(2,1)} %collective-permute-done), kind=kOutput, calls=%fused_computation.45 | convolution fusion | flops 3221225472 | bytes 16777216 | tf_op jit(solution)/shard_map/ijab,jpb->ipa/dot_general | solution.py:61
  120.1 5.9 fusion.95
  126.1 0.2 collective-permute-start.3
  126.3 8.8 %fusion.35 = f32[1024,3072]{1,0:T(8,128)} fusion(bf16[1024,512]{0,1:T(8,128)(2,1)S(1)} %fusion.95, bf16[1,3072,512]{2,1,0:T(8,128)(2,1)} %collective-permute-done.1), kind=kOutput, calls=%fused_computation.42 | convolution fusion | flops 3221225472 | bytes 16777216 | tf_op jit(solution)/shard_map/ijab,jpb->ipa/dot_general | solution.py:61
  135.1 12.5 %fusion.41 = f32[1024,3072]{1,0:T(8,128)} fusion(bf16[1,3072,512]{2,1,0:T(8,128)(2,1)S(1)} %copy-done, bf16[1,3072,1024]{2,1,0:T(8,128)(2,1)} %all-gather.2.cloned.1.call-done, f32[]{:T(128)S(6)} %add.191, f32[512]{0:T(512)S(1)} %dynamic_slice.21, f32[1024]{0:T(1024)S(1)} %copy-done.2, f32[]{:T(128)} %bitcast), kind=kOutput, calls=%fused_computation.48 | convolution fusion | flops 6445072384 | bytes 22026248 | tf_op jit(solution)/shard_map/ijab,jpb->ipa/dot_general | solution.py:43
  147.6 8.4 %fusion.90 = bf16[1024,512]{0,1:T(8,128)(2,1)S(1)} fusion(bf16[1,3072,1024]{2,1,0:T(8,128)(2,1)} %all-gather.2.cloned.1.call-done, bf16[1,3072,512]{2,1,0:T(8,128)(2,1)} %collective-permute-done.2, f32[]{:T(128)S(6)} %add.202, f32[]{:T(128)} %bitcast.19, f32[512]{0:T(512)S(1)} %dynamic_slice.21, f32[1024]{0:T(1024)S(1)} %copy-done.2), kind=kOutput, calls=%fused_computation.65 | convolution fusion | flops 3223846912 | bytes 10491912 | tf_op jit(solution)/shard_map/ipa,jpb->ijab/dot_general | solution.py:22
  156.0 63.9 %collective-permute-done.3 = bf16[1,3072,512]{2,1,0:T(8,128)(2,1)} collective-permute-done((bf16[1,3072,512]{2,1,0:T(8,128)(2,1)}, bf16[1,3072,512]{2,1,0:T(8,128)(2,1)}, u32[]{:S(2)}, u32[]{:S(2)}) %collective-permute-start.3) | collective-permute-done | bytes 3145760 | tf_op jit(solution)/shard_map/ppermute | solution.py:11
  219.9 3.4 collective-permute-start.4
  223.3 8.2 %fusion.32 = f32[1024,3072]{1,0:T(8,128)} fusion(bf16[1024,512]{0,1:T(8,128)(2,1)S(1)} %fusion.90, bf16[1,3072,512]{2,1,0:T(8,128)(2,1)} %collective-permute-done.2), kind=kOutput, calls=%fused_computation.39 | convolution fusion | flops 3221225472 | bytes 16777216 | tf_op jit(solution)/shard_map/ijab,jpb->ipa/dot_general | solution.py:61
  231.6 7.3 %bitcast_add_fusion.3 = f32[1,3072,512]{1,2,0:T(8,128)} fusion(f32[1,3072,512]{1,2,0:T(8,128)} %collective-permute-done.5, bf16[1024,512]{0,1:T(8,128)(2,1)S(1)} %copy-done.11, bf16[1,3072,1024]{2,1,0:T(8,128)(2,1)S(1)} %bitcast.208), kind=kOutput, calls=%fused_computation.10 | convolution fusion | flops 3222798336 | bytes 19922944 | tf_op jit(solution)/shard_map/ijab,ipa->jpb/dot_general | solution.py:67
  238.9 0.2 collective-permute-start.6
  239.1 6.0 fusion.85
  245.1 8.6 %fusion.29 = f32[1024,3072]{1,0:T(8,128)} fusion(bf16[1024,512]{0,1:T(8,128)(2,1)S(1)} %fusion.85, bf16[1,3072,512]{2,1,0:T(8,128)(2,1)} %collective-permute-done.3), kind=kOutput, calls=%fused_computation.36 | convolution fusion | flops 3221225472 | bytes 16777216 | tf_op jit(solution)/shard_map/ijab,jpb->ipa/dot_general | solution.py:61
  253.7 4.2 collective-permute-done.4
  257.8 5.3 fusion.80
  263.1 26.5 %add_bitcast_fusion = f32[1,3072,1024]{1,2,0:T(8,128)} fusion(f32[1024,3072]{1,0:T(8,128)} %fusion.29, f32[1024,3072]{1,0:T(8,128)} %fusion.32, f32[1024,3072]{1,0:T(8,128)} %fusion.35, f32[1024,3072]{1,0:T(8,128)} %fusion.41, f32[1024,3072]{1,0:T(8,128)} %fusion.38, bf16[1024,512]{0,1:T(8,128)(2,1)} %fusion.80, ...), kind=kOutput, calls=%fused_computation | convolution fusion | flops 3236954112 | bytes 79691776 | tf_op jit(solution)/shard_map/ijab,jpb->ipa/dot_general | solution.py:61
  289.7 1.2 copy-done.8
  290.9 5.6 fusion.4
  296.5 28.8 %collective-permute-done.6 = f32[1,3072,512]{1,2,0:T(8,128)} collective-permute-done((f32[1,3072,512]{1,2,0:T(8,128)}, f32[1,3072,512]{1,2,0:T(8,128)}, u32[]{:S(2)}, u32[]{:S(2)}) %collective-permute-start.6) | collective-permute-done | bytes 6291488 | tf_op jit(solution)/shard_map/ppermute | solution.py:11
  325.3 3.9 bitcast_add_fusion.2
  329.2 3.7 collective-permute-start.7
  332.9 5.9 fusion.2
  338.7 62.0 %collective-permute-done.7 = f32[1,3072,512]{1,2,0:T(8,128)S(1)} collective-permute-done((f32[1,3072,512]{1,2,0:T(8,128)S(1)}, f32[1,3072,512]{1,2,0:T(8,128)S(1)}, u32[]{:S(2)}, u32[]{:S(2)}) %collective-permute-start.7) | collective-permute-done | bytes 6291488 | tf_op jit(solution)/shard_map/ppermute | solution.py:11
  400.8 1.6 bitcast_add_fusion.1
  402.4 3.4 collective-permute-start.8
  405.8 6.1 fusion
  411.9 61.8 %collective-permute-done.8 = f32[1,3072,512]{1,2,0:T(8,128)S(1)} collective-permute-done((f32[1,3072,512]{1,2,0:T(8,128)S(1)}, f32[1,3072,512]{1,2,0:T(8,128)S(1)}, u32[]{:S(2)}, u32[]{:S(2)}) %collective-permute-start.8) | collective-permute-done | bytes 6291488 | tf_op jit(solution)/shard_map/ppermute | solution.py:11
  473.7 1.6 bitcast_add_fusion
  475.4 0.1 collective-permute-start.9
  475.5 207.8 %collective-permute-done.9 = f32[1,3072,512]{1,2,0:T(8,128)} collective-permute-done((f32[1,3072,512]{1,2,0:T(8,128)S(1)}, f32[1,3072,512]{1,2,0:T(8,128)}, u32[]{:S(2)}, u32[]{:S(2)}) %collective-permute-start.9) | collective-permute-done | bytes 6291488 | tf_op jit(solution)/shard_map/ppermute | solution.py:11
  683.3 8.8 %add.218 = f32[1,3072,512]{1,2,0:T(8,128)} add(f32[1,3072,512]{1,2,0:T(8,128)} %reduce-scatter.2.cloned.1.call-done, f32[1,3072,512]{1,2,0:T(8,128)} %collective-permute-done.9) | non-fusion elementwise | flops 1572864 | bytes 18874368 | tf_op jit(solution)/shard_map/add | solution.py:79
  692.1 6.6 copy.6
  (33 shorter events, 0.1 us)
Async XLA Ops:
  6.5 39.8 %copy-start.6 = (s32[6,1]{0,1:T(1,128)S(1)}, s32[6,1]{0,1:T(1,128)}, u32[]{:S(2)}) copy-start(s32[6,1]{0,1:T(1,128)} %param.9) | copy-start | bytes 76
  6.5 39.8 %copy-start.1 = (s32[16]{0:T(128)S(1)}, s32[16]{0:T(128)}, u32[]{:S(2)}) copy-start(s32[16]{0:T(128)} %param.6) | copy-start | bytes 196
  6.5 40.5 %copy-start.3 = (f32[16]{0:T(128)S(1)}, f32[16]{0:T(128)}, u32[]{:S(2)}) copy-start(f32[16]{0:T(128)} %param.7) | copy-start | bytes 196
  6.5 46.1 %copy-start.2 = (f32[1024]{0:T(1024)S(1)}, f32[1024]{0:T(1024)}, u32[]{:S(2)}) copy-start(f32[1024]{0:T(1024)} %param.8) | copy-start | bytes 12292
  6.5 84.0 %all-gather.2.cloned.1.call-start = ((), (), s32[]{:S(2)}) async-start(), calls=%async_computation.1 | async-start | bytes 9437184 | tf_op jit(solution)/shard_map/all_gather | solution.py:39
  6.6 36.4 %collective-permute-start = (bf16[1,3072,512]{2,1,0:T(8,128)(2,1)}, bf16[1,3072,512]{2,1,0:T(8,128)(2,1)}, u32[]{:S(2)}, u32[]{:S(2)}) collective-permute-start(bf16[1,3072,512]{2,1,0:T(8,128)(2,1)} %param.5), channel_id=1, source_target_pairs={{0,2},{2,4},{4,6},{6,8},{8,10},{10,12},{12,14},{14,16},{16,18},{18... | collective-permute-start | bytes 9437192 | tf_op jit(solution)/shard_map/ppermute | solution.py:11
  8.5 674.8 %reduce-scatter.2.cloned.1.call-start = ((), (), s32[]{:S(2)}) async-start(), calls=%async_computation.2 | async-start | bytes 18874368 | tf_op jit(solution)/shard_map/reduce_scatter | solution.py:78
  43.0 37.9 %collective-permute-start.1 = (bf16[1,3072,512]{2,1,0:T(8,128)(2,1)}, bf16[1,3072,512]{2,1,0:T(8,128)(2,1)}, u32[]{:S(2)}, u32[]{:S(2)}) collective-permute-start(bf16[1,3072,512]{2,1,0:T(8,128)(2,1)} %collective-permute-done), channel_id=1, source_target_pairs={{0,2},{2,4},{4,6},{6,8},{8,10},{10,12},{12,14},{14,16},{16,18},{18... | collective-permute-start | bytes 9437192 | tf_op jit(solution)/shard_map/ppermute | solution.py:11
  80.9 45.2 %collective-permute-start.2 = (bf16[1,3072,512]{2,1,0:T(8,128)(2,1)}, bf16[1,3072,512]{2,1,0:T(8,128)(2,1)}, u32[]{:S(2)}, u32[]{:S(2)}) collective-permute-start(bf16[1,3072,512]{2,1,0:T(8,128)(2,1)} %collective-permute-done.1), channel_id=1, source_target_pairs={{0,2},{2,4},{4,6},{6,8},{8,10},{10,12},{12,14},{14,16},{16,18},{18... | collective-permute-start | bytes 9437192 | tf_op jit(solution)/shard_map/ppermute | solution.py:11
  90.6 8.1 %copy-start.4 = (bf16[1,3072,1024]{2,1,0:T(8,128)(2,1)S(1)}, bf16[1,3072,1024]{2,1,0:T(8,128)(2,1)}, u32[]{:S(2)}) copy-start(bf16[1,3072,1024]{2,1,0:T(8,128)(2,1)} %all-gather.2.cloned.1.call-done) | copy-start | bytes 18874372
  104.1 127.5 %collective-permute-start.5 = (f32[1,3072,512]{1,2,0:T(8,128)}, f32[1,3072,512]{1,2,0:T(8,128)}, u32[]{:S(2)}, u32[]{:S(2)}) collective-permute-start(f32[1,3072,512]{1,2,0:T(8,128)} %fusion.22), channel_id=1, source_target_pairs={{0,2},{2,4},{4,6},{6,8},{8,10},{10,12},{12,14},{14,16},{16,18},{18... | collective-permute-start | bytes 18874376 | tf_op jit(solution)/shard_map/ppermute | solution.py:11
  111.6 8.5 %copy-start.5 = (bf16[1,3072,1024]{2,1,0:T(8,128)(2,1)S(1)}, bf16[1,3072,1024]{2,1,0:T(8,128)(2,1)}, u32[]{:S(2)}) copy-start(bf16[1,3072,1024]{2,1,0:T(8,128)(2,1)} %all-gather.2.cloned.1.call-done) | copy-start | bytes 18874372
  126.0 9.0 %copy-start.10 = (bf16[1024,512]{0,1:T(8,128)(2,1)}, bf16[1024,512]{0,1:T(8,128)(2,1)S(1)}, u32[]{:S(2)}) copy-start(bf16[1024,512]{0,1:T(8,128)(2,1)S(1)} %fusion.95) | copy-start | bytes 3145732
  126.1 9.0 %copy-start = (bf16[1,3072,512]{2,1,0:T(8,128)(2,1)S(1)}, bf16[1,3072,512]{2,1,0:T(8,128)(2,1)}, u32[]{:S(2)}) copy-start(bf16[1,3072,512]{2,1,0:T(8,128)(2,1)} %param.5) | copy-start | bytes 9437188
  126.1 93.9 %collective-permute-start.3 = (bf16[1,3072,512]{2,1,0:T(8,128)(2,1)}, bf16[1,3072,512]{2,1,0:T(8,128)(2,1)}, u32[]{:S(2)}, u32[]{:S(2)}) collective-permute-start(bf16[1,3072,512]{2,1,0:T(8,128)(2,1)} %collective-permute-done.2), channel_id=1, source_target_pairs={{0,2},{2,4},{4,6},{6,8},{8,10},{10,12},{12,14},{14,16},{16,18},{18... | collective-permute-start | bytes 9437192 | tf_op jit(solution)/shard_map/ppermute | solution.py:11
  147.6 83.9 %slice-start = ((s8[6291456]{0:T(1024)(128)(4,1)}), s8[4194304]{0:T(1024)(128)(4,1)S(1)}, s32[]{:S(2)}) async-start(s8[6291456]{0:T(1024)(128)(4,1)} %bitcast.207), calls=%async_computation.3 | async-start | bytes 8388608
  147.6 83.9 %slice-start.1 = ((s8[6291456]{0:T(1024)(128)(4,1)}), s8[2097152]{0:T(1024)(128)(4,1)S(1)}, s32[]{:S(2)}) async-start(s8[6291456]{0:T(1024)(128)(4,1)} %bitcast.207), calls=%async_computation.4 | async-start | bytes 4194304
  156.0 75.5 %copy-start.7 = (bf16[1024,512]{0,1:T(8,128)(2,1)}, bf16[1024,512]{0,1:T(8,128)(2,1)S(1)}, u32[]{:S(2)}) copy-start(bf16[1024,512]{0,1:T(8,128)(2,1)S(1)} %fusion.90) | copy-start | bytes 3145732
  156.0 75.6 %copy-start.11 = (bf16[1024,512]{0,1:T(8,128)(2,1)S(1)}, bf16[1024,512]{0,1:T(8,128)(2,1)}, u32[]{:S(2)}) copy-start(bf16[1024,512]{0,1:T(8,128)(2,1)} %copy-done.10) | copy-start | bytes 3145732
  219.9 37.9 %collective-permute-start.4 = (bf16[1,3072,512]{2,1,0:T(8,128)(2,1)}, bf16[1,3072,512]{2,1,0:T(8,128)(2,1)S(1)}, u32[]{:S(2)}, u32[]{:S(2)}) collective-permute-start(bf16[1,3072,512]{2,1,0:T(8,128)(2,1)} %collective-permute-done.3), channel_id=1, source_target_pairs={{0,2},{2,4},{4,6},{6,8},{8,10},{10,12},{12,14},{14,16},{16,18},{18... | collective-permute-start | bytes 9437192 | tf_op jit(solution)/shard_map/ppermute | solution.py:11
  238.9 86.4 %collective-permute-start.6 = (f32[1,3072,512]{1,2,0:T(8,128)}, f32[1,3072,512]{1,2,0:T(8,128)}, u32[]{:S(2)}, u32[]{:S(2)}) collective-permute-start(f32[1,3072,512]{1,2,0:T(8,128)} %bitcast_add_fusion.3), channel_id=1, source_target_pairs={{0,2},{2,4},{4,6},{6,8},{8,10},{10,12},{12,14},{14,16},{16,18},{18... | collective-permute-start | bytes 18874376 | tf_op jit(solution)/shard_map/ppermute | solution.py:11
  245.1 8.6 %copy-start.9 = (bf16[1024,512]{0,1:T(8,128)(2,1)}, bf16[1024,512]{0,1:T(8,128)(2,1)S(1)}, u32[]{:S(2)}) copy-start(bf16[1024,512]{0,1:T(8,128)(2,1)S(1)} %fusion.85) | copy-start | bytes 3145732
  289.6 1.2 copy-start.8
  329.2 71.6 %collective-permute-start.7 = (f32[1,3072,512]{1,2,0:T(8,128)S(1)}, f32[1,3072,512]{1,2,0:T(8,128)S(1)}, u32[]{:S(2)}, u32[]{:S(2)}) collective-permute-start(f32[1,3072,512]{1,2,0:T(8,128)S(1)} %bitcast_add_fusion.2), channel_id=1, source_target_pairs={{0,2},{2,4},{4,6},{6,8},{8,10},{10,12},{12,14},{14,16},{16,18},{18... | collective-permute-start | bytes 18874376 | tf_op jit(solution)/shard_map/ppermute | solution.py:11
  402.4 71.4 %collective-permute-start.8 = (f32[1,3072,512]{1,2,0:T(8,128)S(1)}, f32[1,3072,512]{1,2,0:T(8,128)S(1)}, u32[]{:S(2)}, u32[]{:S(2)}) collective-permute-start(f32[1,3072,512]{1,2,0:T(8,128)S(1)} %bitcast_add_fusion.1), channel_id=1, source_target_pairs={{0,2},{2,4},{4,6},{6,8},{8,10},{10,12},{12,14},{14,16},{16,18},{18... | collective-permute-start | bytes 18874376 | tf_op jit(solution)/shard_map/ppermute | solution.py:11
  475.4 207.9 %collective-permute-start.9 = (f32[1,3072,512]{1,2,0:T(8,128)S(1)}, f32[1,3072,512]{1,2,0:T(8,128)}, u32[]{:S(2)}, u32[]{:S(2)}) collective-permute-start(f32[1,3072,512]{1,2,0:T(8,128)S(1)} %bitcast_add_fusion), channel_id=1, source_target_pairs={{0,22},{2,24},{4,26},{6,28},{8,30},{10,0},{12,2},{14,4},{16,6},{18... | collective-permute-start | bytes 18874376 | tf_op jit(solution)/shard_map/ppermute | solution.py:11
Sparse Core Ops, SparseCore 0:
  8.9 81.5 all-gather.1
  289.8 150.3 reduce-scatter.1
where the time goes:
time: 714 us; the launch traced here: 706 us
  waiting for transfers between devices  497 us (70%)
  matrix products  137 us (19%)
  starting transfers between devices  21.5 us (3%)
  between operations  21 us (3%)
  other arithmetic  20.3 us (3%)
  local copies, waits for them, and re-layouts  9.23 us (1%)
    ppermute x10, waiting for transfers between devices, passed_along(): lax.ppermute(array, axis, [(i, (i + by) % length) for i in range(length)])  491 us
    dot_general x5, matrix products, per_device(): jnp.einsum('ijab,jpb->ipa', amplitude, visiting, preferred_element_type=j...  60.5 us
    dot_general x5, matrix products, amplitudes(): jnp.einsum('ipa,jpb->ijab', gathered, visiting, preferred_element_type=jn...  33.7 us
    dot_general x5, matrix products, per_device(): jnp.einsum('ijab,ipa->jpb', stored_amps[round_index - 1], gathered, prefe...  30.2 us
    ppermute x10, starting transfers between devices, passed_along(): lax.ppermute(array, axis, [(i, (i + by) % length) for i in range(length)])  21.4 us
  transfers between devices with their start and end apart: 12, of which 9 were waited for; matrix products, arithmetic and copies ran while one was open for 21% of the time, Pallas kernels for 0%

commit v1 on v0

--- a/solution.py
+++ b/solution.py
@@ -1,9 +1,13 @@
 import jax
 import jax.numpy as jnp
+import numpy as np
 from jax import lax
+from jax.experimental import pallas as pl
+from jax.experimental.pallas import tpu as pltpu
 from jax.sharding import PartitionSpec as P
 
 ROUNDS = 5
+VMEM = 56 * 1024 * 1024
 
 
 def passed_along(array, axis, by):
@@ -26,7 +30,7 @@
     return (weight * coulomb / denominator).astype(jnp.bfloat16)
 
 
-def per_device(three_index, orbital_map, occ_energy, vir_energy, pair_kept):
+def ring_plan(three_index, orbital_map, occ_energy, vir_energy, pair_kept):
     occ_count = three_index.shape[0]
     vir_count = three_index.shape[2]
     blocks = lax.axis_size("wide")
@@ -79,7 +83,235 @@
     return scattered + returned
 
 
+class Routes:
+    def __init__(self, blocks):
+        self.blocks = blocks
+        self.own = list(range(blocks))
+        lead = [self.leads(w) for w in range(blocks)]
+        self.lead = np.array(lead)
+        self.swap = [(w, w ^ 1) for w in range(blocks)]
+
+        def hop(step, by_lead):
+            pairs = []
+            for w in range(blocks):
+                along_z = lead[w] == by_lead
+                pairs.append((w, self.along_z(w, step) if along_z else self.across_x(w)))
+            return pairs
+
+        self.pairs = [hop(1, True), hop(1, False), hop(-1, True), hop(-1, False), hop(-1, True)]
+
+    def place(self, w):
+        return w // 4, (w // 2) % 2, w % 2
+
+    def leads(self, w):
+        _, x, core = self.place(w)
+        return x == core
+
+    def along_z(self, w, step):
+        z, x, core = self.place(w)
+        z = (z + (step if x == 1 else -step)) % (self.blocks // 4)
+        return (z * 2 + x) * 2 + core
+
+    def across_x(self, w):
+        z, x, core = self.place(w)
+        return (z * 2 + 1 - x) * 2 + 1 - core
+
+    def moved(self, ids, pairs):
+        out = [0] * self.blocks
+        for source, target in pairs:
+            out[target] = ids[source]
+        return out
+
+    def chosen(self, ids_lead, ids_other):
+        return [a if lead else b for lead, a, b in zip(self.lead, ids_lead, ids_other)]
+
+
+class Slab:
+    def __init__(self, array, ids):
+        self.array = array
+        self.ids = ids
+
+
+def tile_of(length, most):
+    size = min(length, most)
+    while length % size:
+        size -= 8
+    return size
+
+
+def amplitude_kernel(scalars, rows, slab, vir_rows, vir_cols, out):
+    coulomb = jnp.dot(rows[...], slab[...], preferred_element_type=jnp.float32)
+    denominator = (vir_rows[...] + vir_cols[...]) - scalars[0, 0]
+    out[...] = (scalars[0, 1] * coulomb / denominator).astype(out.dtype)
+
+
+def amplitude_call(scalars, turned, slab, vir_rows, vir_cols):
+    rows, aux = turned.shape
+    cols = slab.shape[1]
+    tile = tile_of(rows, 256)
+    return pl.pallas_call(
+        amplitude_kernel,
+        grid=(rows // tile,),
+        in_specs=[
+            pl.BlockSpec(memory_space=pltpu.SMEM),
+            pl.BlockSpec((tile, aux), lambda i: (i, 0)),
+            pl.BlockSpec((aux, cols), lambda i: (0, 0)),
+            pl.BlockSpec((tile, 1), lambda i: (i, 0)),
+            pl.BlockSpec((1, cols), lambda i: (0, 0)),
+        ],
+        out_specs=pl.BlockSpec((tile, cols), lambda i: (i, 0)),
+        out_shape=jax.ShapeDtypeStruct((rows, cols), jnp.bfloat16),
+        compiler_params=pltpu.CompilerParams(vmem_limit_bytes=VMEM),
+        cost_estimate=pl.CostEstimate(
+            flops=2 * rows * aux * cols,
+            bytes_accessed=2 * (rows * aux + aux * cols + rows * cols),
+            transcendentals=0,
+        ),
+    )(scalars, turned, slab, vir_rows, vir_cols)
+
+
+def density_call(slabs, amps, parts, out_dtype):
+    count = len(slabs)
+    aux, depth = slabs[0].shape
+    cols = amps[0].shape[0]
+    tile = tile_of(aux, 256)
+
+    def kernel(*refs):
+        out = refs[-1]
+        total = None
+        for ref in refs[2 * count : -1]:
+            part = ref[...].astype(jnp.float32)
+            total = part if total is None else total + part
+        for slab, amp in zip(refs[:count], refs[count : 2 * count]):
+            term = lax.dot_general(
+                slab[...], amp[...], (((1,), (1,)), ((), ())), preferred_element_type=jnp.float32
+            )
+            total = term if total is None else total + term
+        out[...] = total.astype(out.dtype)
+
+    bytes_in = sum(x.size * x.dtype.itemsize for x in (*slabs, *amps, *parts))
+    return pl.pallas_call(
+        kernel,
+        grid=(aux // tile,),
+        in_specs=[pl.BlockSpec((tile, depth), lambda i: (i, 0))] * count
+        + [pl.BlockSpec((cols, depth), lambda i: (0, 0))] * count
+        + [pl.BlockSpec((tile, cols), lambda i: (i, 0))] * len(parts),
+        out_specs=pl.BlockSpec((tile, cols), lambda i: (i, 0)),
+        out_shape=jax.ShapeDtypeStruct((aux, cols), out_dtype),
+        compiler_params=pltpu.CompilerParams(vmem_limit_bytes=VMEM),
+        cost_estimate=pl.CostEstimate(
+            flops=2 * aux * depth * cols * count,
+            bytes_accessed=bytes_in + aux * cols * jnp.dtype(out_dtype).itemsize,
+            transcendentals=0,
+        ),
+    )(*slabs, *amps, *parts)
+
+
+def paired_plan(three_index, orbital_map, occ_energy, vir_energy, pair_kept):
+    blocks = lax.axis_size("wide")
+    routes = Routes(blocks)
+    here = lax.axis_index("wide")
+    side = lax.axis_index("narrow")
+    vir_count = three_index.shape[2]
+    lead = jnp.asarray(routes.lead)[here]
+
+    def moved(slab, pairs):
+        return Slab(lax.ppermute(slab.array, "wide", pairs), routes.moved(slab.ids, pairs))
+
+    def swapped(slab):
+        return moved(slab, routes.swap)
+
+    def chosen(slab_lead, slab_other):
+        return Slab(
+            jnp.where(lead, slab_lead.array, slab_other.array),
+            routes.chosen(slab_lead.ids, slab_other.ids),
+        )
+
+    def sibling(array):
+        return lax.ppermute(array, "narrow", [(0, 1), (1, 0)])
+
+    labels = jnp.arange(occ_energy.shape[0], dtype=jnp.int32)
+    picked = orbital_map[:, None] == labels[None, :]
+    energy = jnp.sum(jnp.where(picked, occ_energy[None, :], 0.0), axis=1)
+    kept = lax.all_gather(pair_kept.astype(jnp.float32), "wide", axis=1, tiled=True)
+
+    def scalars(slab):
+        block = jnp.asarray(np.array(slab.ids, np.int32))[here]
+        ahead = (here - block) % blocks
+        behind = (block - here) % blocks
+        weight = jnp.where(
+            ahead <= ROUNDS,
+            kept[jnp.minimum(ahead, ROUNDS), here],
+            kept[jnp.minimum(behind, ROUNDS), block],
+        )
+        return jnp.stack([energy[here] + energy[block], weight]).reshape(1, 2)
+
+    vir_near = lax.dynamic_slice_in_dim(vir_energy, side * vir_count, vir_count)
+    vir_far = lax.dynamic_slice_in_dim(vir_energy, (1 - side) * vir_count, vir_count)
+    near_rows, near_cols = vir_near[:, None], vir_near[None, :]
+    far_rows, far_cols = vir_far[:, None], vir_far[None, :]
+
+    own = Slab(three_index[0], routes.own)
+    r1 = moved(own, routes.pairs[0])
+    own_far = Slab(sibling(own.array), routes.own)
+    mate = swapped(own)
+    s1 = swapped(r1)
+    r2 = moved(chosen(r1, own), routes.pairs[1])
+    s2 = swapped(r2)
+    r3 = moved(chosen(mate, r2), routes.pairs[2])
+    s3 = swapped(r3)
+    r4 = moved(chosen(r3, s2), routes.pairs[3])
+    s4 = swapped(r4)
+    mate_far = swapped(own_far)
+    r5 = moved(chosen(own, mate), routes.pairs[4])
+    s5 = swapped(r5)
+    r6 = moved(chosen(own_far, mate_far), routes.pairs[4])
+    s6 = swapped(r6)
+
+    turned = own.array.T
+    turned_far = own_far.array.T
+
+    def near_amp(slab):
+        return amplitude_call(scalars(slab), turned, slab.array, near_rows, near_cols)
+
+    def far_amp(slab):
+        return amplitude_call(scalars(slab), turned_far, slab.array, far_rows, near_cols)
+
+    def near_amp_of_far(slab):
+        return amplitude_call(scalars(slab), turned, slab.array, near_rows, far_cols)
+
+    early = [r1, s1, r2, s2, r3, s3, s4]
+    outgoing = density_call(
+        [s.array for s in early], [far_amp(s) for s in early], [], jnp.bfloat16
+    )
+    incoming = sibling(outgoing)
+    held = early + [own, mate, r5, s5]
+    held_far = [own_far, mate_far]
+    partial = density_call(
+        [s.array for s in held + held_far],
+        [near_amp(s) for s in held] + [near_amp_of_far(s) for s in held_far],
+        [],
+        jnp.float32,
+    )
+    late = [r6, s6]
+    density = density_call(
+        [s.array for s in late],
+        [near_amp_of_far(s) for s in late],
+        [partial, incoming],
+        jnp.float32,
+    )
+    return density[None]
+
+
 def solution(mesh):
+    wide, narrow = mesh.shape["wide"], mesh.shape["narrow"]
+    paired = narrow == 2 and wide % 4 == 0 and wide > 2 * ROUNDS + 1 and ROUNDS == 5
+
+    def per_device(three_index, *rest):
+        if paired and three_index.shape[0] == 1:
+            return paired_plan(three_index, *rest)
+        return ring_plan(three_index, *rest)
+
     placed = (P("wide", None, "narrow"), P(), P(), P(), P(None, "wide"))
     return jax.shard_map(
         per_device, mesh=mesh, in_specs=placed, out_specs=P("wide", None, "narrow"), check_vma=False

time: 714 us -> 453 us (0.63)
  waiting for transfers between devices: 497 us -> 104 us
  Pallas kernels: 0 us -> 176 us
  matrix products: 137 us -> 0 us
  blocking collectives: 0 us -> 50.2 us
  between operations: 21 us -> 61 us
  local copies, waits for them, and re-layouts: 9.23 us -> 23.3 us
    ppermute x10 -> x16, waiting for transfers between devices: 491 us -> 104 us  [the longest x14 74.2 us: moved(): lax.ppermute(slab.array, 'wide', pairs)]
    pallas_call x0 -> x25, Pallas kernels: none -> 176 us  [the longest x22 113 us: amplitude_call(): pl.pallas_call(amplitude_kernel, grid=(rows // tile,), in_specs=[pl.Block...]
    dot_general x16 -> x0, matrix products: 137 us -> none  [the longest x5 60.5 us: per_device(): jnp.einsum('ijab,jpb->ipa', amplitude, visiting, preferred_element_type=j...]
    all_gather x0 -> x1, blocking collectives: none -> 50.2 us  [paired_plan(): lax.all_gather(pair_kept.astype(jnp.float32), 'wide', axis=1, tiled=True)]
    add x4 -> x0, other arithmetic: 15.9 us -> none  [the longest x1 8.81 us: per_device(): return scattered + returned]
    select_n x0 -> x4, other arithmetic: none -> 12.9 us  [chosen(): jnp.where(lead, slab_lead.array, slab_other.array)]
    dynamic_slice x2 -> x13, local copies, waits for them, and re-layouts: 0.76 us -> 8.4 us  [the longest x10 6.3 us: scalars(): block = jnp.asarray(np.array(slab.ids, np.int32))[here]]
    ppermute x10 -> x16, starting transfers between devices: 21.4 us -> 15.1 us  [the longest x14 12.6 us: moved(): lax.ppermute(slab.array, 'wide', pairs)]
  transfers between devices with their start and end apart: 12 -> 16, of which waited for: 9 -> 4; matrix products, arithmetic and copies ran while one was open for 21% -> 7% of each run, Pallas kernels for 0% -> 36%
where the time goes in v1:
time: 453 us; the launch traced here: 450 us
  Pallas kernels  176 us (39%)
  waiting for transfers between devices  104 us (23%)
  between operations  61 us (13%)
  blocking collectives  50.2 us (11%)
  local copies, waits for them, and re-layouts  23.3 us (5%)
  other arithmetic  20 us (4%)
  starting transfers between devices  15.1 us (3%)
    pallas_call x22, Pallas kernels, amplitude_call(): pl.pallas_call(amplitude_kernel, grid=(rows // tile,), in_specs=[pl.Block...  113 us
    ppermute x14, waiting for transfers between devices, moved(): lax.ppermute(slab.array, 'wide', pairs)  74.2 us
    pallas_call x3, Pallas kernels, density_call(): pl.pallas_call(kernel, grid=(aux // tile,), in_specs=[pl.BlockSpec((tile,...  62.8 us
    all_gather x1, blocking collectives, paired_plan(): lax.all_gather(pair_kept.astype(jnp.float32), 'wide', axis=1, tiled=True)  50.2 us
    ppermute x2, waiting for transfers between devices, sibling(): return lax.ppermute(array, 'narrow', [(0, 1), (1, 0)])  29.7 us
    select_n x4, other arithmetic, chosen(): jnp.where(lead, slab_lead.array, slab_other.array)  12.9 us
    ppermute x14, starting transfers between devices, moved(): lax.ppermute(slab.array, 'wide', pairs)  12.6 us
  transfers between devices with their start and end apart: 16, of which 4 were waited for; matrix products, arithmetic and copies ran while one was open for 7% of the time, Pallas kernels for 36%

profile of v1, /device:TPU:3, one launch (start us, length us, event | category | flops | bytes accessed | tf_op | source)
XLA Modules:
  0.0 449.7 jit_solution(119106998802970194)
XLA Ops:
  0.0 1.3 collective-permute-start.4
  1.3 1.3 dynamic_slice.297
  2.6 35.7 %collective-permute-done.4.slab.refs_0_ = bf16[3072,512]{1,0:T(8,128)(2,1)} collective-permute-done((bf16[3072,512]{1,0:T(8,128)(2,1)}, bf16[3072,512]{1,0:T(8,128)(2,1)}, u32[]{:S(2)}, u32[]{:S(2)}) %collective-permute-start.4) | collective-permute-done | bytes 3145760 | tf_op jit(solution)/shard_map/ppermute | solution.py:219
  38.3 1.6 copy-done.6
  39.9 6.2 %broadcast_select_fusion = (bf16[3072,512]{1,0:T(8,128)(2,1)}, bf16[3072,512]{1,0:T(8,128)(2,1)S(1)}) fusion(bf16[3072,512]{1,0:T(8,128)(2,1)} %copy-done.6, pred[]{:T(512)} %bitcast, bf16[1,3072,512]{2,1,0:T(8,128)(2,1)} %param.28, bf16[3072,512]{1,0:T(8,128)(2,1)} %collective-permute-done.4.slab.refs_0_), kind=kLoop, calls=%fused_computation | loop fusion | flops 3145728 | bytes 15728641 | tf_op jit(solution)/shard_map/jit(_where)/select_n | solution.py:226
  46.1 1.2 collective-permute-start.6
  47.4 1.2 collective-permute-start
  48.6 34.5 %collective-permute-done.6.slab.refs_2_ = bf16[3072,512]{1,0:T(8,128)(2,1)S(1)} collective-permute-done((bf16[3072,512]{1,0:T(8,128)(2,1)S(1)}, bf16[3072,512]{1,0:T(8,128)(2,1)S(1)}, u32[]{:S(2)}, u32[]{:S(2)}) %collective-permute-start.6) | collective-permute-done | bytes 3145760 | tf_op jit(solution)/shard_map/ppermute | solution.py:219
  83.1 0.9 broadcast_select_fusion.2
  84.1 3.5 collective-permute-start.9
  87.6 29.7 %collective-permute-done.slab.refs_11_ = bf16[3072,512]{1,0:T(8,128)(2,1)S(1)} collective-permute-done((bf16[3072,512]{1,0:T(8,128)(2,1)S(1)}, bf16[3072,512]{1,0:T(8,128)(2,1)S(1)}, u32[]{:S(2)}, u32[]{:S(2)}) %collective-permute-start) | collective-permute-done | bytes 3145760 | tf_op jit(solution)/shard_map/ppermute | solution.py:231
  117.9 3.9 collective-permute-done.9.slab.refs_4_
  121.8 3.1 broadcast_select_fusion.1
  125.5 2.8 collective-permute-start.11
  128.4 1.8 collective-permute-start.13
  130.2 2.7 broadcast_select_fusion.4
  165.2 0.9 copy.170.vir_rows
  184.0 3.1 copy.139.rows
  192.5 50.2 %all-gather = f32[16,1,6]{2,1,0:T(1,128)S(1)} all-gather(f32[1,1,6]{2,1,0:T(1,128)S(1)} %convert_bitcast_fusion), channel_id=1, replica_groups=mesh['wide'=16,'narrow'=2] {'wide'}, dimensions={0}, use_global_device_ids=true | all-gather | bytes 408 | tf_op jit(solution)/shard_map/all_gather | solution.py:236
  265.4 5.3 %shard_map.271.refs_20_ = bf16[512,512]{1,0:T(8,128)(2,1)} custom-call(f32[1,2]{1,0:T(1,128)} %maximum_bitcast_fusion.9.scalars, bf16[512,3072]{1,0:T(8,128)(2,1)} %copy.139.rows, bf16[3072,512]{1,0:T(8,128)(2,1)} %bitcast.81, f32[512,1]{1,0:T(8,128)} %copy.140.vir_rows, f32[1,512]{1,0:T(1,128)} %bitcast.87), custom_call_target="tpu_custom_call" | custom-call | flops 1610612736 | bytes 6815744 | tf_op jit(solution)/shard_map/pallas_call | solution.py:152
  270.7 3.1 copy.169.rows
  273.8 5.1 %shard_map.272.refs_21_ = bf16[512,512]{1,0:T(8,128)(2,1)} custom-call(f32[1,2]{1,0:T(1,128)} %maximum_bitcast_fusion.10.scalars, bf16[512,3072]{1,0:T(8,128)(2,1)} %copy.139.rows, bf16[3072,512]{1,0:T(8,128)(2,1)} %copy-done.6, f32[512,1]{1,0:T(8,128)} %copy.140.vir_rows, f32[1,512]{1,0:T(1,128)} %bitcast.88), custom_call_target="tpu_custom_call" | custom-call | flops 1610612736 | bytes 6815744 | tf_op jit(solution)/shard_map/pallas_call | solution.py:152
  278.9 5.1 %shard_map.275.refs_24_ = bf16[512,512]{1,0:T(8,128)(2,1)} custom-call(f32[1,2]{1,0:T(1,128)} %maximum_bitcast_fusion.9.scalars, bf16[512,3072]{1,0:T(8,128)(2,1)} %copy.139.rows, bf16[3072,512]{1,0:T(8,128)(2,1)} %copy-done.2, f32[512,1]{1,0:T(8,128)} %copy.140.vir_rows, f32[1,512]{1,0:T(1,128)} %bitcast.106), custom_call_target="tpu_custom_call" | custom-call | flops 1610612736 | bytes 6815744 | tf_op jit(solution)/shard_map/pallas_call | solution.py:152
  284.0 5.1 %shard_map.264.refs_13_ = bf16[512,512]{1,0:T(8,128)(2,1)} custom-call(f32[1,2]{1,0:T(1,128)} %maximum_bitcast_fusion.2.scalars, bf16[512,3072]{1,0:T(8,128)(2,1)} %copy.139.rows, bf16[3072,512]{1,0:T(8,128)(2,1)} %collective-permute-done.4.slab.refs_0_, f32[512,1]{1,0:T(8,128)} %copy.140.vir_rows, f32[1,512]{1,0:T(1,128)} %bitcast.89), custom_call_target="tpu_custom_call" | custom-call | flops 1610612736 | bytes 6815744 | tf_op jit(solution)/shard_map/pallas_call | solution.py:152
  289.5 5.1 %shard_map.278.refs_7_ = bf16[512,512]{1,0:T(8,128)(2,1)} custom-call(f32[1,2]{1,0:T(1,128)} %maximum_bitcast_fusion.2.scalars, bf16[512,3072]{1,0:T(8,128)(2,1)} %copy.169.rows, bf16[3072,512]{1,0:T(8,128)(2,1)} %collective-permute-done.4.slab.refs_0_, f32[512,1]{1,0:T(8,128)} %copy.170.vir_rows, f32[1,512]{1,0:T(1,128)} %bitcast.90), custom_call_target="tpu_custom_call" | custom-call | flops 1610612736 | bytes 6815744 | tf_op jit(solution)/shard_map/pallas_call | solution.py:152
  294.6 5.1 %shard_map.280.refs_9_ = bf16[512,512]{1,0:T(8,128)(2,1)} custom-call(f32[1,2]{1,0:T(1,128)} %maximum_bitcast_fusion.4.scalars, bf16[512,3072]{1,0:T(8,128)(2,1)} %copy.169.rows, bf16[3072,512]{1,0:T(8,128)(2,1)} %copy-done.1, f32[512,1]{1,0:T(8,128)} %copy.170.vir_rows, f32[1,512]{1,0:T(1,128)} %bitcast.91), custom_call_target="tpu_custom_call" | custom-call | flops 1610612736 | bytes 6815744 | tf_op jit(solution)/shard_map/pallas_call | solution.py:152
  299.9 5.1 %shard_map.266.refs_15_ = bf16[512,512]{1,0:T(8,128)(2,1)} custom-call(f32[1,2]{1,0:T(1,128)} %maximum_bitcast_fusion.4.scalars, bf16[512,3072]{1,0:T(8,128)(2,1)} %copy.139.rows, bf16[3072,512]{1,0:T(8,128)(2,1)} %copy-done.1, f32[512,1]{1,0:T(8,128)} %copy.140.vir_rows, f32[1,512]{1,0:T(1,128)} %bitcast.92), custom_call_target="tpu_custom_call" | custom-call | flops 1610612736 | bytes 6815744 | tf_op jit(solution)/shard_map/pallas_call | solution.py:152
  305.0 5.2 %shard_map.276.refs_25_ = bf16[512,512]{1,0:T(8,128)(2,1)} custom-call(f32[1,2]{1,0:T(1,128)} %maximum_bitcast_fusion.10.scalars, bf16[512,3072]{1,0:T(8,128)(2,1)} %copy.139.rows, bf16[3072,512]{1,0:T(8,128)(2,1)} %copy-done.8, f32[512,1]{1,0:T(8,128)} %copy.140.vir_rows, f32[1,512]{1,0:T(1,128)} %bitcast.107), custom_call_target="tpu_custom_call" | custom-call | flops 1610612736 | bytes 6815744 | tf_op jit(solution)/shard_map/pallas_call | solution.py:152
  310.2 5.1 %shard_map.279.refs_8_ = bf16[512,512]{1,0:T(8,128)(2,1)} custom-call(f32[1,2]{1,0:T(1,128)} %maximum_bitcast_fusion.3.scalars, bf16[512,3072]{1,0:T(8,128)(2,1)} %copy.169.rows, bf16[3072,512]{1,0:T(8,128)(2,1)} %collective-permute-done.5.slab.refs_1_, f32[512,1]{1,0:T(8,128)} %copy.170.vir_rows, f32[1,512]{1,0:T(1,128)} %bitcast.93), custom_call_target="tpu_custom_call" | custom-call | flops 1610612736 | bytes 6815744 | tf_op jit(solution)/shard_map/pallas_call | solution.py:152
  315.4 5.1 %shard_map.265.refs_14_ = bf16[512,512]{1,0:T(8,128)(2,1)} custom-call(f32[1,2]{1,0:T(1,128)} %maximum_bitcast_fusion.3.scalars, bf16[512,3072]{1,0:T(8,128)(2,1)} %copy.139.rows, bf16[3072,512]{1,0:T(8,128)(2,1)} %collective-permute-done.5.slab.refs_1_, f32[512,1]{1,0:T(8,128)} %copy.140.vir_rows, f32[1,512]{1,0:T(1,128)} %bitcast.94), custom_call_target="tpu_custom_call" | custom-call | flops 1610612736 | bytes 6815744 | tf_op jit(solution)/shard_map/pallas_call | solution.py:152
  320.5 5.1 %shard_map.282.refs_11_ = bf16[512,512]{1,0:T(8,128)(2,1)} custom-call(f32[1,2]{1,0:T(1,128)} %maximum_bitcast_fusion.6.scalars, bf16[512,3072]{1,0:T(8,128)(2,1)} %copy.169.rows, bf16[3072,512]{1,0:T(8,128)(2,1)} %copy-done.4, f32[512,1]{1,0:T(8,128)} %copy.170.vir_rows, f32[1,512]{1,0:T(1,128)} %bitcast.95), custom_call_target="tpu_custom_call" | custom-call | flops 1610612736 | bytes 6815744 | tf_op jit(solution)/shard_map/pallas_call | solution.py:152
  325.6 5.1 %shard_map.281.refs_10_ = bf16[512,512]{1,0:T(8,128)(2,1)} custom-call(f32[1,2]{1,0:T(1,128)} %maximum_bitcast_fusion.5.scalars, bf16[512,3072]{1,0:T(8,128)(2,1)} %copy.169.rows, bf16[3072,512]{1,0:T(8,128)(2,1)} %copy-done.5, f32[512,1]{1,0:T(8,128)} %copy.170.vir_rows, f32[1,512]{1,0:T(1,128)} %bitcast.96), custom_call_target="tpu_custom_call" | custom-call | flops 1610612736 | bytes 6815744 | tf_op jit(solution)/shard_map/pallas_call | solution.py:152
  330.8 5.1 %shard_map.283.refs_12_ = bf16[512,512]{1,0:T(8,128)(2,1)} custom-call(f32[1,2]{1,0:T(1,128)} %maximum_bitcast_fusion.7.scalars, bf16[512,3072]{1,0:T(8,128)(2,1)} %copy.169.rows, bf16[3072,512]{1,0:T(8,128)(2,1)} %collective-permute-done.10.slab.refs_5_, f32[512,1]{1,0:T(8,128)} %copy.170.vir_rows, f32[1,512]{1,0:T(1,128)} %bitcast.97), custom_call_target="tpu_custom_call" | custom-call | flops 1610612736 | bytes 6815744 | tf_op jit(solution)/shard_map/pallas_call | solution.py:152
  335.9 5.1 %shard_map.284.refs_13_ = bf16[512,512]{1,0:T(8,128)(2,1)} custom-call(f32[1,2]{1,0:T(1,128)} %maximum_bitcast_fusion.8.scalars, bf16[512,3072]{1,0:T(8,128)(2,1)} %copy.169.rows, bf16[3072,512]{1,0:T(8,128)(2,1)} %collective-permute-done.12.slab.refs_6_, f32[512,1]{1,0:T(8,128)} %copy.170.vir_rows, f32[1,512]{1,0:T(1,128)} %bitcast.98), custom_call_target="tpu_custom_call" | custom-call | flops 1610612736 | bytes 6815744 | tf_op jit(solution)/shard_map/pallas_call | solution.py:152
  341.1 19.5 %shard_map.285 = bf16[3072,512]{1,0:T(8,128)(2,1)} custom-call(bf16[3072,512]{1,0:T(8,128)(2,1)} %collective-permute-done.4.slab.refs_0_, bf16[3072,512]{1,0:T(8,128)(2,1)} %collective-permute-done.5.slab.refs_1_, bf16[3072,512]{1,0:T(8,128)(2,1)} %copy-done.1, bf16[3072,512]{1,0:T(8,128)(2,1)} %copy-done.5, bf16[3072,512]{1,0:T(8,128)(2,1)} %copy-done.4, ...), custom_call_target="tpu_custom_call" | custom-call | flops 11274289152 | bytes 28835840 | tf_op jit(solution)/shard_map/pallas_call | solution.py:193
  360.6 1.2 collective-permute-start.15
  361.8 5.1 %shard_map.273.refs_22_ = bf16[512,512]{1,0:T(8,128)(2,1)} custom-call(f32[1,2]{1,0:T(1,128)} %maximum_bitcast_fusion.scalars, bf16[512,3072]{1,0:T(8,128)(2,1)} %copy.139.rows, bf16[3072,512]{1,0:T(8,128)(2,1)} %collective-permute-done.13.slab.refs_9_, f32[512,1]{1,0:T(8,128)} %copy.140.vir_rows, f32[1,512]{1,0:T(1,128)} %bitcast.99), custom_call_target="tpu_custom_call" | custom-call | flops 1610612736 | bytes 6815744 | tf_op jit(solution)/shard_map/pallas_call | solution.py:152
  366.9 5.4 %shard_map.268.refs_17_ = bf16[512,512]{1,0:T(8,128)(2,1)} custom-call(f32[1,2]{1,0:T(1,128)} %maximum_bitcast_fusion.6.scalars, bf16[512,3072]{1,0:T(8,128)(2,1)} %copy.139.rows, bf16[3072,512]{1,0:T(8,128)(2,1)} %copy-done.4, f32[512,1]{1,0:T(8,128)} %copy.140.vir_rows, f32[1,512]{1,0:T(1,128)} %bitcast.100), custom_call_target="tpu_custom_call" | custom-call | flops 1610612736 | bytes 6815744 | tf_op jit(solution)/shard_map/pallas_call | solution.py:152
  372.3 5.1 %shard_map.267.refs_16_ = bf16[512,512]{1,0:T(8,128)(2,1)} custom-call(f32[1,2]{1,0:T(1,128)} %maximum_bitcast_fusion.5.scalars, bf16[512,3072]{1,0:T(8,128)(2,1)} %copy.139.rows, bf16[3072,512]{1,0:T(8,128)(2,1)} %copy-done.5, f32[512,1]{1,0:T(8,128)} %copy.140.vir_rows, f32[1,512]{1,0:T(1,128)} %bitcast.101), custom_call_target="tpu_custom_call" | custom-call | flops 1610612736 | bytes 6815744 | tf_op jit(solution)/shard_map/pallas_call | solution.py:152
  377.4 5.1 %shard_map.262.refs_2_ = bf16[512,512]{1,0:T(8,128)(2,1)} custom-call(f32[1,2]{1,0:T(1,128)} %maximum_bitcast_fusion.scalars, bf16[512,3072]{1,0:T(8,128)(2,1)} %copy.139.rows, bf16[3072,512]{1,0:T(8,128)(2,1)} %collective-permute-done.2.slab.refs_0_, f32[512,1]{1,0:T(8,128)} %copy.140.vir_rows, f32[1,512]{1,0:T(1,128)} %bitcast.108), custom_call_target="tpu_custom_call" | custom-call | flops 1610612736 | bytes 6815744 | tf_op jit(solution)/shard_map/pallas_call | solution.py:152
  382.6 1.7 copy-done.10
  384.2 5.1 %shard_map.274.refs_23_ = bf16[512,512]{1,0:T(8,128)(2,1)} custom-call(f32[1,2]{1,0:T(1,128)} %maximum_bitcast_fusion.1.scalars, bf16[512,3072]{1,0:T(8,128)(2,1)} %copy.139.rows, bf16[3072,512]{1,0:T(8,128)(2,1)} %copy-done.10, f32[512,1]{1,0:T(8,128)} %copy.140.vir_rows, f32[1,512]{1,0:T(1,128)} %bitcast.102), custom_call_target="tpu_custom_call" | custom-call | flops 1610612736 | bytes 6815744 | tf_op jit(solution)/shard_map/pallas_call | solution.py:152
  389.4 5.1 %shard_map.269.refs_18_ = bf16[512,512]{1,0:T(8,128)(2,1)} custom-call(f32[1,2]{1,0:T(1,128)} %maximum_bitcast_fusion.7.scalars, bf16[512,3072]{1,0:T(8,128)(2,1)} %copy.139.rows, bf16[3072,512]{1,0:T(8,128)(2,1)} %collective-permute-done.10.slab.refs_5_, f32[512,1]{1,0:T(8,128)} %copy.140.vir_rows, f32[1,512]{1,0:T(1,128)} %bitcast.103), custom_call_target="tpu_custom_call" | custom-call | flops 1610612736 | bytes 6815744 | tf_op jit(solution)/shard_map/pallas_call | solution.py:152
  394.5 1.6 copy-done.9
  396.2 5.1 %shard_map.263.refs_3_ = bf16[512,512]{1,0:T(8,128)(2,1)} custom-call(f32[1,2]{1,0:T(1,128)} %maximum_bitcast_fusion.1.scalars, bf16[512,3072]{1,0:T(8,128)(2,1)} %copy.139.rows, bf16[3072,512]{1,0:T(8,128)(2,1)} %copy-done.9, f32[512,1]{1,0:T(8,128)} %copy.140.vir_rows, f32[1,512]{1,0:T(1,128)} %bitcast.109), custom_call_target="tpu_custom_call" | custom-call | flops 1610612736 | bytes 6815744 | tf_op jit(solution)/shard_map/pallas_call | solution.py:152
  401.3 5.1 %shard_map.270.refs_19_ = bf16[512,512]{1,0:T(8,128)(2,1)} custom-call(f32[1,2]{1,0:T(1,128)} %maximum_bitcast_fusion.8.scalars, bf16[512,3072]{1,0:T(8,128)(2,1)} %copy.139.rows, bf16[3072,512]{1,0:T(8,128)(2,1)} %collective-permute-done.12.slab.refs_6_, f32[512,1]{1,0:T(8,128)} %copy.140.vir_rows, f32[1,512]{1,0:T(1,128)} %bitcast.104), custom_call_target="tpu_custom_call" | custom-call | flops 1610612736 | bytes 6815744 | tf_op jit(solution)/shard_map/pallas_call | solution.py:152
  406.4 29.1 %shard_map.277.refs_4_ = f32[3072,512]{1,0:T(8,128)} custom-call(bf16[3072,512]{1,0:T(8,128)(2,1)} %collective-permute-done.4.slab.refs_0_, bf16[3072,512]{1,0:T(8,128)(2,1)} %collective-permute-done.5.slab.refs_1_, bf16[3072,512]{1,0:T(8,128)(2,1)} %copy-done.1, bf16[3072,512]{1,0:T(8,128)(2,1)} %copy-done.5, bf16[3072,512]{1,0:T(8,128)(2,1)} %copy-done.4, ...), custom_call_target="tpu_custom_call" | custom-call | flops 20937965568 | bytes 54001664 | tf_op jit(solution)/shard_map/pallas_call | solution.py:193
  435.5 14.2 %shard_map.286 = f32[3072,512]{1,0:T(8,128)} custom-call(bf16[3072,512]{1,0:T(8,128)(2,1)} %collective-permute-done.2.slab.refs_0_, bf16[3072,512]{1,0:T(8,128)(2,1)} %copy-done.9, bf16[512,512]{1,0:T(8,128)(2,1)} %shard_map.262.refs_2_, bf16[512,512]{1,0:T(8,128)(2,1)} %shard_map.263.refs_3_, f32[3072,512]{1,0:T(8,128)} %shard_map.277.refs_4_, ...), custom_call_target="tpu_custom_call" | custom-call | flops 3221225472 | bytes 23068672 | tf_op jit(solution)/shard_map/pallas_call | solution.py:193
  (100 shorter events, 19.2 us)
Async XLA Ops:
  0.0 38.3 %collective-permute-start.4 = (bf16[3072,512]{1,0:T(8,128)(2,1)}, bf16[3072,512]{1,0:T(8,128)(2,1)}, u32[]{:S(2)}, u32[]{:S(2)}) collective-permute-start(bf16[3072,512]{1,0:T(8,128)(2,1)} %bitcast.79), channel_id=1, source_target_pairs={{0,24},{2,4},{4,2},{6,14},{8,0},{10,12},{12,10},{14,22},{16,8},{18... | collective-permute-start | bytes 9437192 | tf_op jit(solution)/shard_map/ppermute | solution.py:219
  1.3 37.0 %collective-permute-start.8 = (bf16[3072,512]{1,0:T(8,128)(2,1)}, bf16[3072,512]{1,0:T(8,128)(2,1)S(1)}, u32[]{:S(2)}, u32[]{:S(2)}) collective-permute-start(bf16[3072,512]{1,0:T(8,128)(2,1)} %bitcast.80), channel_id=1, source_target_pairs={{0,2},{2,0},{4,6},{6,4},{8,10},{10,8},{12,14},{14,12},{16,18},{18,... | collective-permute-start | bytes 9437192 | tf_op jit(solution)/shard_map/ppermute | solution.py:219
  38.3 1.6 copy-start.6
  39.9 7.4 %copy-start = (bf16[1,3072,512]{2,1,0:T(8,128)(2,1)S(1)}, bf16[1,3072,512]{2,1,0:T(8,128)(2,1)}, u32[]{:S(2)}) copy-start(bf16[1,3072,512]{2,1,0:T(8,128)(2,1)} %param.28) | copy-start | bytes 9437188
  39.9 43.2 %copy-start.7 = (bf16[3072,512]{1,0:T(8,128)(2,1)S(1)}, bf16[3072,512]{1,0:T(8,128)(2,1)}, u32[]{:S(2)}) copy-start(bf16[3072,512]{1,0:T(8,128)(2,1)} %copy-done.6) | copy-start | bytes 9437188
  46.1 37.0 %collective-permute-start.6 = (bf16[3072,512]{1,0:T(8,128)(2,1)S(1)}, bf16[3072,512]{1,0:T(8,128)(2,1)S(1)}, u32[]{:S(2)}, u32[]{:S(2)}) collective-permute-start(bf16[3072,512]{1,0:T(8,128)(2,1)S(1)} %get-tuple-element.6), channel_id=1, source_target_pairs={{0,6},{2,26},{4,12},{6,0},{8,14},{10,2},{12,20},{14,8},{16,22},{18... | collective-permute-start | bytes 9437192 | tf_op jit(solution)/shard_map/ppermute | solution.py:219
  47.4 69.9 %collective-permute-start = (bf16[3072,512]{1,0:T(8,128)(2,1)S(1)}, bf16[3072,512]{1,0:T(8,128)(2,1)S(1)}, u32[]{:S(2)}, u32[]{:S(2)}) collective-permute-start(bf16[3072,512]{1,0:T(8,128)(2,1)S(1)} %bitcast.83), channel_id=1, source_target_pairs={{0,1},{1,0},{2,3},{3,2},{4,5},{5,4},{6,7},{7,6},{8,9},{9,8},{10,11... | collective-permute-start | bytes 9437192 | tf_op jit(solution)/shard_map/ppermute | solution.py:231
  83.1 4.5 copy-start.1
  84.1 37.7 %collective-permute-start.9 = (bf16[3072,512]{1,0:T(8,128)(2,1)S(1)}, bf16[3072,512]{1,0:T(8,128)(2,1)S(1)}, u32[]{:S(2)}, u32[]{:S(2)}) collective-permute-start(bf16[3072,512]{1,0:T(8,128)(2,1)S(1)} %broadcast_select_fusion.2), channel_id=1, source_target_pairs={{0,8},{2,4},{4,2},{6,30},{8,16},{10,12},{12,10},{14,6},{16,24},{18... | collective-permute-start | bytes 9437192 | tf_op jit(solution)/shard_map/ppermute | solution.py:219
  87.6 34.2 %collective-permute-start.7 = (bf16[3072,512]{1,0:T(8,128)(2,1)S(1)}, bf16[3072,512]{1,0:T(8,128)(2,1)S(1)}, u32[]{:S(2)}, u32[]{:S(2)}) collective-permute-start(bf16[3072,512]{1,0:T(8,128)(2,1)S(1)} %collective-permute-done.6.slab.refs_2_), channel_id=1, source_target_pairs={{0,2},{2,0},{4,6},{6,4},{8,10},{10,8},{12,14},{14,12},{16,18},{18,... | collective-permute-start | bytes 9437192 | tf_op jit(solution)/shard_map/ppermute | solution.py:219
  117.3 12.9 %copy-start.2 = (bf16[3072,512]{1,0:T(8,128)(2,1)}, bf16[3072,512]{1,0:T(8,128)(2,1)S(1)}, u32[]{:S(2)}) copy-start(bf16[3072,512]{1,0:T(8,128)(2,1)S(1)} %collective-permute-done.slab.refs_11_) | copy-start | bytes 9437188
  117.3 12.9 %collective-permute-start.1 = (bf16[3072,512]{1,0:T(8,128)(2,1)S(1)}, bf16[3072,512]{1,0:T(8,128)(2,1)S(1)}, u32[]{:S(2)}, u32[]{:S(2)}) collective-permute-start(bf16[3072,512]{1,0:T(8,128)(2,1)S(1)} %collective-permute-done.slab.refs_11_), channel_id=1, source_target_pairs={{0,2},{2,0},{4,6},{6,4},{8,10},{10,8},{12,14},{14,12},{16,18},{18,... | collective-permute-start | bytes 9437192 | tf_op jit(solution)/shard_map/ppermute | solution.py:219
  121.8 3.1 copy-start.4
  121.8 3.7 copy-start.5
  125.5 132.7 %collective-permute-start.11 = (bf16[3072,512]{1,0:T(8,128)(2,1)}, bf16[3072,512]{1,0:T(8,128)(2,1)}, u32[]{:S(2)}, u32[]{:S(2)}) collective-permute-start(bf16[3072,512]{1,0:T(8,128)(2,1)} %broadcast_select_fusion.1), channel_id=1, source_target_pairs={{0,6},{2,10},{4,28},{6,0},{8,14},{10,18},{12,4},{14,8},{16,22},{18... | collective-permute-start | bytes 9437192 | tf_op jit(solution)/shard_map/ppermute | solution.py:219
  128.3 4.7 %copy-start.26 = (s32[16]{0:T(128)S(1)}, s32[16]{0:T(128)}, u32[]{:S(2)}) copy-start(s32[16]{0:T(128)} %constant.234.clone) | copy-start | bytes 196
  128.3 6.0 %copy-start.25 = (s32[16]{0:T(128)S(1)}, s32[16]{0:T(128)}, u32[]{:S(2)}) copy-start(s32[16]{0:T(128)} %constant.235.clone) | copy-start | bytes 196
  128.3 8.0 %copy-start.24 = (s32[16]{0:T(128)S(1)}, s32[16]{0:T(128)}, u32[]{:S(2)}) copy-start(s32[16]{0:T(128)} %constant.236.clone) | copy-start | bytes 196
  128.3 9.8 %copy-start.23 = (s32[16]{0:T(128)S(1)}, s32[16]{0:T(128)}, u32[]{:S(2)}) copy-start(s32[16]{0:T(128)} %constant.237.clone) | copy-start | bytes 196
  128.3 11.9 %copy-start.22 = (s32[16]{0:T(128)S(1)}, s32[16]{0:T(128)}, u32[]{:S(2)}) copy-start(s32[16]{0:T(128)} %constant.238.clone) | copy-start | bytes 196
  128.3 20.1 %copy-start.21 = (s32[16]{0:T(128)S(1)}, s32[16]{0:T(128)}, u32[]{:S(2)}) copy-start(s32[16]{0:T(128)} %constant.239.clone) | copy-start | bytes 196
  128.3 22.0 %copy-start.20 = (s32[16]{0:T(128)S(1)}, s32[16]{0:T(128)}, u32[]{:S(2)}) copy-start(s32[16]{0:T(128)} %constant.240.clone) | copy-start | bytes 196
  128.3 23.9 %copy-start.19 = (s32[16]{0:T(128)S(1)}, s32[16]{0:T(128)}, u32[]{:S(2)}) copy-start(s32[16]{0:T(128)} %constant.231.clone) | copy-start | bytes 196
  128.4 25.9 %copy-start.18 = (s32[16]{0:T(128)S(1)}, s32[16]{0:T(128)}, u32[]{:S(2)}) copy-start(s32[16]{0:T(128)} %constant.232.clone) | copy-start | bytes 196
  128.4 27.6 %copy-start.17 = (s32[16]{0:T(128)S(1)}, s32[16]{0:T(128)}, u32[]{:S(2)}) copy-start(s32[16]{0:T(128)} %constant.233.clone) | copy-start | bytes 196
  128.4 36.7 %copy-start.13 = (f32[1024]{0:T(1024)S(1)}, f32[1024]{0:T(1024)}, u32[]{:S(2)}) copy-start(f32[1024]{0:T(1024)} %param.31) | copy-start | bytes 12292
  128.4 44.0 %copy-start.14 = (s32[6,1]{0,1:T(1,128)S(1)}, s32[6,1]{0,1:T(1,128)}, u32[]{:S(2)}) copy-start(s32[6,1]{0,1:T(1,128)} %param.32) | copy-start | bytes 76
  128.4 44.6 %copy-start.15 = (f32[16]{0:T(128)S(1)}, f32[16]{0:T(128)}, u32[]{:S(2)}) copy-start(f32[16]{0:T(128)} %param.30) | copy-start | bytes 196
  128.4 44.5 %copy-start.16 = (s32[16]{0:T(128)S(1)}, s32[16]{0:T(128)}, u32[]{:S(2)}) copy-start(s32[16]{0:T(128)} %param.29) | copy-start | bytes 196
  128.4 160.7 %collective-permute-start.13 = (bf16[3072,512]{1,0:T(8,128)(2,1)}, bf16[3072,512]{1,0:T(8,128)(2,1)}, u32[]{:S(2)}, u32[]{:S(2)}) collective-permute-start(bf16[3072,512]{1,0:T(8,128)(2,1)} %get-tuple-element.5), channel_id=1, source_target_pairs={{0,8},{2,4},{4,2},{6,30},{8,16},{10,12},{12,10},{14,6},{16,24},{18... | collective-permute-start | bytes 9437192 | tf_op jit(solution)/shard_map/ppermute | solution.py:219
  130.2 2.7 copy-start.8
  132.9 166.8 %collective-permute-start.2 = (bf16[3072,512]{1,0:T(8,128)(2,1)}, bf16[3072,512]{1,0:T(8,128)(2,1)}, u32[]{:S(2)}, u32[]{:S(2)}) collective-permute-start(bf16[3072,512]{1,0:T(8,128)(2,1)} %broadcast_select_fusion.4), channel_id=1, source_target_pairs={{0,8},{2,4},{4,2},{6,30},{8,16},{10,12},{12,10},{14,6},{16,24},{18... | collective-permute-start | bytes 9437192 | tf_op jit(solution)/shard_map/ppermute | solution.py:219
  133.0 177.3 %collective-permute-start.5 = (bf16[3072,512]{1,0:T(8,128)(2,1)}, bf16[3072,512]{1,0:T(8,128)(2,1)}, u32[]{:S(2)}, u32[]{:S(2)}) collective-permute-start(bf16[3072,512]{1,0:T(8,128)(2,1)} %collective-permute-done.4.slab.refs_0_), channel_id=1, source_target_pairs={{0,2},{2,0},{4,6},{6,4},{8,10},{10,8},{12,14},{14,12},{16,18},{18,... | collective-permute-start | bytes 9437192 | tf_op jit(solution)/shard_map/ppermute | solution.py:219
  165.2 21.9 %copy-start.11 = (f32[512]{0:T(512)}, f32[512]{0:T(512)S(1)}, u32[]{:S(2)}) copy-start(f32[512]{0:T(512)S(1)} %get-tuple-element.30) | copy-start | bytes 6148
  165.2 21.9 %copy-start.12 = (f32[512]{0:T(512)}, f32[512]{0:T(512)S(1)}, u32[]{:S(2)}) copy-start(f32[512]{0:T(512)S(1)} %get-tuple-element.29) | copy-start | bytes 6148
  172.4 158.4 %collective-permute-start.10 = (bf16[3072,512]{1,0:T(8,128)(2,1)}, bf16[3072,512]{1,0:T(8,128)(2,1)}, u32[]{:S(2)}, u32[]{:S(2)}) collective-permute-start(bf16[3072,512]{1,0:T(8,128)(2,1)} %copy-done.4), channel_id=1, source_target_pairs={{0,2},{2,0},{4,6},{6,4},{8,10},{10,8},{12,14},{14,12},{16,18},{18,... | collective-permute-start | bytes 9437192 | tf_op jit(solution)/shard_map/ppermute | solution.py:219
  258.2 77.7 %collective-permute-start.12 = (bf16[3072,512]{1,0:T(8,128)(2,1)}, bf16[3072,512]{1,0:T(8,128)(2,1)}, u32[]{:S(2)}, u32[]{:S(2)}) collective-permute-start(bf16[3072,512]{1,0:T(8,128)(2,1)} %collective-permute-done.11), channel_id=1, source_target_pairs={{0,2},{2,0},{4,6},{6,4},{8,10},{10,8},{12,14},{14,12},{16,18},{18,... | collective-permute-start | bytes 9437192 | tf_op jit(solution)/shard_map/ppermute | solution.py:219
  265.4 5.3 %copy-start.3 = (bf16[3072,512]{1,0:T(8,128)(2,1)S(1)}, bf16[3072,512]{1,0:T(8,128)(2,1)}, u32[]{:S(2)}) copy-start(bf16[3072,512]{1,0:T(8,128)(2,1)} %copy-done.2) | copy-start | bytes 9437188
  289.2 93.4 %collective-permute-start.14 = (bf16[3072,512]{1,0:T(8,128)(2,1)}, bf16[3072,512]{1,0:T(8,128)(2,1)S(1)}, u32[]{:S(2)}, u32[]{:S(2)}) collective-permute-start(bf16[3072,512]{1,0:T(8,128)(2,1)} %collective-permute-done.13.slab.refs_9_), channel_id=1, source_target_pairs={{0,2},{2,0},{4,6},{6,4},{8,10},{10,8},{12,14},{14,12},{16,18},{18,... | collective-permute-start | bytes 9437192 | tf_op jit(solution)/shard_map/ppermute | solution.py:219
  299.7 94.8 %collective-permute-start.3 = (bf16[3072,512]{1,0:T(8,128)(2,1)}, bf16[3072,512]{1,0:T(8,128)(2,1)S(1)}, u32[]{:S(2)}, u32[]{:S(2)}) collective-permute-start(bf16[3072,512]{1,0:T(8,128)(2,1)} %collective-permute-done.2.slab.refs_0_), channel_id=1, source_target_pairs={{0,2},{2,0},{4,6},{6,4},{8,10},{10,8},{12,14},{14,12},{16,18},{18,... | collective-permute-start | bytes 9437192 | tf_op jit(solution)/shard_map/ppermute | solution.py:219
  360.6 74.9 %collective-permute-start.15 = (bf16[3072,512]{1,0:T(8,128)(2,1)}, bf16[3072,512]{1,0:T(8,128)(2,1)}, u32[]{:S(2)}, u32[]{:S(2)}) collective-permute-start(bf16[3072,512]{1,0:T(8,128)(2,1)} %shard_map.285), channel_id=1, source_target_pairs={{0,1},{1,0},{2,3},{3,2},{4,5},{5,4},{6,7},{7,6},{8,9},{9,8},{10,11... | collective-permute-start | bytes 9437192 | tf_op jit(solution)/shard_map/ppermute | solution.py:231
  382.6 1.7 copy-start.10
  394.5 1.6 copy-start.9

commit v2 on v0

--- a/solution.py
+++ b/solution.py
@@ -1,9 +1,13 @@
 import jax
 import jax.numpy as jnp
+import numpy as np
 from jax import lax
+from jax.experimental import pallas as pl
+from jax.experimental.pallas import tpu as pltpu
 from jax.sharding import PartitionSpec as P
 
 ROUNDS = 5
+VMEM = 56 * 1024 * 1024
 
 
 def passed_along(array, axis, by):
@@ -26,7 +30,7 @@
     return (weight * coulomb / denominator).astype(jnp.bfloat16)
 
 
-def per_device(three_index, orbital_map, occ_energy, vir_energy, pair_kept):
+def ring_plan(three_index, orbital_map, occ_energy, vir_energy, pair_kept):
     occ_count = three_index.shape[0]
     vir_count = three_index.shape[2]
     blocks = lax.axis_size("wide")
@@ -79,7 +83,238 @@
     return scattered + returned
 
 
+class Routes:
+    def __init__(self, blocks):
+        self.blocks = blocks
+        everyone = range(blocks)
+        self.lead = [self.place(w)[1] == self.place(w)[2] for w in everyone]
+        self.swap = [(w, w ^ 1) for w in everyone]
+        self.onward = [(w, self.along_z(w, 1)) for w in everyone]
+        self.backward = [(w, self.along_z(w, -1)) for w in everyone]
+        self.across = [(w, self.across_x(w)) for w in everyone]
+        self.last = [pair[0 if lead else 1] for lead, *pair in zip(self.lead, self.backward, self.across)]
+
+    def place(self, w):
+        return w // 4, (w // 2) % 2, w % 2
+
+    def along_z(self, w, step):
+        z, x, core = self.place(w)
+        z = (z + (step if x == 1 else -step)) % (self.blocks // 4)
+        return (z * 2 + x) * 2 + core
+
+    def across_x(self, w):
+        z, x, core = self.place(w)
+        return (z * 2 + 1 - x) * 2 + 1 - core
+
+    def moved(self, ids, pairs):
+        out = [0] * self.blocks
+        for source, target in pairs:
+            out[target] = ids[source]
+        return out
+
+
+class Slab:
+    def __init__(self, array, ids):
+        self.array = array
+        self.ids = ids
+
+
+def tile_of(length, most):
+    size = min(length, most)
+    while length % size:
+        size -= 8
+    return size
+
+
+def amplitude_kernel(scalars, rows, slab, vir_rows, vir_cols, out):
+    coulomb = jnp.dot(rows[...], slab[...], preferred_element_type=jnp.float32)
+    denominator = (vir_rows[...] + vir_cols[...]) - scalars[0, 0]
+    out[...] = (scalars[0, 1] * coulomb / denominator).astype(out.dtype)
+
+
+def amplitude_call(scalars, turned, slab, vir_rows, vir_cols, first, count):
+    aux = turned.shape[1]
+    cols = slab.shape[1]
+    tile = cols
+    return pl.pallas_call(
+        amplitude_kernel,
+        grid=(count,),
+        in_specs=[
+            pl.BlockSpec(memory_space=pltpu.SMEM),
+            pl.BlockSpec((tile, aux), lambda i: (first + i, 0)),
+            pl.BlockSpec((aux, cols), lambda i: (0, 0)),
+            pl.BlockSpec((tile, 1), lambda i: (first + i, 0)),
+            pl.BlockSpec((1, cols), lambda i: (0, 0)),
+        ],
+        out_specs=pl.BlockSpec((tile, cols), lambda i: (i, 0)),
+        out_shape=jax.ShapeDtypeStruct((count * tile, cols), jnp.bfloat16),
+        compiler_params=pltpu.CompilerParams(vmem_limit_bytes=VMEM),
+        cost_estimate=pl.CostEstimate(
+            flops=2 * count * tile * aux * cols,
+            bytes_accessed=2 * (count * tile * aux + aux * cols + count * tile * cols),
+            transcendentals=0,
+        ),
+    )(scalars, turned, slab, vir_rows, vir_cols)
+
+
+def density_call(terms, parts, out_dtype, rows=None):
+    count = len(terms)
+    aux, depth = terms[0][0].shape if terms else parts[0].shape
+    cols = depth
+    begin, length = rows or (0, aux)
+    tile = tile_of(length, 512)
+    skip = begin // tile
+
+    def kernel(*refs):
+        out = refs[-1]
+        total = None
+        for ref in refs[2 * count : -1]:
+            part = ref[...].astype(jnp.float32)
+            total = part if total is None else total + part
+        for slab, amp in zip(refs[:count], refs[count : 2 * count]):
+            term = lax.dot_general(
+                slab[...], amp[...], (((1,), (1,)), ((), ())), preferred_element_type=jnp.float32
+            )
+            total = term if total is None else total + term
+        out[...] = total.astype(out.dtype)
+
+    def rows_of(array):
+        shift = skip if array.shape[0] == aux else 0
+        return pl.BlockSpec((tile, array.shape[1]), lambda i: (i + shift, 0))
+
+    def amp_block(index):
+        return pl.BlockSpec((cols, depth), lambda i: (index, 0))
+
+    bytes_in = sum(t[0].size * 2 + cols * depth * 2 for t in terms)
+    bytes_in += sum(p.size * p.dtype.itemsize for p in parts)
+    return pl.pallas_call(
+        kernel,
+        grid=(length // tile,),
+        in_specs=[rows_of(t[0]) for t in terms]
+        + [amp_block(t[2]) for t in terms]
+        + [rows_of(p) for p in parts],
+        out_specs=pl.BlockSpec((tile, cols), lambda i: (i, 0)),
+        out_shape=jax.ShapeDtypeStruct((length, cols), out_dtype),
+        compiler_params=pltpu.CompilerParams(vmem_limit_bytes=VMEM),
+        cost_estimate=pl.CostEstimate(
+            flops=2 * length * depth * cols * count,
+            bytes_accessed=bytes_in * length // aux + length * cols * jnp.dtype(out_dtype).itemsize,
+            transcendentals=0,
+        ),
+    )(*[t[0] for t in terms], *[t[1] for t in terms], *parts)
+
+
+def kept_ahead(pair_kept, blocks):
+    run = pair_kept.astype(jnp.float32).reshape(1, ROUNDS + 1)
+    while run.shape[0] < ROUNDS + 1:
+        have = run.shape[0]
+        take = min(have, ROUNDS + 1 - have)
+        run = jnp.concatenate([run, passed_along(run[:take], "wide", -have)])
+    return jnp.diagonal(run)
+
+
+def paired_plan(three_index, orbital_map, occ_energy, vir_energy, pair_kept):
+    blocks = lax.axis_size("wide")
+    routes = Routes(blocks)
+    here = lax.axis_index("wide")
+    side = lax.axis_index("narrow")
+    aux, vir_count = three_index.shape[1:]
+    lead = jnp.asarray(np.array(routes.lead))[here]
+
+    def moved(slab, pairs):
+        return Slab(lax.ppermute(slab.array, "wide", pairs), routes.moved(slab.ids, pairs))
+
+    def swapped(slab):
+        return moved(slab, routes.swap)
+
+    def sibling(array):
+        return lax.ppermute(array, "narrow", [(0, 1), (1, 0)])
+
+    def after(slab, *others):
+        return Slab(lax.optimization_barrier((slab.array, *others))[0], slab.ids)
+
+    labels = jnp.arange(occ_energy.shape[0], dtype=jnp.int32)
+    picked = orbital_map[:, None] == labels[None, :]
+    energy = jnp.sum(jnp.where(picked, occ_energy[None, :], 0.0), axis=1)
+    behind = pair_kept[:, 0].astype(jnp.float32)
+    ahead = kept_ahead(pair_kept, blocks)
+
+    vir_near = lax.dynamic_slice_in_dim(vir_energy, side * vir_count, vir_count)
+    vir_far = lax.dynamic_slice_in_dim(vir_energy, (1 - side) * vir_count, vir_count)
+    vir_rows = jnp.concatenate([vir_near, vir_far])[:, None]
+    near_cols, far_cols = vir_near[None, :], vir_far[None, :]
+
+    own = Slab(three_index[0], list(range(blocks)))
+    onward = moved(own, routes.onward)
+    across = moved(own, routes.across)
+    own_far = Slab(sibling(own.array), own.ids)
+    mate = swapped(own)
+    mate_far = swapped(own_far)
+    turned = jnp.concatenate([own.array, own_far.array], axis=1).T
+
+    def scalars(slab):
+        block = jnp.asarray(np.array(slab.ids, np.int32))[here]
+        back = (here - block) % blocks
+        forth = (block - here) % blocks
+        weight = jnp.where(
+            back <= ROUNDS, behind[jnp.minimum(back, ROUNDS)], ahead[jnp.minimum(forth, ROUNDS)]
+        )
+        return jnp.stack([energy[here] + energy[block], weight]).reshape(1, 2)
+
+    def amp(slab, cols=near_cols, first=0, count=2):
+        return amplitude_call(scalars(slab), turned, slab.array, vir_rows, cols, first, count)
+
+    near, far = 0, 1
+    at_home = [
+        (own.array, amp(own, count=1), near),
+        (own_far.array, amp(own_far, far_cols, count=1), near),
+        (mate.array, amp(mate, count=1), near),
+        (mate_far.array, amp(mate_far, far_cols, count=1), near),
+    ]
+    onward = after(onward, *[t[1] for t in at_home])
+
+    onward_across = moved(onward, routes.across)
+    backward = moved(after(own, onward.array), routes.backward)
+    first = [onward, across, swapped(onward), swapped(across)]
+    first = [(s.array, amp(s)) for s in first]
+    out_part = density_call([(*t, far) for t in first], [], jnp.float32)
+    near_part = density_call([(*t, near) for t in first] + at_home, [], jnp.float32)
+    backward = after(backward, out_part, near_part)
+
+    second = [onward_across, swapped(onward_across), backward, swapped(backward)]
+    last = moved(
+        Slab(
+            jnp.where(lead, onward_across.array, backward.array),
+            [a if lead else b for lead, a, b in zip(routes.lead, onward_across.ids, backward.ids)],
+        ),
+        routes.last,
+    )
+    second = [(s.array, amp(s)) for s in second]
+    out_part = density_call([(*t, far) for t in second], [out_part], jnp.float32)
+    near_part = density_call([(*t, near) for t in second], [near_part], jnp.float32)
+    last = after(last, out_part, near_part)
+
+    last_far = amp(last, first=far, count=1)
+    ranges = [(begin, aux // 2) for begin in range(0, aux, aux // 2)]
+    incoming = []
+    for rows in ranges:
+        outgoing = density_call([(last.array, last_far, near)], [out_part], jnp.bfloat16, rows)
+        incoming.append(sibling(outgoing))
+    last_near = amp(last, first=near, count=1)
+    near_part = density_call([(last.array, last_near, near)], [near_part], jnp.float32)
+    density = near_part + jnp.concatenate(incoming).astype(jnp.float32)
+    return density[None]
+
+
 def solution(mesh):
+    wide, narrow = mesh.shape["wide"], mesh.shape["narrow"]
+    paired = narrow == 2 and wide % 4 == 0 and wide > 2 * ROUNDS + 1 and ROUNDS == 5
+
+    def per_device(three_index, *rest):
+        if paired and three_index.shape[0] == 1:
+            return paired_plan(three_index, *rest)
+        return ring_plan(three_index, *rest)
+
     placed = (P("wide", None, "narrow"), P(), P(), P(), P(None, "wide"))
     return jax.shard_map(
         per_device, mesh=mesh, in_specs=placed, out_specs=P("wide", None, "narrow"), check_vma=False

time: 714 us -> 457 us (0.64)
  waiting for transfers between devices: 497 us -> 150 us
  Pallas kernels: 0 us -> 171 us
  matrix products: 137 us -> 0 us
  between operations: 21 us -> 59 us
  local copies, waits for them, and re-layouts: 9.23 us -> 30 us
    ppermute x10 -> x3, waiting for transfers between devices: 491 us -> 20.9 us  [passed_along(): lax.ppermute(array, axis, [(i, (i + by) % length) for i in range(length)])]
    pallas_call x0 -> x21, Pallas kernels: none -> 171 us  [the longest x14 92.1 us: amplitude_call(): pl.pallas_call(amplitude_kernel, grid=(count,), in_specs=[pl.BlockSpec(me...]
    dot_general x16 -> x0, matrix products: 137 us -> none  [the longest x5 60.5 us: per_device(): jnp.einsum('ijab,jpb->ipa', amplitude, visiting, preferred_element_type=j...]
    ppermute x0 -> x14, waiting for transfers between devices: none -> 129 us  [the longest x3 121 us: sibling(): return lax.ppermute(array, 'narrow', [(0, 1), (1, 0)])]
    add x4 -> x0, other arithmetic: 15.9 us -> none  [the longest x1 8.81 us: per_device(): return scattered + returned]
    dynamic_slice x2 -> x15, local copies, waits for them, and re-layouts: 0.76 us -> 16.2 us  [the longest x10 12.7 us: scalars(): block = jnp.asarray(np.array(slab.ids, np.int32))[here]]
    ppermute x10 -> x3, starting transfers between devices: 21.4 us -> 7.02 us  [passed_along(): lax.ppermute(array, axis, [(i, (i + by) % length) for i in range(length)])]
    ppermute x0 -> x14, starting transfers between devices: none -> 11.8 us  [the longest x11 9.13 us: moved(): lax.ppermute(slab.array, 'wide', pairs)]
  transfers between devices with their start and end apart: 12 -> 17, of which waited for: 9 -> 8; matrix products, arithmetic and copies ran while one was open for 21% -> 10% of each run, Pallas kernels for 0% -> 34%
where the time goes in v2:
time: 457 us; the launch traced here: 454 us
  Pallas kernels  171 us (37%)
  waiting for transfers between devices  150 us (33%)
  between operations  59 us (13%)
  local copies, waits for them, and re-layouts  30 us (7%)
  other arithmetic  25.7 us (6%)
  starting transfers between devices  18.9 us (4%)
    ppermute x3, waiting for transfers between devices, sibling(): return lax.ppermute(array, 'narrow', [(0, 1), (1, 0)])  121 us
    pallas_call x14, Pallas kernels, amplitude_call(): pl.pallas_call(amplitude_kernel, grid=(count,), in_specs=[pl.BlockSpec(me...  92.1 us
    pallas_call x7, Pallas kernels, density_call(): pl.pallas_call(kernel, grid=(length // tile,), in_specs=[rows_of(t[0]) fo...  78.9 us
    ppermute x3, waiting for transfers between devices, passed_along(): lax.ppermute(array, axis, [(i, (i + by) % length) for i in range(length)])  20.9 us
    dynamic_slice x10, local copies, waits for them, and re-layouts, scalars(): block = jnp.asarray(np.array(slab.ids, np.int32))[here]  12.7 us
  transfers between devices with their start and end apart: 17, of which 8 were waited for; matrix products, arithmetic and copies ran while one was open for 10% of the time, Pallas kernels for 34%

profile of v2, /device:TPU:3, one launch (start us, length us, event | category | flops | bytes accessed | tf_op | source)
XLA Modules:
  0.0 454.1 jit_solution(3625471606354173409)
XLA Ops:
  0.0 1.2 collective-permute-start.4
  2.3 66.9 %collective-permute-done.4.slab.refs_5_ = bf16[3072,512]{1,0:T(8,128)(2,1)} collective-permute-done((bf16[3072,512]{1,0:T(8,128)(2,1)}, bf16[3072,512]{1,0:T(8,128)(2,1)}, u32[]{:S(2)}, u32[]{:S(2)}) %collective-permute-start.4) | collective-permute-done | bytes 3145760 | tf_op jit(solution)/shard_map/ppermute | solution.py:231
  69.3 1.5 collective-permute-start.6
  70.8 1.3 collective-permute-start
  73.1 1.3 dynamic_slice.205
  75.0 1.3 dynamic_slice.213
  76.9 1.2 dynamic_slice.217
  78.8 1.3 dynamic_slice.221
  80.8 1.3 dynamic_slice.225
  82.7 1.3 dynamic_slice.229
  86.5 1.3 dynamic_slice.237
  90.3 1.2 dynamic_slice.245
  124.1 16.9 %collective-permute-done.1 = f32[1,6]{1,0:T(1,128)S(1)} collective-permute-done((f32[1,6]{1,0:T(1,128)S(1)}, f32[1,6]{1,0:T(1,128)S(1)}, u32[]{:S(2)}, u32[]{:S(2)}) %collective-permute-start.1) | collective-permute-done | bytes 56 | tf_op jit(solution)/shard_map/ppermute | solution.py:15
  141.1 3.3 collective-permute-done.2
  144.4 6.7 %collective-permute-start.3 = (f32[2,6]{1,0:T(2,128)S(1)}, f32[2,6]{1,0:T(2,128)S(1)}, u32[]{:S(2)}, u32[]{:S(2)}) collective-permute-start(f32[2,6]{1,0:T(2,128)S(1)} %pad_maximum_fusion.2), channel_id=1, source_target_pairs={{0,24},{2,26},{4,28},{6,30},{8,0},{10,2},{12,4},{14,6},{16,8},{18,... | collective-permute-start | bytes 152 | tf_op jit(solution)/shard_map/ppermute | solution.py:15
  156.9 6.4 %maximum_bitcast_fusion = bf16[1024,3072]{0,1:T(8,128)(2,1)} fusion(bf16[3072,512]{1,0:T(8,128)(2,1)} %collective-permute-done.4.slab.refs_5_, bf16[3072,512]{1,0:T(8,128)(2,1)} %bitcast.82), kind=kLoop, calls=%fused_computation.1 | loop fusion | flops 12582912 | bytes 12582912 | tf_op jit(solution)/shard_map/transpose | solution.py:253
  163.3 8.6 %copy.63.rows = bf16[1024,3072]{1,0:T(8,128)(2,1)} copy(bf16[1024,3072]{0,1:T(8,128)(2,1)} %maximum_bitcast_fusion) | data formatting | bytes 12582912 | tf_op jit(solution)/shard_map/transpose | solution.py:253
  172.0 5.4 %shard_map.190.refs_12_ = bf16[512,512]{1,0:T(8,128)(2,1)} custom-call(f32[1,2]{1,0:T(1,128)} %maximum_bitcast_fusion.1.scalars, bf16[1024,3072]{1,0:T(8,128)(2,1)} %copy.63.rows, bf16[3072,512]{1,0:T(8,128)(2,1)} %bitcast.83, f32[1024,1]{1,0:T(8,128)} %copy.64.vir_rows, f32[1,512]{1,0:T(1,128)} %bitcast.86), custom_call_target="tpu_custom_call" | custom-call | flops 1610612736 | bytes 6815744 | tf_op jit(solution)/shard_map/pallas_call | solution.py:139
  177.4 5.5 %shard_map.191.refs_13_ = bf16[512,512]{1,0:T(8,128)(2,1)} custom-call(f32[1,2]{1,0:T(1,128)} %maximum_bitcast_fusion.1.scalars, bf16[1024,3072]{1,0:T(8,128)(2,1)} %copy.63.rows, bf16[3072,512]{1,0:T(8,128)(2,1)} %collective-permute-done.4.slab.refs_5_, f32[1024,1]{1,0:T(8,128)} %copy.64.vir_rows, f32[1,512]{1,0:T(1,128)} %bitcast.98), custom_call_target="tpu_custom_call" | custom-call | flops 1610612736 | bytes 6815744 | tf_op jit(solution)/shard_map/pallas_call | solution.py:139
  182.9 1.7 copy-done.2
  184.6 5.5 %shard_map.192.refs_14_ = bf16[512,512]{1,0:T(8,128)(2,1)} custom-call(f32[1,2]{1,0:T(1,128)} %maximum_bitcast_fusion.2.scalars, bf16[1024,3072]{1,0:T(8,128)(2,1)} %copy.63.rows, bf16[3072,512]{1,0:T(8,128)(2,1)} %copy-done.2, f32[1024,1]{1,0:T(8,128)} %copy.64.vir_rows, f32[1,512]{1,0:T(1,128)} %bitcast.87), custom_call_target="tpu_custom_call" | custom-call | flops 1610612736 | bytes 6815744 | tf_op jit(solution)/shard_map/pallas_call | solution.py:139
  190.0 5.6 %shard_map.193.refs_15_ = bf16[512,512]{1,0:T(8,128)(2,1)} custom-call(f32[1,2]{1,0:T(1,128)} %maximum_bitcast_fusion.2.scalars, bf16[1024,3072]{1,0:T(8,128)(2,1)} %copy.63.rows, bf16[3072,512]{1,0:T(8,128)(2,1)} %collective-permute-done.6.slab.refs_7_, f32[1024,1]{1,0:T(8,128)} %copy.64.vir_rows, f32[1,512]{1,0:T(1,128)} %bitcast.99), custom_call_target="tpu_custom_call" | custom-call | flops 1610612736 | bytes 6815744 | tf_op jit(solution)/shard_map/pallas_call | solution.py:139
  206.1 3.5 collective-permute-start.8
  212.1 7.4 %shard_map.195.refs_5_.refs_9_ = bf16[1024,512]{1,0:T(8,128)(2,1)} custom-call(f32[1,2]{1,0:T(1,128)} %maximum_bitcast_fusion.4.scalars, bf16[1024,3072]{1,0:T(8,128)(2,1)} %copy.63.rows, bf16[3072,512]{1,0:T(8,128)(2,1)} %collective-permute-done.9.slab.refs_1_, f32[1024,1]{1,0:T(8,128)} %copy.64.vir_rows, f32[1,512]{1,0:T(1,128)} %bitcast.88), custom_call_target="tpu_custom_call" | custom-call | flops 3221225472 | bytes 10485760 | tf_op jit(solution)/shard_map/pallas_call | solution.py:139
  219.5 7.4 %shard_map.194.refs_4_.refs_8_ = bf16[1024,512]{1,0:T(8,128)(2,1)} custom-call(f32[1,2]{1,0:T(1,128)} %maximum_bitcast_fusion.3.scalars, bf16[1024,3072]{1,0:T(8,128)(2,1)} %copy.63.rows, bf16[3072,512]{1,0:T(8,128)(2,1)} %collective-permute-done.slab.refs_0_, f32[1024,1]{1,0:T(8,128)} %copy.64.vir_rows, f32[1,512]{1,0:T(1,128)} %bitcast.89), custom_call_target="tpu_custom_call" | custom-call | flops 3221225472 | bytes 10485760 | tf_op jit(solution)/shard_map/pallas_call | solution.py:139
  226.9 7.4 %shard_map.197.refs_7_.refs_11_ = bf16[1024,512]{1,0:T(8,128)(2,1)} custom-call(f32[1,2]{1,0:T(1,128)} %maximum_bitcast_fusion.6.scalars, bf16[1024,3072]{1,0:T(8,128)(2,1)} %copy.63.rows, bf16[3072,512]{1,0:T(8,128)(2,1)} %collective-permute-done.11.slab.refs_3_, f32[1024,1]{1,0:T(8,128)} %copy.64.vir_rows, f32[1,512]{1,0:T(1,128)} %bitcast.90), custom_call_target="tpu_custom_call" | custom-call | flops 3221225472 | bytes 10485760 | tf_op jit(solution)/shard_map/pallas_call | solution.py:139
  234.3 7.4 %shard_map.196.refs_6_.refs_10_ = bf16[1024,512]{1,0:T(8,128)(2,1)} custom-call(f32[1,2]{1,0:T(1,128)} %maximum_bitcast_fusion.5.scalars, bf16[1024,3072]{1,0:T(8,128)(2,1)} %copy.63.rows, bf16[3072,512]{1,0:T(8,128)(2,1)} %collective-permute-done.10.slab.refs_2_, f32[1024,1]{1,0:T(8,128)} %copy.64.vir_rows, f32[1,512]{1,0:T(1,128)} %bitcast.91), custom_call_target="tpu_custom_call" | custom-call | flops 3221225472 | bytes 10485760 | tf_op jit(solution)/shard_map/pallas_call | solution.py:139
  241.7 12.5 %shard_map.198.refs_8_ = f32[3072,512]{1,0:T(8,128)} custom-call(bf16[3072,512]{1,0:T(8,128)(2,1)} %collective-permute-done.slab.refs_0_, bf16[3072,512]{1,0:T(8,128)(2,1)} %collective-permute-done.9.slab.refs_1_, bf16[3072,512]{1,0:T(8,128)(2,1)} %collective-permute-done.10.slab.refs_2_, bf16[3072,512]{1,0:T(8,128)(2,1)} %collective-permute-done.11.slab.refs_3_, ...), custom_call_target="tpu_custom_call" | custom-call | flops 6442450944 | bytes 20971520 | tf_op jit(solution)/shard_map/pallas_call | solution.py:190
  254.3 19.4 %shard_map.199.refs_8_ = f32[3072,512]{1,0:T(8,128)} custom-call(bf16[3072,512]{1,0:T(8,128)(2,1)} %collective-permute-done.slab.refs_0_, bf16[3072,512]{1,0:T(8,128)(2,1)} %collective-permute-done.9.slab.refs_1_, bf16[3072,512]{1,0:T(8,128)(2,1)} %collective-permute-done.10.slab.refs_2_, bf16[3072,512]{1,0:T(8,128)(2,1)} %collective-permute-done.11.slab.refs_3_, ...), custom_call_target="tpu_custom_call" | custom-call | flops 12884901888 | bytes 35651584 | tf_op jit(solution)/shard_map/pallas_call | solution.py:190
  273.7 3.4 collective-permute-done.8.slab.refs_2_
  277.9 4.5 collective-permute-done.7.slab.refs_0_
  283.4 4.5 broadcast_select_fusion
  303.2 7.4 %shard_map.202.refs_6_ = bf16[1024,512]{1,0:T(8,128)(2,1)} custom-call(f32[1,2]{1,0:T(1,128)} %maximum_bitcast_fusion.9.scalars, bf16[1024,3072]{1,0:T(8,128)(2,1)} %copy.63.rows, bf16[3072,512]{1,0:T(8,128)(2,1)} %collective-permute-done.8.slab.refs_2_, f32[1024,1]{1,0:T(8,128)} %copy.64.vir_rows, f32[1,512]{1,0:T(1,128)} %bitcast.92), custom_call_target="tpu_custom_call" | custom-call | flops 3221225472 | bytes 10485760 | tf_op jit(solution)/shard_map/pallas_call | solution.py:139
  310.6 7.4 %shard_map.200.refs_4_ = bf16[1024,512]{1,0:T(8,128)(2,1)} custom-call(f32[1,2]{1,0:T(1,128)} %maximum_bitcast_fusion.7.scalars, bf16[1024,3072]{1,0:T(8,128)(2,1)} %copy.63.rows, bf16[3072,512]{1,0:T(8,128)(2,1)} %collective-permute-done.7.slab.refs_0_, f32[1024,1]{1,0:T(8,128)} %copy.64.vir_rows, f32[1,512]{1,0:T(1,128)} %bitcast.93), custom_call_target="tpu_custom_call" | custom-call | flops 3221225472 | bytes 10485760 | tf_op jit(solution)/shard_map/pallas_call | solution.py:139
  318.0 7.4 %shard_map.203.refs_7_ = bf16[1024,512]{1,0:T(8,128)(2,1)} custom-call(f32[1,2]{1,0:T(1,128)} %maximum_bitcast_fusion.10.scalars, bf16[1024,3072]{1,0:T(8,128)(2,1)} %copy.63.rows, bf16[3072,512]{1,0:T(8,128)(2,1)} %collective-permute-done.14.slab.refs_3_, f32[1024,1]{1,0:T(8,128)} %copy.64.vir_rows, f32[1,512]{1,0:T(1,128)} %bitcast.94), custom_call_target="tpu_custom_call" | custom-call | flops 3221225472 | bytes 10485760 | tf_op jit(solution)/shard_map/pallas_call | solution.py:139
  325.4 7.4 %shard_map.201.refs_5_ = bf16[1024,512]{1,0:T(8,128)(2,1)} custom-call(f32[1,2]{1,0:T(1,128)} %maximum_bitcast_fusion.8.scalars, bf16[1024,3072]{1,0:T(8,128)(2,1)} %copy.63.rows, bf16[3072,512]{1,0:T(8,128)(2,1)} %collective-permute-done.13.slab.refs_1_, f32[1024,1]{1,0:T(8,128)} %copy.64.vir_rows, f32[1,512]{1,0:T(1,128)} %bitcast.95), custom_call_target="tpu_custom_call" | custom-call | flops 3221225472 | bytes 10485760 | tf_op jit(solution)/shard_map/pallas_call | solution.py:139
  332.8 13.8 %shard_map.205.refs_2_ = f32[3072,512]{1,0:T(8,128)} custom-call(bf16[3072,512]{1,0:T(8,128)(2,1)} %collective-permute-done.7.slab.refs_0_, bf16[3072,512]{1,0:T(8,128)(2,1)} %collective-permute-done.13.slab.refs_1_, bf16[3072,512]{1,0:T(8,128)(2,1)} %collective-permute-done.8.slab.refs_2_, bf16[3072,512]{1,0:T(8,128)(2,1)} %collective-permute-done.14.slab.refs_3_, ...), custom_call_target="tpu_custom_call" | custom-call | flops 6442450944 | bytes 27262976 | tf_op jit(solution)/shard_map/pallas_call | solution.py:190
  346.7 13.8 %shard_map.204.refs_2_ = f32[3072,512]{1,0:T(8,128)} custom-call(bf16[3072,512]{1,0:T(8,128)(2,1)} %collective-permute-done.7.slab.refs_0_, bf16[3072,512]{1,0:T(8,128)(2,1)} %collective-permute-done.13.slab.refs_1_, bf16[3072,512]{1,0:T(8,128)(2,1)} %collective-permute-done.8.slab.refs_2_, bf16[3072,512]{1,0:T(8,128)(2,1)} %collective-permute-done.14.slab.refs_3_, ...), custom_call_target="tpu_custom_call" | custom-call | flops 6442450944 | bytes 27262976 | tf_op jit(solution)/shard_map/pallas_call | solution.py:190
  360.5 1.7 copy-done
  362.2 5.5 %shard_map.208.refs_1_ = bf16[512,512]{1,0:T(8,128)(2,1)} custom-call(f32[1,2]{1,0:T(1,128)} %maximum_bitcast_fusion.11.scalars, bf16[1024,3072]{1,0:T(8,128)(2,1)} %copy.63.rows, bf16[3072,512]{1,0:T(8,128)(2,1)} %copy-done, f32[1024,1]{1,0:T(8,128)} %copy.64.vir_rows, f32[1,512]{1,0:T(1,128)} %bitcast.96), custom_call_target="tpu_custom_call" | custom-call | flops 1610612736 | bytes 6815744 | tf_op jit(solution)/shard_map/pallas_call | solution.py:139
  367.7 5.2 %shard_map.209 = bf16[1536,512]{1,0:T(8,128)(2,1)} custom-call(bf16[3072,512]{1,0:T(8,128)(2,1)} %copy-done, bf16[512,512]{1,0:T(8,128)(2,1)} %shard_map.208.refs_1_, f32[3072,512]{1,0:T(8,128)} %shard_map.204.refs_2_), custom_call_target="tpu_custom_call" | custom-call | flops 805306368 | bytes 6553600 | tf_op jit(solution)/shard_map/pallas_call | solution.py:190
  372.9 5.2 %shard_map.210 = bf16[1536,512]{1,0:T(8,128)(2,1)} custom-call(bf16[3072,512]{1,0:T(8,128)(2,1)} %copy-done, bf16[512,512]{1,0:T(8,128)(2,1)} %shard_map.208.refs_1_, f32[3072,512]{1,0:T(8,128)} %shard_map.204.refs_2_), custom_call_target="tpu_custom_call" | custom-call | flops 805306368 | bytes 6553600 | tf_op jit(solution)/shard_map/pallas_call | solution.py:190
  378.1 1.2 collective-permute-start.15
  379.5 5.5 %shard_map.206.refs_1_ = bf16[512,512]{1,0:T(8,128)(2,1)} custom-call(f32[1,2]{1,0:T(1,128)} %maximum_bitcast_fusion.11.scalars, bf16[1024,3072]{1,0:T(8,128)(2,1)} %copy.63.rows, bf16[3072,512]{1,0:T(8,128)(2,1)} %copy-done, f32[1024,1]{1,0:T(8,128)} %copy.64.vir_rows, f32[1,512]{1,0:T(1,128)} %bitcast.97), custom_call_target="tpu_custom_call" | custom-call | flops 1610612736 | bytes 6815744 | tf_op jit(solution)/shard_map/pallas_call | solution.py:139
  385.0 8.9 %shard_map.207 = f32[3072,512]{1,0:T(8,128)} custom-call(bf16[3072,512]{1,0:T(8,128)(2,1)} %copy-done, bf16[512,512]{1,0:T(8,128)(2,1)} %shard_map.206.refs_1_, f32[3072,512]{1,0:T(8,128)} %shard_map.205.refs_2_), custom_call_target="tpu_custom_call" | custom-call | flops 1610612736 | bytes 16252928 | tf_op jit(solution)/shard_map/pallas_call | solution.py:190
  393.9 20.0 %collective-permute-done.15 = bf16[1536,512]{1,0:T(8,128)(2,1)S(1)} collective-permute-done((bf16[1536,512]{1,0:T(8,128)(2,1)S(1)}, bf16[1536,512]{1,0:T(8,128)(2,1)S(1)}, u32[]{:S(2)}, u32[]{:S(2)}) %collective-permute-start.15) | collective-permute-done | bytes 1572896 | tf_op jit(solution)/shard_map/ppermute | solution.py:231
  413.9 33.7 %collective-permute-done.16 = bf16[1536,512]{1,0:T(8,128)(2,1)S(1)} collective-permute-done((bf16[1536,512]{1,0:T(8,128)(2,1)}, bf16[1536,512]{1,0:T(8,128)(2,1)S(1)}, u32[]{:S(2)}, u32[]{:S(2)}) %collective-permute-start.16) | collective-permute-done | bytes 1572896 | tf_op jit(solution)/shard_map/ppermute | solution.py:231
  447.6 6.5 %add_bitcast_fusion = f32[1,3072,512]{2,1,0:T(8,128)} fusion(f32[3072,512]{1,0:T(8,128)} %shard_map.207, bf16[1536,512]{1,0:T(8,128)(2,1)S(1)} %collective-permute-done.16, bf16[1536,512]{1,0:T(8,128)(2,1)S(1)} %collective-permute-done.15), kind=kLoop, calls=%fused_computation.2 | loop fusion | flops 7864320 | bytes 15728640 | tf_op jit(solution)/shard_map/broadcast_in_dim | solution.py:306
  (59 shorter events, 20.0 us)
Async XLA Ops:
  0.0 69.3 %collective-permute-start.4 = (bf16[3072,512]{1,0:T(8,128)(2,1)}, bf16[3072,512]{1,0:T(8,128)(2,1)}, u32[]{:S(2)}, u32[]{:S(2)}) collective-permute-start(bf16[3072,512]{1,0:T(8,128)(2,1)} %bitcast.78), channel_id=1, source_target_pairs={{0,1},{1,0},{2,3},{3,2},{4,5},{5,4},{6,7},{7,6},{8,9},{9,8},{10,11... | collective-permute-start | bytes 9437192 | tf_op jit(solution)/shard_map/ppermute | solution.py:231
  1.2 170.7 %collective-permute-start.9 = (bf16[3072,512]{1,0:T(8,128)(2,1)}, bf16[3072,512]{1,0:T(8,128)(2,1)}, u32[]{:S(2)}, u32[]{:S(2)}) collective-permute-start(bf16[3072,512]{1,0:T(8,128)(2,1)} %bitcast.79), channel_id=1, source_target_pairs={{0,6},{2,4},{4,2},{6,0},{8,14},{10,12},{12,10},{14,8},{16,22},{18,... | collective-permute-start | bytes 9437192 | tf_op jit(solution)/shard_map/ppermute | solution.py:225
  2.3 180.5 %collective-permute-start.5 = (bf16[3072,512]{1,0:T(8,128)(2,1)}, bf16[3072,512]{1,0:T(8,128)(2,1)S(1)}, u32[]{:S(2)}, u32[]{:S(2)}) collective-permute-start(bf16[3072,512]{1,0:T(8,128)(2,1)} %bitcast.80), channel_id=1, source_target_pairs={{0,2},{2,0},{4,6},{6,4},{8,10},{10,8},{12,14},{14,12},{16,18},{18,... | collective-permute-start | bytes 9437192 | tf_op jit(solution)/shard_map/ppermute | solution.py:225
  69.3 120.8 %collective-permute-start.6 = (bf16[3072,512]{1,0:T(8,128)(2,1)}, bf16[3072,512]{1,0:T(8,128)(2,1)}, u32[]{:S(2)}, u32[]{:S(2)}) collective-permute-start(bf16[3072,512]{1,0:T(8,128)(2,1)} %collective-permute-done.4.slab.refs_5_), channel_id=1, source_target_pairs={{0,2},{2,0},{4,6},{6,4},{8,10},{10,8},{12,14},{14,12},{16,18},{18,... | collective-permute-start | bytes 9437192 | tf_op jit(solution)/shard_map/ppermute | solution.py:225
  70.8 124.8 %collective-permute-start = (bf16[3072,512]{1,0:T(8,128)(2,1)}, bf16[3072,512]{1,0:T(8,128)(2,1)}, u32[]{:S(2)}, u32[]{:S(2)}) collective-permute-start(bf16[3072,512]{1,0:T(8,128)(2,1)} %bitcast.81), channel_id=1, source_target_pairs={{0,24},{2,26},{4,12},{6,14},{8,0},{10,2},{12,20},{14,22},{16,8},{1... | collective-permute-start | bytes 9437192 | tf_op jit(solution)/shard_map/ppermute | solution.py:225
  72.8 68.3 %collective-permute-start.1 = (f32[1,6]{1,0:T(1,128)S(1)}, f32[1,6]{1,0:T(1,128)S(1)}, u32[]{:S(2)}, u32[]{:S(2)}) collective-permute-start(f32[1,6]{1,0:T(1,128)S(1)} %get-tuple-element.49), channel_id=1, source_target_pairs={{0,30},{2,0},{4,2},{6,4},{8,6},{10,8},{12,10},{14,12},{16,14},{18,... | collective-permute-start | bytes 80 | tf_op jit(solution)/shard_map/ppermute | solution.py:15
  112.0 51.3 %copy-start.4 = (f32[512]{0:T(512)}, f32[512]{0:T(512)S(1)}, u32[]{:S(2)}) copy-start(f32[512]{0:T(512)S(1)} %get-tuple-element.13) | copy-start | bytes 6148
  112.0 51.3 %copy-start.5 = (f32[512]{0:T(512)}, f32[512]{0:T(512)S(1)}, u32[]{:S(2)}) copy-start(f32[512]{0:T(512)S(1)} %get-tuple-element.14) | copy-start | bytes 6148
  141.1 3.4 collective-permute-start.2
  144.4 7.4 %collective-permute-start.3 = (f32[2,6]{1,0:T(2,128)S(1)}, f32[2,6]{1,0:T(2,128)S(1)}, u32[]{:S(2)}, u32[]{:S(2)}) collective-permute-start(f32[2,6]{1,0:T(2,128)S(1)} %pad_maximum_fusion.2), channel_id=1, source_target_pairs={{0,24},{2,26},{4,28},{6,30},{8,0},{10,2},{12,4},{14,6},{16,8},{18,... | collective-permute-start | bytes 152 | tf_op jit(solution)/shard_map/ppermute | solution.py:15
  172.0 55.0 %collective-permute-start.11 = (bf16[3072,512]{1,0:T(8,128)(2,1)}, bf16[3072,512]{1,0:T(8,128)(2,1)}, u32[]{:S(2)}, u32[]{:S(2)}) collective-permute-start(bf16[3072,512]{1,0:T(8,128)(2,1)} %collective-permute-done.9.slab.refs_1_), channel_id=1, source_target_pairs={{0,2},{2,0},{4,6},{6,4},{8,10},{10,8},{12,14},{14,12},{16,18},{18,... | collective-permute-start | bytes 9437192 | tf_op jit(solution)/shard_map/ppermute | solution.py:225
  182.9 1.7 copy-start.2
  190.0 16.1 %copy-start.1 = (bf16[1,3072,512]{2,1,0:T(8,128)(2,1)S(1)}, bf16[1,3072,512]{2,1,0:T(8,128)(2,1)}, u32[]{:S(2)}) copy-start(bf16[1,3072,512]{2,1,0:T(8,128)(2,1)} %param.20) | copy-start | bytes 9437188
  195.7 38.7 %collective-permute-start.10 = (bf16[3072,512]{1,0:T(8,128)(2,1)}, bf16[3072,512]{1,0:T(8,128)(2,1)}, u32[]{:S(2)}, u32[]{:S(2)}) collective-permute-start(bf16[3072,512]{1,0:T(8,128)(2,1)} %collective-permute-done.slab.refs_0_), channel_id=1, source_target_pairs={{0,2},{2,0},{4,6},{6,4},{8,10},{10,8},{12,14},{14,12},{16,18},{18,... | collective-permute-start | bytes 9437192 | tf_op jit(solution)/shard_map/ppermute | solution.py:225
  206.1 71.0 %collective-permute-start.8 = (bf16[3072,512]{1,0:T(8,128)(2,1)S(1)}, bf16[3072,512]{1,0:T(8,128)(2,1)}, u32[]{:S(2)}, u32[]{:S(2)}) collective-permute-start(bf16[3072,512]{1,0:T(8,128)(2,1)S(1)} %bitcast.85), channel_id=1, source_target_pairs={{0,8},{2,10},{4,28},{6,30},{8,16},{10,18},{12,4},{14,6},{16,24},{1... | collective-permute-start | bytes 9437192 | tf_op jit(solution)/shard_map/ppermute | solution.py:225
  212.1 70.3 %collective-permute-start.7 = (bf16[3072,512]{1,0:T(8,128)(2,1)}, bf16[3072,512]{1,0:T(8,128)(2,1)}, u32[]{:S(2)}, u32[]{:S(2)}) collective-permute-start(bf16[3072,512]{1,0:T(8,128)(2,1)} %collective-permute-done.slab.refs_0_), channel_id=1, source_target_pairs={{0,6},{2,4},{4,2},{6,0},{8,14},{10,12},{12,10},{14,8},{16,22},{18,... | collective-permute-start | bytes 9437192 | tf_op jit(solution)/shard_map/ppermute | solution.py:225
  254.3 28.5 %copy-start.6 = (pred[16]{0:T(512)(128)(4,1)S(1)}, pred[16]{0:T(512)(128)(4,1)}, u32[]{:S(2)}) copy-start(pred[16]{0:T(512)(128)(4,1)} %constant.185.clone) | copy-start | bytes 52
  277.1 40.9 %collective-permute-start.14 = (bf16[3072,512]{1,0:T(8,128)(2,1)}, bf16[3072,512]{1,0:T(8,128)(2,1)}, u32[]{:S(2)}, u32[]{:S(2)}) collective-permute-start(bf16[3072,512]{1,0:T(8,128)(2,1)} %collective-permute-done.8.slab.refs_2_), channel_id=1, source_target_pairs={{0,2},{2,0},{4,6},{6,4},{8,10},{10,8},{12,14},{14,12},{16,18},{18,... | collective-permute-start | bytes 9437192 | tf_op jit(solution)/shard_map/ppermute | solution.py:225
  282.4 43.0 %collective-permute-start.13 = (bf16[3072,512]{1,0:T(8,128)(2,1)}, bf16[3072,512]{1,0:T(8,128)(2,1)}, u32[]{:S(2)}, u32[]{:S(2)}) collective-permute-start(bf16[3072,512]{1,0:T(8,128)(2,1)} %collective-permute-done.7.slab.refs_0_), channel_id=1, source_target_pairs={{0,2},{2,0},{4,6},{6,4},{8,10},{10,8},{12,14},{14,12},{16,18},{18,... | collective-permute-start | bytes 9437192 | tf_op jit(solution)/shard_map/ppermute | solution.py:225
  287.9 72.6 %collective-permute-start.12 = (bf16[3072,512]{1,0:T(8,128)(2,1)}, bf16[3072,512]{1,0:T(8,128)(2,1)S(1)}, u32[]{:S(2)}, u32[]{:S(2)}) collective-permute-start(bf16[3072,512]{1,0:T(8,128)(2,1)} %broadcast_select_fusion), channel_id=1, source_target_pairs={{0,8},{2,4},{4,2},{6,30},{8,16},{10,12},{12,10},{14,6},{16,24},{18... | collective-permute-start | bytes 9437192 | tf_op jit(solution)/shard_map/ppermute | solution.py:225
  360.5 1.7 copy-start
  372.9 5.2 %copy-start.3 = (bf16[1536,512]{1,0:T(8,128)(2,1)S(1)}, bf16[1536,512]{1,0:T(8,128)(2,1)}, u32[]{:S(2)}) copy-start(bf16[1536,512]{1,0:T(8,128)(2,1)} %shard_map.209) | copy-start | bytes 4718596
  378.1 35.9 %collective-permute-start.15 = (bf16[1536,512]{1,0:T(8,128)(2,1)S(1)}, bf16[1536,512]{1,0:T(8,128)(2,1)S(1)}, u32[]{:S(2)}, u32[]{:S(2)}) collective-permute-start(bf16[1536,512]{1,0:T(8,128)(2,1)S(1)} %copy-done.3), channel_id=1, source_target_pairs={{0,1},{1,0},{2,3},{3,2},{4,5},{5,4},{6,7},{7,6},{8,9},{9,8},{10,11... | collective-permute-start | bytes 4718600 | tf_op jit(solution)/shard_map/ppermute | solution.py:231
  379.3 68.3 %collective-permute-start.16 = (bf16[1536,512]{1,0:T(8,128)(2,1)}, bf16[1536,512]{1,0:T(8,128)(2,1)S(1)}, u32[]{:S(2)}, u32[]{:S(2)}) collective-permute-start(bf16[1536,512]{1,0:T(8,128)(2,1)} %shard_map.210), channel_id=1, source_target_pairs={{0,1},{1,0},{2,3},{3,2},{4,5},{5,4},{6,7},{7,6},{8,9},{9,8},{10,11... | collective-permute-start | bytes 4718600 | tf_op jit(solution)/shard_map/ppermute | solution.py:231

commit v3 on v0

--- a/solution.py
+++ b/solution.py
@@ -1,9 +1,14 @@
 import jax
 import jax.numpy as jnp
+import numpy as np
 from jax import lax
+from jax.experimental import pallas as pl
+from jax.experimental.pallas import tpu as pltpu
 from jax.sharding import PartitionSpec as P
 
 ROUNDS = 5
+PIECES = 2
+VMEM = 56 * 1024 * 1024
 
 
 def passed_along(array, axis, by):
@@ -26,7 +31,7 @@
     return (weight * coulomb / denominator).astype(jnp.bfloat16)
 
 
-def per_device(three_index, orbital_map, occ_energy, vir_energy, pair_kept):
+def ring_plan(three_index, orbital_map, occ_energy, vir_energy, pair_kept):
     occ_count = three_index.shape[0]
     vir_count = three_index.shape[2]
     blocks = lax.axis_size("wide")
@@ -79,7 +84,370 @@
     return scattered + returned
 
 
+class Routes:
+    def __init__(self, blocks):
+        self.blocks = blocks
+        everyone = range(blocks)
+        self.lead = [self.place(w)[1] == self.place(w)[2] for w in everyone]
+        self.swap = [(w, w ^ 1) for w in everyone]
+        onward = [(w, self.along_z(w, 1)) for w in everyone]
+        backward = [(w, self.along_z(w, -1)) for w in everyone]
+        across = [(w, self.across_x(w)) for w in everyone]
+        self.rounds = [
+            self.either(onward, across),
+            self.either(across, onward),
+            self.either(backward, across),
+            self.either(across, backward),
+            self.either(backward, across),
+        ]
+
+    def place(self, w):
+        return w // 4, (w // 2) % 2, w % 2
+
+    def along_z(self, w, step):
+        z, x, core = self.place(w)
+        z = (z + (step if x == 1 else -step)) % (self.blocks // 4)
+        return (z * 2 + x) * 2 + core
+
+    def across_x(self, w):
+        z, x, core = self.place(w)
+        return (z * 2 + 1 - x) * 2 + 1 - core
+
+    def either(self, of_lead, of_other):
+        return [a if lead else b for lead, a, b in zip(self.lead, of_lead, of_other)]
+
+    def moved(self, ids, pairs):
+        out = [0] * self.blocks
+        for source, target in pairs:
+            out[target] = ids[source]
+        return out
+
+
+class Slab:
+    def __init__(self, pieces, ids, far=False):
+        self.pieces = list(pieces)
+        self.ids = ids
+        self.far = far
+
+
+def copy_in(sources, place, sems, start):
+    row = 0
+    for index, source in enumerate(sources):
+        rows = source.shape[0]
+        copy = pltpu.make_async_copy(source, place.at[pl.ds(row, rows)], sems.at[index])
+        copy.start() if start else copy.wait()
+        row += rows
+
+
+def amplitude_call(table, base, slabs, turned, vir_rows, vir_cols):
+    count = len(slabs)
+    pieces = len(slabs[0].pieces)
+    rows, aux = turned.shape
+    cols = slabs[0].pieces[0].shape[1]
+    tile = cols
+    blocks = rows // tile
+
+    def kernel(scalars, *refs):
+        sources = [refs[s * pieces : (s + 1) * pieces] for s in range(count)]
+        row_ref, vir_row_ref, vir_col_ref, out, held, sems = refs[count * pieces :]
+        s, j = pl.program_id(0), pl.program_id(1)
+        slot = s % 2
+
+        def fetch(which, start):
+            for index in range(count):
+
+                @pl.when(which == index)
+                def _(index=index):
+                    copy_in(sources[index], held.at[index % 2], sems.at[index % 2], start)
+
+        @pl.when(jnp.logical_and(s == 0, j == 0))
+        def _():
+            fetch(s, True)
+
+        @pl.when(j == 0)
+        def _():
+            fetch(s, False)
+            fetch(s + 1, True)
+
+        coulomb = jnp.dot(row_ref[...], held[slot], preferred_element_type=jnp.float32)
+        denominator = (vir_row_ref[...] + vir_col_ref[0]) - scalars[base + s, 0]
+        out[0] = (scalars[base + s, 1] * coulomb / denominator).astype(out.dtype)
+
+    def block(s, j):
+        return jnp.where(s % 2 == 1, blocks - 1 - j, j)
+
+    return pl.pallas_call(
+        kernel,
+        grid=(count, blocks),
+        in_specs=[pl.BlockSpec(memory_space=pltpu.SMEM)]
+        + [pl.BlockSpec(memory_space=pl.ANY)] * (count * pieces)
+        + [
+            pl.BlockSpec((tile, aux), lambda s, j: (block(s, j), 0)),
+            pl.BlockSpec((tile, 1), lambda s, j: (block(s, j), 0)),
+            pl.BlockSpec((1, 1, cols), lambda s, j: (s, 0, 0)),
+        ],
+        out_specs=pl.BlockSpec((1, tile, cols), lambda s, j: (s, block(s, j), 0)),
+        out_shape=jax.ShapeDtypeStruct((count, rows, cols), jnp.bfloat16),
+        scratch_shapes=[
+            pltpu.VMEM((2, aux, cols), jnp.bfloat16),
+            pltpu.SemaphoreType.DMA((2, pieces)),
+        ],
+        compiler_params=pltpu.CompilerParams(vmem_limit_bytes=VMEM),
+        cost_estimate=pl.CostEstimate(
+            flops=2 * count * rows * aux * cols,
+            bytes_accessed=2 * (count * rows * aux + count * aux * cols + count * rows * cols),
+            transcendentals=0,
+        ),
+    )(table, *[p for s in slabs for p in s.pieces], turned, vir_rows, vir_cols)
+
+
+def density_call(terms, parts, out_dtype, rows=None):
+    count = len(terms)
+    pieces = len(terms[0][0].pieces)
+    piece_rows, depth = terms[0][0].pieces[0].shape
+    aux = piece_rows * pieces
+    cols = depth
+    begin, length = rows or (0, aux)
+    tile = 512
+    while length % tile or begin % tile or piece_rows % tile:
+        tile //= 2
+    first, steps, in_piece = begin // tile, length // tile, piece_rows // tile
+    counts = [len(part) for part in parts]
+    parts = [p for part in parts for p in part]
+
+    def kernel(*refs):
+        sources = [refs[s * pieces : (s + 1) * pieces] for s in range(count)]
+        refs = refs[count * pieces :]
+        amps, part_refs = refs[:count], refs[count : count + len(parts)]
+        out, left, right, left_sems, right_sems = refs[count + len(parts) :]
+        step = pl.program_id(0)
+        slot = step % 2
+
+        def amp_copies():
+            for s, (_, _, place, block) in enumerate(terms):
+                yield pltpu.make_async_copy(
+                    amps[s].at[place, pl.ds(block * cols, cols), :],
+                    right.at[:, pl.ds(s * depth, depth)],
+                    right_sems.at[s],
+                )
+
+        def fetch(which, start):
+            at = which + first
+            for piece in range(pieces):
+
+                @pl.when(jnp.logical_and(which < steps, at // in_piece == piece))
+                def _(piece=piece):
+                    row = pl.multiple_of((at - piece * in_piece) * tile, tile)
+                    for s in range(count):
+                        copy = pltpu.make_async_copy(
+                            sources[s][piece].at[pl.ds(row, tile), :],
+                            left.at[which % 2, :, pl.ds(s * depth, depth)],
+                            left_sems.at[which % 2, s],
+                        )
+                        copy.start() if start else copy.wait()
+
+        @pl.when(step == 0)
+        def _():
+            for copy in amp_copies():
+                copy.start()
+            fetch(step, True)
+            for copy in amp_copies():
+                copy.wait()
+
+        fetch(step, False)
+        fetch(step + 1, True)
+        total = lax.dot_general(
+            left[slot], right[...], (((1,), (1,)), ((), ())), preferred_element_type=jnp.float32
+        )
+        at = 0
+        for many in counts:
+            part = part_refs[at][...]
+            for index in range(1, many):
+                part = jnp.where(step >= index * steps // many, part_refs[at + index][...], part)
+            total = total + part.astype(jnp.float32)
+            at += many
+        out[...] = total.astype(out.dtype)
+
+    def rows_of(many, index):
+        within = steps // many
+        return pl.BlockSpec((tile, cols), lambda i: (jnp.clip(i - index * within, 0, within - 1), 0))
+
+    bytes_moved = 2 * count * (length * depth + cols * depth)
+    bytes_moved += sum(length * cols * p.dtype.itemsize for p in parts)
+    return pl.pallas_call(
+        kernel,
+        grid=(steps,),
+        in_specs=[pl.BlockSpec(memory_space=pl.ANY)] * (count * pieces + count)
+        + [rows_of(many, index) for many in counts for index in range(many)],
+        out_specs=pl.BlockSpec((tile, cols), lambda i: (i, 0)),
+        out_shape=jax.ShapeDtypeStruct((length, cols), out_dtype),
+        scratch_shapes=[
+            pltpu.VMEM((2, tile, count * depth), jnp.bfloat16),
+            pltpu.VMEM((cols, count * depth), jnp.bfloat16),
+            pltpu.SemaphoreType.DMA((2, count)),
+            pltpu.SemaphoreType.DMA((count,)),
+        ],
+        compiler_params=pltpu.CompilerParams(vmem_limit_bytes=VMEM),
+        cost_estimate=pl.CostEstimate(
+            flops=2 * length * depth * cols * count,
+            bytes_accessed=bytes_moved + length * cols * jnp.dtype(out_dtype).itemsize,
+            transcendentals=0,
+        ),
+    )(*[p for t in terms for p in t[0].pieces], *[t[1] for t in terms], *parts)
+
+
+def paired_plan(three_index, orbital_map, occ_energy, vir_energy, pair_kept):
+    blocks = lax.axis_size("wide")
+    routes = Routes(blocks)
+    here = lax.axis_index("wide")
+    side = lax.axis_index("narrow")
+    aux, vir_count = three_index.shape[1:]
+    piece_rows = aux // PIECES
+    lead = jnp.asarray(np.array(routes.lead))[here]
+
+    def moved(slab, pairs):
+        sent = [lax.ppermute(p, "wide", pairs) for p in slab.pieces]
+        return Slab(sent, routes.moved(slab.ids, pairs), slab.far)
+
+    def swapped(slab):
+        return moved(slab, routes.swap)
+
+    def chosen(slab_lead, slab_other):
+        pairs = zip(slab_lead.pieces, slab_other.pieces)
+        return Slab(
+            [jnp.where(lead, a, b) for a, b in pairs],
+            routes.either(slab_lead.ids, slab_other.ids),
+            slab_lead.far,
+        )
+
+    def sibling(array):
+        return lax.ppermute(array, "narrow", [(0, 1), (1, 0)])
+
+    def after(slab, other):
+        pairs = zip(slab.pieces, other.pieces)
+        return Slab([lax.optimization_barrier(pair)[0] for pair in pairs], slab.ids, slab.far)
+
+    whole = three_index[0]
+    own = Slab([whole[i * piece_rows : (i + 1) * piece_rows] for i in range(PIECES)], list(range(blocks)))
+    r1 = moved(own, routes.rounds[0])
+    own_far = Slab([sibling(p) for p in own.pieces], own.ids, True)
+    mate = swapped(own)
+    ahead = [passed_along(pair_kept[r].astype(jnp.float32), "wide", -r) for r in range(1, ROUNDS + 1)]
+    r2 = moved(chosen(r1, own), routes.rounds[1])
+    s1, s2 = swapped(r1), swapped(r2)
+    mate_far = swapped(own_far)
+
+    labels = jnp.arange(occ_energy.shape[0], dtype=jnp.int32)
+    picked = orbital_map[:, None] == labels[None, :]
+    energy = jnp.sum(jnp.where(picked, occ_energy[None, :], 0.0), axis=1)
+    kept = jnp.concatenate([pair_kept[:, 0].astype(jnp.float32), *ahead])
+
+    def table_of(slabs):
+        ids = np.array([s.ids for s in slabs], np.int32).T
+        back = (np.arange(blocks)[:, None] - ids) % blocks
+        forth = (ids - np.arange(blocks)[:, None]) % blocks
+        which = np.where(back <= ROUNDS, back, ROUNDS + forth)
+        block, which = jnp.asarray(np.stack([ids, which]))[:, here]
+        places = jnp.arange(blocks, dtype=jnp.int32)
+        mine = jnp.sum(jnp.where(places == here, energy, 0.0))
+        theirs = jnp.sum(jnp.where(block[:, None] == places[None, :], energy[None, :], 0.0), axis=1)
+        spots = jnp.arange(kept.shape[0], dtype=jnp.int32)
+        weight = jnp.sum(jnp.where(which[:, None] == spots[None, :], kept[None, :], 0.0), axis=1)
+        return jnp.stack([mine + theirs, weight], axis=1)
+
+    vir_near = lax.dynamic_slice_in_dim(vir_energy, side * vir_count, vir_count)
+    vir_far = lax.dynamic_slice_in_dim(vir_energy, (1 - side) * vir_count, vir_count)
+    vir_rows = jnp.concatenate([vir_near, vir_far])[:, None]
+    turned = jnp.concatenate([whole, jnp.concatenate(own_far.pieces)], axis=1).T
+    turned_near = whole.T
+
+    def amps(table, base, slabs, both):
+        cols = jnp.stack([vir_far if s.far else vir_near for s in slabs])[:, None, :]
+        if both:
+            return amplitude_call(table, base, slabs, turned, vir_rows, cols)
+        return amplitude_call(table, base, slabs, turned_near, vir_near[:, None], cols)
+
+    def terms(slabs, stack, block):
+        return [(s, stack, place, block) for place, s in enumerate(slabs)]
+
+    near, far = 0, 1
+    r3 = moved(chosen(mate, r2), routes.rounds[2])
+    r4_sent = chosen(r3, s2)
+    home = [own, own_far, mate, mate_far]
+    first = [r1, s1, r2, s2]
+    r5_ids = routes.moved(routes.either(own.ids, mate.ids), routes.rounds[4])
+    late_ids = [r5_ids, routes.moved(r5_ids, routes.swap)]
+    s3 = swapped(r3)
+    r4 = moved(r4_sent, routes.rounds[3])
+    s4 = swapped(r4)
+    second = [r3, s3]
+    third = [s4]
+    late = [Slab([], ids) for ids in late_ids * 2]
+    table = table_of(home + first + second + third + late)
+    at = 0
+    home_amps = amps(table, at, home, False)
+    at += len(home)
+    first_amps = amps(table, at, first, True)
+    at += len(first)
+
+    half = aux // 2
+    out_parts = [
+        density_call(terms(first, first_amps, far), [], jnp.float32, (begin, half))
+        for begin in range(0, aux, half)
+    ]
+    near_part = density_call(
+        terms(home, home_amps, near) + terms(first, first_amps, near), [], jnp.float32
+    )
+    second_amps = amps(table, at, second, True)
+    at += len(second)
+
+    r5 = moved(after(chosen(own, mate), r4), routes.rounds[4])
+    s5 = swapped(r5)
+    third_amps = amps(table, at, after_all(third, near_part, second_amps), True)
+    at += len(third)
+    outgoing = terms(second, second_amps, far) + terms(third, third_amps, far)
+    incoming = [
+        sibling(density_call(outgoing, [[part]], jnp.bfloat16, (index * half, half)))
+        for index, part in enumerate(out_parts)
+    ]
+    r6 = moved(after(chosen(own_far, mate_far), r5), routes.rounds[4])
+    s6 = swapped(r6)
+    near_part = density_call(
+        terms(second, second_amps, near) + terms(third, third_amps, near), [[near_part]], jnp.float32
+    )
+    fourth = [r5, s5]
+    fourth_amps = amps(table, at, fourth, False)
+    at += len(fourth)
+    near_part = density_call(terms(fourth, fourth_amps, near), [[near_part]], jnp.float32)
+
+    fifth = [r6, s6]
+    fifth_amps = amps(table, at, after_all(fifth, near_part), False)
+    density = density_call(
+        terms(fifth, fifth_amps, near), [[near_part], incoming], jnp.float32
+    )
+    return density[None]
+
+
+def after_all(slabs, *others):
+    pieces = [p for s in slabs for p in s.pieces]
+    pieces = lax.optimization_barrier((*pieces, *others))[: len(pieces)]
+    out = []
+    for slab in slabs:
+        count = len(slab.pieces)
+        out.append(Slab(pieces[:count], slab.ids, slab.far))
+        pieces = pieces[count:]
+    return out
+
+
 def solution(mesh):
+    wide, narrow = mesh.shape["wide"], mesh.shape["narrow"]
+    paired = narrow == 2 and wide % 4 == 0 and wide > 2 * ROUNDS + 1 and ROUNDS == 5
+
+    def per_device(three_index, *rest):
+        if paired and three_index.shape[0] == 1:
+            return paired_plan(three_index, *rest)
+        return ring_plan(three_index, *rest)
+
     placed = (P("wide", None, "narrow"), P(), P(), P(), P(None, "wide"))
     return jax.shard_map(
         per_device, mesh=mesh, in_specs=placed, out_specs=P("wide", None, "narrow"), check_vma=False

time: 714 us -> 373 us (0.52)
  waiting for transfers between devices: 497 us -> 92 us
  Pallas kernels: 0 us -> 158 us
  matrix products: 137 us -> 0 us
  starting transfers between devices: 21.5 us -> 52.3 us
  local copies, waits for them, and re-layouts: 9.23 us -> 30.4 us
  between operations: 21 us -> 3.67 us
  other arithmetic: 20.3 us -> 32.9 us
    ppermute x10 -> x5, waiting for transfers between devices: 491 us -> 2.55 us  [passed_along(): lax.ppermute(array, axis, [(i, (i + by) % length) for i in range(length)])]
    pallas_call x0 -> x14, Pallas kernels: none -> 158 us  [the longest x8 86.8 us: density_call(): pl.pallas_call(kernel, grid=(steps,), in_specs=[pl.BlockSpec(memory_space...]
    dot_general x16 -> x0, matrix products: 137 us -> none  [the longest x5 60.5 us: per_device(): jnp.einsum('ijab,jpb->ipa', amplitude, visiting, preferred_element_type=j...]
    ppermute x0 -> x32, waiting for transfers between devices: none -> 89.5 us  [the longest x28 73.1 us: moved(): sent = [lax.ppermute(p, 'wide', pairs) for p in slab.pieces]]
    ppermute x0 -> x32, starting transfers between devices: none -> 25.6 us  [the longest x28 22.6 us: moved(): sent = [lax.ppermute(p, 'wide', pairs) for p in slab.pieces]]
    select_n x0 -> x7, other arithmetic: none -> 25.6 us  [chosen(): jnp.where(lead, a, b)]
    add x4 -> x1, other arithmetic: 15.9 us -> 0.61 us  [table_of(): return jnp.stack([mine + theirs, weight], axis=1)]
    transpose x0 -> x2, local copies, waits for them, and re-layouts: none -> 11.7 us  [the longest x1 8.61 us: paired_plan(): turned = jnp.concatenate([whole, jnp.concatenate(own_far.pieces)], axis=1).T]
  transfers between devices with their start and end apart: 12 -> 37, of which waited for: 9 -> 7; matrix products, arithmetic and copies ran while one was open for 21% -> 13% of each run, Pallas kernels for 0% -> 40%
where the time goes in v3:
time: 373 us; the launch traced here: 370 us
  Pallas kernels  158 us (42%)
  waiting for transfers between devices  92 us (25%)
  starting transfers between devices  52.3 us (14%)
  other arithmetic  32.9 us (9%)
  local copies, waits for them, and re-layouts  30.4 us (8%)
    pallas_call x8, Pallas kernels, density_call(): pl.pallas_call(kernel, grid=(steps,), in_specs=[pl.BlockSpec(memory_space...  86.8 us
    ppermute x28, waiting for transfers between devices, moved(): sent = [lax.ppermute(p, 'wide', pairs) for p in slab.pieces]  73.1 us
    pallas_call x6, Pallas kernels, amplitude_call(): pl.pallas_call(kernel, grid=(count, blocks), in_specs=[pl.BlockSpec(memor...  71.6 us
    ppermute x5, starting transfers between devices, passed_along(): lax.ppermute(array, axis, [(i, (i + by) % length) for i in range(length)])  26.7 us
    select_n x7, other arithmetic, chosen(): jnp.where(lead, a, b)  25.6 us
    ppermute x28, starting transfers between devices, moved(): sent = [lax.ppermute(p, 'wide', pairs) for p in slab.pieces]  22.6 us
    ppermute x4, waiting for transfers between devices, sibling(): return lax.ppermute(array, 'narrow', [(0, 1), (1, 0)])  16.4 us
    transpose x1, local copies, waits for them, and re-layouts, paired_plan(): turned = jnp.concatenate([whole, jnp.concatenate(own_far.pieces)], axis=1).T  8.61 us
  transfers between devices with their start and end apart: 37, of which 7 were waited for; matrix products, arithmetic and copies ran while one was open for 13% of the time, Pallas kernels for 40%

profile of v3, /device:TPU:3, one launch (start us, length us, event | category | flops | bytes accessed | tf_op | source)
XLA Modules:
  0.0 369.7 jit_solution(6393454807384291246)
XLA Ops:
  0.0 3.9 %slice_bitcast_fusion = (bf16[1536,512]{1,0:T(8,128)(2,1)}, bf16[1536,512]{1,0:T(8,128)(2,1)}) fusion(bf16[1,3072,512]{2,1,0:T(8,128)(2,1)} %param.7), kind=kLoop, calls=%fused_computation.1 | loop fusion | bytes 6291456 | tf_op jit(solution)/shard_map/slice | solution.py:331
  3.9 1.3 collective-permute-start.13
  5.2 1.3 collective-permute-start.3
  7.6 17.7 %collective-permute-done.13.refs_1_.refs_9_ = bf16[1536,512]{1,0:T(8,128)(2,1)} collective-permute-done((bf16[1536,512]{1,0:T(8,128)(2,1)}, bf16[1536,512]{1,0:T(8,128)(2,1)}, u32[]{:S(2)}, u32[]{:S(2)}) %collective-permute-start.13) | collective-permute-done | bytes 1572896 | tf_op jit(solution)/shard_map/ppermute | solution.py:309
  25.4 16.9 %collective-permute-done.3.refs_0_.refs_8_ = bf16[1536,512]{1,0:T(8,128)(2,1)} collective-permute-done((bf16[1536,512]{1,0:T(8,128)(2,1)}, bf16[1536,512]{1,0:T(8,128)(2,1)}, u32[]{:S(2)}, u32[]{:S(2)}) %collective-permute-start.3) | collective-permute-done | bytes 1572896 | tf_op jit(solution)/shard_map/ppermute | solution.py:309
  42.2 5.4 %broadcast_select_fusion.2 = (bf16[1536,512]{1,0:T(8,128)(2,1)}, bf16[1536,512]{1,0:T(8,128)(2,1)}, bf16[1536,512]{1,0:T(8,128)(2,1)}, bf16[1536,512]{1,0:T(8,128)(2,1)}) fusion(bf16[1536,512]{1,0:T(8,128)(2,1)} %collective-permute-done.13.refs_1_.refs_9_, pred[]{:T(512)} %bitcast, bf16[1,3072,512]{2,1,0:T(8,128)(2,1)S(1)} %copy-done, ...), kind=kLoop, calls=%fused_computation.5 | loop fusion | flops 3145728 | bytes 15728641 | tf_op jit(solution)/shard_map/jit(_where)/select_n | solution.py:318
  47.6 1.2 collective-permute-start.14
  49.4 1.2 collective-permute-start
  52.1 2.2 collective-permute-start.22
  59.4 3.1 copy.58.refs_4_.refs_8_
  63.2 4.8 %collective-permute-done.14.refs_5_.refs_13_ = bf16[1536,512]{1,0:T(8,128)(2,1)} collective-permute-done((bf16[1536,512]{1,0:T(8,128)(2,1)}, bf16[1536,512]{1,0:T(8,128)(2,1)}, u32[]{:S(2)}, u32[]{:S(2)}) %collective-permute-start.14) | collective-permute-done | bytes 1572896 | tf_op jit(solution)/shard_map/ppermute | solution.py:309
  68.1 3.4 broadcast_select_fusion.1
  71.5 3.5 collective-permute-start.15
  74.9 19.0 %collective-permute-done.4.refs_4_.refs_12_ = bf16[1536,512]{1,0:T(8,128)(2,1)} collective-permute-done((bf16[1536,512]{1,0:T(8,128)(2,1)}, bf16[1536,512]{1,0:T(8,128)(2,1)}, u32[]{:S(2)}, u32[]{:S(2)}) %collective-permute-start.4) | collective-permute-done | bytes 1572896 | tf_op jit(solution)/shard_map/ppermute | solution.py:309
  94.0 2.0 collective-permute-start.16
  95.9 3.3 broadcast_select_fusion.6
  100.0 2.5 collective-permute-done.23
  102.5 9.0 %collective-permute-start.24 = (f32[1]{0:T(128)}, f32[1]{0:T(128)}, u32[]{:S(2)}, u32[]{:S(2)}) collective-permute-start(f32[1]{0:T(128)} %bitcast.9), channel_id=1, source_target_pairs={{0,26},{2,28},{4,30},{6,0},{8,2},{10,4},{12,6},{14,8},{16,10},{18,... | collective-permute-start | bytes 20 | tf_op jit(solution)/shard_map/ppermute | solution.py:16
  111.5 7.1 %collective-permute-start.25 = (f32[1]{0:T(128)}, f32[1]{0:T(128)}, u32[]{:S(2)}, u32[]{:S(2)}) collective-permute-start(f32[1]{0:T(128)} %bitcast.10), channel_id=1, source_target_pairs={{0,24},{2,26},{4,28},{6,30},{8,0},{10,2},{12,4},{14,6},{16,8},{18,... | collective-permute-start | bytes 20 | tf_op jit(solution)/shard_map/ppermute | solution.py:16
  118.6 7.7 %collective-permute-start.26 = (f32[1]{0:T(128)}, f32[1]{0:T(128)}, u32[]{:S(2)}, u32[]{:S(2)}) collective-permute-start(f32[1]{0:T(128)} %bitcast.11), channel_id=1, source_target_pairs={{0,22},{2,24},{4,26},{6,28},{8,30},{10,0},{12,2},{14,4},{16,6},{18... | collective-permute-start | bytes 20 | tf_op jit(solution)/shard_map/ppermute | solution.py:16
  128.9 3.1 concatenate.12
  133.5 3.4 broadcast_select_fusion
  136.9 14.6 %collective-permute-done.5.refs_0_ = bf16[1536,512]{1,0:T(8,128)(2,1)} collective-permute-done((bf16[1536,512]{1,0:T(8,128)(2,1)}, bf16[1536,512]{1,0:T(8,128)(2,1)}, u32[]{:S(2)}, u32[]{:S(2)}) %collective-permute-start.5) | collective-permute-done | bytes 1572896 | tf_op jit(solution)/shard_map/ppermute | solution.py:309
  151.5 3.3 broadcast_select_fusion.5
  154.8 5.5 %maximum_bitcast_fusion = bf16[1024,3072]{0,1:T(8,128)(2,1)} fusion(bf16[1536,512]{1,0:T(8,128)(2,1)} %collective-permute-done.10.refs_3_, bf16[1536,512]{1,0:T(8,128)(2,1)} %collective-permute-done.refs_2_, bf16[3072,512]{1,0:T(8,128)(2,1)S(1)} %bitcast.43), kind=kLoop, calls=%fused_computation | loop fusion | flops 18874368 | bytes 12582912 | tf_op jit(solution)/shard_map/transpose | solution.py:361
  160.2 8.6 %copy.62.refs_4_.refs_8_.refs_2_ = bf16[1024,3072]{1,0:T(8,128)(2,1)} copy(bf16[1024,3072]{0,1:T(8,128)(2,1)} %maximum_bitcast_fusion) | data formatting | bytes 12582912 | tf_op jit(solution)/shard_map/transpose | solution.py:361
  168.9 5.5 %collective-permute-start.33 = (bf16[1536,512]{1,0:T(8,128)(2,1)}, bf16[1536,512]{1,0:T(8,128)(2,1)S(1)}, u32[]{:S(2)}, u32[]{:S(2)}) collective-permute-start(bf16[1536,512]{1,0:T(8,128)(2,1)} %collective-permute-done.3.refs_0_.refs_8_), channel_id=1, source_target_pairs={{0,2},{2,0},{4,6},{6,4},{8,10},{10,8},{12,14},{14,12},{16,18},{18,... | collective-permute-start | bytes 4718600 | tf_op jit(solution)/shard_map/ppermute | solution.py:309
  174.5 3.3 broadcast_select_fusion.4
  177.8 3.5 broadcast_select_fusion.9
  181.8 2.0 collective-permute-start.8
  183.7 12.3 %shard_map.75.refs_16_.refs_17_.refs_18_.refs_19_ = bf16[4,512,512]{2,1,0:T(8,128)(2,1)} custom-call(f32[15,2]{1,0:T(8,128)} %copy.75.scalars, bf16[1536,512]{1,0:T(8,128)(2,1)} %get-tuple-element.30.refs_0_, bf16[1536,512]{1,0:T(8,128)(2,1)} %get-tuple-element.29.refs_1_, bf16[1536,512]{1,0:T(8,128)(2,1)} %collective-permute-done.refs_2_, ...), custom_call_target="tpu_custom_call" | custom-call | flops 6442450944 | bytes 27262976 | tf_op jit(solution)/shard_map/pallas_call | solution.py:179
  197.7 20.7 %shard_map.76.refs_20_.refs_21_.refs_22_.refs_23_.refs_8_.refs_9_.refs_10_.refs_11_ = bf16[4,1024,512]{2,1,0:T(8,128)(2,1)} custom-call(f32[15,2]{1,0:T(8,128)} %copy.75.scalars, bf16[1536,512]{1,0:T(8,128)(2,1)} %collective-permute-done.3.refs_0_.refs_8_, bf16[1536,512]{1,0:T(8,128)(2,1)} %collective-permute-done.13.refs_1_.refs_9_, ...), custom_call_target="tpu_custom_call" | custom-call | flops 12884901888 | bytes 41943040 | tf_op jit(solution)/shard_map/pallas_call | solution.py:179
  220.9 19.1 %shard_map.77.refs_9_ = f32[3072,512]{1,0:T(8,128)} custom-call(bf16[1536,512]{1,0:T(8,128)(2,1)} %get-tuple-element.30.refs_0_, bf16[1536,512]{1,0:T(8,128)(2,1)} %get-tuple-element.29.refs_1_, bf16[1536,512]{1,0:T(8,128)(2,1)} %collective-permute-done.refs_2_, bf16[1536,512]{1,0:T(8,128)(2,1)} %collective-permute-done.10.refs_3_, ...), custom_call_target="tpu_custom_call" | custom-call | flops 12884901888 | bytes 35651584 | tf_op jit(solution)/shard_map/pallas_call | solution.py:277
  240.0 7.7 %shard_map.84.refs_9_ = f32[1536,512]{1,0:T(8,128)} custom-call(bf16[1536,512]{1,0:T(8,128)(2,1)} %collective-permute-done.3.refs_0_.refs_8_, bf16[1536,512]{1,0:T(8,128)(2,1)} %collective-permute-done.13.refs_1_.refs_9_, bf16[1536,512]{1,0:T(8,128)(2,1)} %copy-done.1, bf16[1536,512]{1,0:T(8,128)(2,1)} %copy-done.2, ...), custom_call_target="tpu_custom_call" | custom-call | flops 3221225472 | bytes 11534336 | tf_op jit(solution)/shard_map/pallas_call | solution.py:277
  247.9 8.2 %shard_map.82.refs_9_ = f32[1536,512]{1,0:T(8,128)} custom-call(bf16[1536,512]{1,0:T(8,128)(2,1)} %collective-permute-done.3.refs_0_.refs_8_, bf16[1536,512]{1,0:T(8,128)(2,1)} %collective-permute-done.13.refs_1_.refs_9_, bf16[1536,512]{1,0:T(8,128)(2,1)} %copy-done.1, bf16[1536,512]{1,0:T(8,128)(2,1)} %copy-done.2, ...), custom_call_target="tpu_custom_call" | custom-call | flops 3221225472 | bytes 11534336 | tf_op jit(solution)/shard_map/pallas_call | solution.py:277
  256.2 13.1 %shard_map.74.refs_6_.refs_7_ = bf16[2,1024,512]{2,1,0:T(8,128)(2,1)} custom-call(f32[15,2]{1,0:T(8,128)} %copy.75.scalars, bf16[1536,512]{1,0:T(8,128)(2,1)} %collective-permute-done.5.refs_0_, bf16[1536,512]{1,0:T(8,128)(2,1)} %collective-permute-done.15.refs_1_, bf16[1536,512]{1,0:T(8,128)(2,1)} %copy-done.4, bf16[1536,512]{1,0:T(8,128)(2,1)} %copy-done.3, ...), custom_call_target="tpu_custom_call" | custom-call | flops 6442450944 | bytes 20971520 | tf_op jit(solution)/shard_map/pallas_call | solution.py:179
  270.5 8.6 %shard_map.78.refs_8_ = bf16[1,1024,512]{2,1,0:T(8,128)(2,1)} custom-call(f32[15,2]{1,0:T(8,128)} %copy.75.scalars, bf16[1536,512]{1,0:T(8,128)(2,1)} %copy-done.6, bf16[1536,512]{1,0:T(8,128)(2,1)} %copy-done.5, bf16[1024,3072]{1,0:T(8,128)(2,1)} %copy.62.refs_4_.refs_8_.refs_2_, f32[1024,1]{1,0:T(8,128)} %copy.63.refs_5_.refs_9_.refs_3_, f32[1,1,512]{2,1,0:T(1,128)} %bitcast.47), custom_call_target="tpu_custom_call" | custom-call | flops 3221225472 | bytes 10485760 | tf_op jit(solution)/shard_map/pallas_call | solution.py:179
  279.7 7.9 %shard_map.85 = bf16[1536,512]{1,0:T(8,128)(2,1)} custom-call(bf16[1536,512]{1,0:T(8,128)(2,1)} %collective-permute-done.5.refs_0_, bf16[1536,512]{1,0:T(8,128)(2,1)} %collective-permute-done.15.refs_1_, bf16[1536,512]{1,0:T(8,128)(2,1)} %copy-done.4, bf16[1536,512]{1,0:T(8,128)(2,1)} %copy-done.3, bf16[1536,512]{1,0:T(8,128)(2,1)} %copy-done.6, ...), custom_call_target="tpu_custom_call" | custom-call | flops 2415919104 | bytes 11010048 | tf_op jit(solution)/shard_map/pallas_call | solution.py:277
  287.7 1.3 collective-permute-start.36
  289.0 7.9 %shard_map.83 = bf16[1536,512]{1,0:T(8,128)(2,1)} custom-call(bf16[1536,512]{1,0:T(8,128)(2,1)} %collective-permute-done.5.refs_0_, bf16[1536,512]{1,0:T(8,128)(2,1)} %collective-permute-done.15.refs_1_, bf16[1536,512]{1,0:T(8,128)(2,1)} %copy-done.4, bf16[1536,512]{1,0:T(8,128)(2,1)} %copy-done.3, bf16[1536,512]{1,0:T(8,128)(2,1)} %copy-done.6, ...), custom_call_target="tpu_custom_call" | custom-call | flops 2415919104 | bytes 11010048 | tf_op jit(solution)/shard_map/pallas_call | solution.py:277
  298.1 12.8 %shard_map.79.refs_6_ = f32[3072,512]{1,0:T(8,128)} custom-call(bf16[1536,512]{1,0:T(8,128)(2,1)} %collective-permute-done.5.refs_0_, bf16[1536,512]{1,0:T(8,128)(2,1)} %collective-permute-done.15.refs_1_, bf16[1536,512]{1,0:T(8,128)(2,1)} %copy-done.4, bf16[1536,512]{1,0:T(8,128)(2,1)} %copy-done.3, bf16[1536,512]{1,0:T(8,128)(2,1)} %copy-done.6, ...), custom_call_target="tpu_custom_call" | custom-call | flops 4831838208 | bytes 23592960 | tf_op jit(solution)/shard_map/pallas_call | solution.py:277
  310.9 8.4 %shard_map.73.refs_4_.refs_5_ = bf16[2,512,512]{2,1,0:T(8,128)(2,1)} custom-call(f32[15,2]{1,0:T(8,128)} %copy.75.scalars, bf16[1536,512]{1,0:T(8,128)(2,1)} %collective-permute-done.8.refs_0_, bf16[1536,512]{1,0:T(8,128)(2,1)} %collective-permute-done.18.refs_1_, bf16[1536,512]{1,0:T(8,128)(2,1)} %collective-permute-done.27.refs_2_, ...), custom_call_target="tpu_custom_call" | custom-call | flops 3221225472 | bytes 13631488 | tf_op jit(solution)/shard_map/pallas_call | solution.py:179
  319.3 11.2 %shard_map.80.refs_6_ = f32[3072,512]{1,0:T(8,128)} custom-call(bf16[1536,512]{1,0:T(8,128)(2,1)} %collective-permute-done.8.refs_0_, bf16[1536,512]{1,0:T(8,128)(2,1)} %collective-permute-done.18.refs_1_, bf16[1536,512]{1,0:T(8,128)(2,1)} %collective-permute-done.27.refs_2_, bf16[1536,512]{1,0:T(8,128)(2,1)} %copy-done.9, ...), custom_call_target="tpu_custom_call" | custom-call | flops 3221225472 | bytes 19922944 | tf_op jit(solution)/shard_map/pallas_call | solution.py:277
  330.6 1.1 copy-done.10
  331.7 1.1 copy-done.11
  332.9 8.4 %shard_map.81.refs_4_.refs_5_ = bf16[2,512,512]{2,1,0:T(8,128)(2,1)} custom-call(f32[15,2]{1,0:T(8,128)} %copy.75.scalars, bf16[1536,512]{1,0:T(8,128)(2,1)} %collective-permute-done.9.refs_0_, bf16[1536,512]{1,0:T(8,128)(2,1)} %copy-done.8, bf16[1536,512]{1,0:T(8,128)(2,1)} %copy-done.11, bf16[1536,512]{1,0:T(8,128)(2,1)} %copy-done.10, ...), custom_call_target="tpu_custom_call" | custom-call | flops 3221225472 | bytes 13631488 | tf_op jit(solution)/shard_map/pallas_call | solution.py:179
  341.3 16.4 %collective-permute-done.35.refs_7_ = bf16[1536,512]{1,0:T(8,128)(2,1)} collective-permute-done((bf16[1536,512]{1,0:T(8,128)(2,1)}, bf16[1536,512]{1,0:T(8,128)(2,1)}, u32[]{:S(2)}, u32[]{:S(2)}) %collective-permute-start.35) | collective-permute-done | bytes 1572896 | tf_op jit(solution)/shard_map/ppermute | solution.py:324
  357.7 11.9 %shard_map.86 = f32[3072,512]{1,0:T(8,128)} custom-call(bf16[1536,512]{1,0:T(8,128)(2,1)} %collective-permute-done.9.refs_0_, bf16[1536,512]{1,0:T(8,128)(2,1)} %copy-done.8, bf16[1536,512]{1,0:T(8,128)(2,1)} %copy-done.11, bf16[1536,512]{1,0:T(8,128)(2,1)} %copy-done.10, bf16[2,512,512]{2,1,0:T(8,128)(2,1)} %shard_map.81.refs_4_.refs_5_, ...), custom_call_target="tpu_custom_call" | custom-call | flops 3221225472 | bytes 26214400 | tf_op jit(solution)/shard_map/pallas_call | solution.py:277
  (112 shorter events, 18.3 us)
Async XLA Ops:
  0.0 7.0 %copy-start.18 = (pred[16]{0:T(512)(128)(4,1)S(1)}, pred[16]{0:T(512)(128)(4,1)}, u32[]{:S(2)}) copy-start(pred[16]{0:T(512)(128)(4,1)} %constant.24.clone) | copy-start | bytes 52
  0.0 42.2 %copy-start = (bf16[1,3072,512]{2,1,0:T(8,128)(2,1)S(1)}, bf16[1,3072,512]{2,1,0:T(8,128)(2,1)}, u32[]{:S(2)}) copy-start(bf16[1,3072,512]{2,1,0:T(8,128)(2,1)} %param.7) | copy-start | bytes 9437188
  3.9 21.4 %collective-permute-start.13 = (bf16[1536,512]{1,0:T(8,128)(2,1)}, bf16[1536,512]{1,0:T(8,128)(2,1)}, u32[]{:S(2)}, u32[]{:S(2)}) collective-permute-start(bf16[1536,512]{1,0:T(8,128)(2,1)} %get-tuple-element.29.refs_1_), channel_id=1, source_target_pairs={{0,24},{2,4},{4,2},{6,14},{8,0},{10,12},{12,10},{14,22},{16,8},{18... | collective-permute-start | bytes 4718600 | tf_op jit(solution)/shard_map/ppermute | solution.py:309
  5.2 37.0 %collective-permute-start.3 = (bf16[1536,512]{1,0:T(8,128)(2,1)}, bf16[1536,512]{1,0:T(8,128)(2,1)}, u32[]{:S(2)}, u32[]{:S(2)}) collective-permute-start(bf16[1536,512]{1,0:T(8,128)(2,1)} %get-tuple-element.30.refs_0_), channel_id=1, source_target_pairs={{0,24},{2,4},{4,2},{6,14},{8,0},{10,12},{12,10},{14,22},{16,8},{18... | collective-permute-start | bytes 4718600 | tf_op jit(solution)/shard_map/ppermute | solution.py:309
  6.5 35.7 %collective-permute-start.12 = (bf16[1536,512]{1,0:T(8,128)(2,1)}, bf16[1536,512]{1,0:T(8,128)(2,1)}, u32[]{:S(2)}, u32[]{:S(2)}) collective-permute-start(bf16[1536,512]{1,0:T(8,128)(2,1)} %get-tuple-element.29.refs_1_), channel_id=1, source_target_pairs={{0,2},{2,0},{4,6},{6,4},{8,10},{10,8},{12,14},{14,12},{16,18},{18,... | collective-permute-start | bytes 4718600 | tf_op jit(solution)/shard_map/ppermute | solution.py:309
  6.5 35.7 %collective-permute-start.2 = (bf16[1536,512]{1,0:T(8,128)(2,1)}, bf16[1536,512]{1,0:T(8,128)(2,1)}, u32[]{:S(2)}, u32[]{:S(2)}) collective-permute-start(bf16[1536,512]{1,0:T(8,128)(2,1)} %get-tuple-element.30.refs_0_), channel_id=1, source_target_pairs={{0,2},{2,0},{4,6},{6,4},{8,10},{10,8},{12,14},{14,12},{16,18},{18,... | collective-permute-start | bytes 4718600 | tf_op jit(solution)/shard_map/ppermute | solution.py:309
  42.2 8.6 %copy-start.14 = (s32[6,1]{0,1:T(1,128)S(1)}, s32[6,1]{0,1:T(1,128)}, u32[]{:S(2)}) copy-start(s32[6,1]{0,1:T(1,128)} %param.11) | copy-start | bytes 76
  42.2 12.1 %copy-start.15 = (f32[1024]{0:T(1024)S(1)}, f32[1024]{0:T(1024)}, u32[]{:S(2)}) copy-start(f32[1024]{0:T(1024)} %param.10) | copy-start | bytes 12292
  47.6 20.5 %collective-permute-start.14 = (bf16[1536,512]{1,0:T(8,128)(2,1)}, bf16[1536,512]{1,0:T(8,128)(2,1)}, u32[]{:S(2)}, u32[]{:S(2)}) collective-permute-start(bf16[1536,512]{1,0:T(8,128)(2,1)} %get-tuple-element.25), channel_id=1, source_target_pairs={{0,6},{2,26},{4,12},{6,0},{8,14},{10,2},{12,20},{14,8},{16,22},{18... | collective-permute-start | bytes 4718600 | tf_op jit(solution)/shard_map/ppermute | solution.py:309
  48.8 45.1 %collective-permute-start.4 = (bf16[1536,512]{1,0:T(8,128)(2,1)}, bf16[1536,512]{1,0:T(8,128)(2,1)}, u32[]{:S(2)}, u32[]{:S(2)}) collective-permute-start(bf16[1536,512]{1,0:T(8,128)(2,1)} %get-tuple-element.27), channel_id=1, source_target_pairs={{0,6},{2,26},{4,12},{6,0},{8,14},{10,2},{12,20},{14,8},{16,22},{18... | collective-permute-start | bytes 4718600 | tf_op jit(solution)/shard_map/ppermute | solution.py:309
  49.4 77.4 %collective-permute-start = (bf16[1536,512]{1,0:T(8,128)(2,1)}, bf16[1536,512]{1,0:T(8,128)(2,1)}, u32[]{:S(2)}, u32[]{:S(2)}) collective-permute-start(bf16[1536,512]{1,0:T(8,128)(2,1)} %get-tuple-element.30.refs_0_), channel_id=1, source_target_pairs={{0,1},{1,0},{2,3},{3,2},{4,5},{5,4},{6,7},{7,6},{8,9},{9,8},{10,11... | collective-permute-start | bytes 4718600 | tf_op jit(solution)/shard_map/ppermute | solution.py:324
  50.6 82.3 %collective-permute-start.10 = (bf16[1536,512]{1,0:T(8,128)(2,1)}, bf16[1536,512]{1,0:T(8,128)(2,1)}, u32[]{:S(2)}, u32[]{:S(2)}) collective-permute-start(bf16[1536,512]{1,0:T(8,128)(2,1)} %get-tuple-element.29.refs_1_), channel_id=1, source_target_pairs={{0,1},{1,0},{2,3},{3,2},{4,5},{5,4},{6,7},{7,6},{8,9},{9,8},{10,11... | collective-permute-start | bytes 4718600 | tf_op jit(solution)/shard_map/ppermute | solution.py:324
  52.1 47.2 %collective-permute-start.22 = (f32[1]{0:T(128)}, f32[1]{0:T(128)}, u32[]{:S(2)}, u32[]{:S(2)}) collective-permute-start(f32[1]{0:T(128)} %bitcast.7), channel_id=1, source_target_pairs={{0,30},{2,0},{4,2},{6,4},{8,6},{10,8},{12,10},{14,12},{16,14},{18,... | collective-permute-start | bytes 20 | tf_op jit(solution)/shard_map/ppermute | solution.py:16
  54.4 141.8 %copy-start.13 = (f32[512]{0:T(512)}, f32[512]{0:T(512)S(1)}, u32[]{:S(2)}) copy-start(f32[512]{0:T(512)S(1)} %get-tuple-element.34) | copy-start | bytes 6148
  71.5 62.0 %collective-permute-start.15 = (bf16[1536,512]{1,0:T(8,128)(2,1)}, bf16[1536,512]{1,0:T(8,128)(2,1)}, u32[]{:S(2)}, u32[]{:S(2)}) collective-permute-start(bf16[1536,512]{1,0:T(8,128)(2,1)} %broadcast_select_fusion.1), channel_id=1, source_target_pairs={{0,8},{2,4},{4,2},{6,30},{8,16},{10,12},{12,10},{14,6},{16,24},{18... | collective-permute-start | bytes 4718600 | tf_op jit(solution)/shard_map/ppermute | solution.py:309
  94.0 39.5 %collective-permute-start.16 = (bf16[1536,512]{1,0:T(8,128)(2,1)}, bf16[1536,512]{1,0:T(8,128)(2,1)}, u32[]{:S(2)}, u32[]{:S(2)}) collective-permute-start(bf16[1536,512]{1,0:T(8,128)(2,1)} %collective-permute-done.14.refs_5_.refs_13_), channel_id=1, source_target_pairs={{0,2},{2,0},{4,6},{6,4},{8,10},{10,8},{12,14},{14,12},{16,18},{18,... | collective-permute-start | bytes 4718600 | tf_op jit(solution)/shard_map/ppermute | solution.py:309
  99.2 3.3 collective-permute-start.23
  102.5 9.0 %collective-permute-start.24 = (f32[1]{0:T(128)}, f32[1]{0:T(128)}, u32[]{:S(2)}, u32[]{:S(2)}) collective-permute-start(f32[1]{0:T(128)} %bitcast.9), channel_id=1, source_target_pairs={{0,26},{2,28},{4,30},{6,0},{8,2},{10,4},{12,6},{14,8},{16,10},{18,... | collective-permute-start | bytes 20 | tf_op jit(solution)/shard_map/ppermute | solution.py:16
  111.5 7.1 %collective-permute-start.25 = (f32[1]{0:T(128)}, f32[1]{0:T(128)}, u32[]{:S(2)}, u32[]{:S(2)}) collective-permute-start(f32[1]{0:T(128)} %bitcast.10), channel_id=1, source_target_pairs={{0,24},{2,26},{4,28},{6,30},{8,0},{10,2},{12,4},{14,6},{16,8},{18,... | collective-permute-start | bytes 20 | tf_op jit(solution)/shard_map/ppermute | solution.py:16
  118.6 7.7 %collective-permute-start.26 = (f32[1]{0:T(128)}, f32[1]{0:T(128)}, u32[]{:S(2)}, u32[]{:S(2)}) collective-permute-start(f32[1]{0:T(128)} %bitcast.11), channel_id=1, source_target_pairs={{0,22},{2,24},{4,26},{6,28},{8,30},{10,0},{12,2},{14,4},{16,6},{18... | collective-permute-start | bytes 20 | tf_op jit(solution)/shard_map/ppermute | solution.py:16
  126.3 25.2 %collective-permute-start.5 = (bf16[1536,512]{1,0:T(8,128)(2,1)}, bf16[1536,512]{1,0:T(8,128)(2,1)}, u32[]{:S(2)}, u32[]{:S(2)}) collective-permute-start(bf16[1536,512]{1,0:T(8,128)(2,1)} %broadcast_select_fusion.6), channel_id=1, source_target_pairs={{0,8},{2,4},{4,2},{6,30},{8,16},{10,12},{12,10},{14,6},{16,24},{18... | collective-permute-start | bytes 4718600 | tf_op jit(solution)/shard_map/ppermute | solution.py:309
  126.7 10.1 %collective-permute-start.6 = (bf16[1536,512]{1,0:T(8,128)(2,1)}, bf16[1536,512]{1,0:T(8,128)(2,1)}, u32[]{:S(2)}, u32[]{:S(2)}) collective-permute-start(bf16[1536,512]{1,0:T(8,128)(2,1)} %collective-permute-done.4.refs_4_.refs_12_), channel_id=1, source_target_pairs={{0,2},{2,0},{4,6},{6,4},{8,10},{10,8},{12,14},{14,12},{16,18},{18,... | collective-permute-start | bytes 4718600 | tf_op jit(solution)/shard_map/ppermute | solution.py:309
  132.9 44.9 %collective-permute-start.1 = (bf16[1536,512]{1,0:T(8,128)(2,1)}, bf16[1536,512]{1,0:T(8,128)(2,1)}, u32[]{:S(2)}, u32[]{:S(2)}) collective-permute-start(bf16[1536,512]{1,0:T(8,128)(2,1)} %collective-permute-done.refs_2_), channel_id=1, source_target_pairs={{0,2},{2,0},{4,6},{6,4},{8,10},{10,8},{12,14},{14,12},{16,18},{18,... | collective-permute-start | bytes 4718600 | tf_op jit(solution)/shard_map/ppermute | solution.py:309
  133.4 41.0 %collective-permute-start.11 = (bf16[1536,512]{1,0:T(8,128)(2,1)}, bf16[1536,512]{1,0:T(8,128)(2,1)}, u32[]{:S(2)}, u32[]{:S(2)}) collective-permute-start(bf16[1536,512]{1,0:T(8,128)(2,1)} %collective-permute-done.10.refs_3_), channel_id=1, source_target_pairs={{0,2},{2,0},{4,6},{6,4},{8,10},{10,8},{12,14},{14,12},{16,18},{18,... | collective-permute-start | bytes 4718600 | tf_op jit(solution)/shard_map/ppermute | solution.py:309
  136.9 44.9 %collective-permute-start.17 = (bf16[1536,512]{1,0:T(8,128)(2,1)}, bf16[1536,512]{1,0:T(8,128)(2,1)}, u32[]{:S(2)}, u32[]{:S(2)}) collective-permute-start(bf16[1536,512]{1,0:T(8,128)(2,1)} %broadcast_select_fusion), channel_id=1, source_target_pairs={{0,6},{2,10},{4,28},{6,0},{8,14},{10,18},{12,4},{14,8},{16,22},{18... | collective-permute-start | bytes 4718600 | tf_op jit(solution)/shard_map/ppermute | solution.py:309
  154.8 27.0 %collective-permute-start.7 = (bf16[1536,512]{1,0:T(8,128)(2,1)}, bf16[1536,512]{1,0:T(8,128)(2,1)}, u32[]{:S(2)}, u32[]{:S(2)}) collective-permute-start(bf16[1536,512]{1,0:T(8,128)(2,1)} %broadcast_select_fusion.5), channel_id=1, source_target_pairs={{0,6},{2,10},{4,28},{6,0},{8,14},{10,18},{12,4},{14,8},{16,22},{18... | collective-permute-start | bytes 4718600 | tf_op jit(solution)/shard_map/ppermute | solution.py:309
  168.9 27.2 %collective-permute-start.33 = (bf16[1536,512]{1,0:T(8,128)(2,1)}, bf16[1536,512]{1,0:T(8,128)(2,1)S(1)}, u32[]{:S(2)}, u32[]{:S(2)}) collective-permute-start(bf16[1536,512]{1,0:T(8,128)(2,1)} %collective-permute-done.3.refs_0_.refs_8_), channel_id=1, source_target_pairs={{0,2},{2,0},{4,6},{6,4},{8,10},{10,8},{12,14},{14,12},{16,18},{18,... | collective-permute-start | bytes 4718600 | tf_op jit(solution)/shard_map/ppermute | solution.py:309
  174.4 21.7 %collective-permute-start.34 = (bf16[1536,512]{1,0:T(8,128)(2,1)}, bf16[1536,512]{1,0:T(8,128)(2,1)S(1)}, u32[]{:S(2)}, u32[]{:S(2)}) collective-permute-start(bf16[1536,512]{1,0:T(8,128)(2,1)} %collective-permute-done.13.refs_1_.refs_9_), channel_id=1, source_target_pairs={{0,2},{2,0},{4,6},{6,4},{8,10},{10,8},{12,14},{14,12},{16,18},{18,... | collective-permute-start | bytes 4718600 | tf_op jit(solution)/shard_map/ppermute | solution.py:309
  181.3 38.7 %collective-permute-start.30 = (bf16[1536,512]{1,0:T(8,128)(2,1)}, bf16[1536,512]{1,0:T(8,128)(2,1)S(1)}, u32[]{:S(2)}, u32[]{:S(2)}) collective-permute-start(bf16[1536,512]{1,0:T(8,128)(2,1)} %collective-permute-done.15.refs_1_), channel_id=1, source_target_pairs={{0,2},{2,0},{4,6},{6,4},{8,10},{10,8},{12,14},{14,12},{16,18},{18,... | collective-permute-start | bytes 4718600 | tf_op jit(solution)/shard_map/ppermute | solution.py:309
  181.7 36.9 %collective-permute-start.18 = (bf16[1536,512]{1,0:T(8,128)(2,1)}, bf16[1536,512]{1,0:T(8,128)(2,1)}, u32[]{:S(2)}, u32[]{:S(2)}) collective-permute-start(bf16[1536,512]{1,0:T(8,128)(2,1)} %get-tuple-element.17), channel_id=1, source_target_pairs={{0,8},{2,4},{4,2},{6,30},{8,16},{10,12},{12,10},{14,6},{16,24},{18... | collective-permute-start | bytes 4718600 | tf_op jit(solution)/shard_map/ppermute | solution.py:309
  181.8 37.2 %collective-permute-start.8 = (bf16[1536,512]{1,0:T(8,128)(2,1)S(1)}, bf16[1536,512]{1,0:T(8,128)(2,1)}, u32[]{:S(2)}, u32[]{:S(2)}) collective-permute-start(bf16[1536,512]{1,0:T(8,128)(2,1)S(1)} %copy-done.7), channel_id=1, source_target_pairs={{0,8},{2,4},{4,2},{6,30},{8,16},{10,12},{12,10},{14,6},{16,24},{18... | collective-permute-start | bytes 4718600 | tf_op jit(solution)/shard_map/ppermute | solution.py:309
  196.1 51.7 %collective-permute-start.29 = (bf16[1536,512]{1,0:T(8,128)(2,1)}, bf16[1536,512]{1,0:T(8,128)(2,1)S(1)}, u32[]{:S(2)}, u32[]{:S(2)}) collective-permute-start(bf16[1536,512]{1,0:T(8,128)(2,1)} %collective-permute-done.5.refs_0_), channel_id=1, source_target_pairs={{0,2},{2,0},{4,6},{6,4},{8,10},{10,8},{12,14},{14,12},{16,18},{18,... | collective-permute-start | bytes 4718600 | tf_op jit(solution)/shard_map/ppermute | solution.py:309
  218.4 37.7 %collective-permute-start.32 = (bf16[1536,512]{1,0:T(8,128)(2,1)}, bf16[1536,512]{1,0:T(8,128)(2,1)S(1)}, u32[]{:S(2)}, u32[]{:S(2)}) collective-permute-start(bf16[1536,512]{1,0:T(8,128)(2,1)} %collective-permute-done.17), channel_id=1, source_target_pairs={{0,2},{2,0},{4,6},{6,4},{8,10},{10,8},{12,14},{14,12},{16,18},{18,... | collective-permute-start | bytes 4718600 | tf_op jit(solution)/shard_map/ppermute | solution.py:309
  218.6 50.7 %collective-permute-start.31 = (bf16[1536,512]{1,0:T(8,128)(2,1)}, bf16[1536,512]{1,0:T(8,128)(2,1)S(1)}, u32[]{:S(2)}, u32[]{:S(2)}) collective-permute-start(bf16[1536,512]{1,0:T(8,128)(2,1)} %collective-permute-done.7), channel_id=1, source_target_pairs={{0,2},{2,0},{4,6},{6,4},{8,10},{10,8},{12,14},{14,12},{16,18},{18,... | collective-permute-start | bytes 4718600 | tf_op jit(solution)/shard_map/ppermute | solution.py:309
  219.0 60.1 %collective-permute-start.19 = (bf16[1536,512]{1,0:T(8,128)(2,1)}, bf16[1536,512]{1,0:T(8,128)(2,1)S(1)}, u32[]{:S(2)}, u32[]{:S(2)}) collective-permute-start(bf16[1536,512]{1,0:T(8,128)(2,1)} %broadcast_select_fusion.4), channel_id=1, source_target_pairs={{0,8},{2,4},{4,2},{6,30},{8,16},{10,12},{12,10},{14,6},{16,24},{18... | collective-permute-start | bytes 4718600 | tf_op jit(solution)/shard_map/ppermute | solution.py:309
  220.0 20.0 %copy-start.3 = (bf16[1536,512]{1,0:T(8,128)(2,1)}, bf16[1536,512]{1,0:T(8,128)(2,1)S(1)}, u32[]{:S(2)}) copy-start(bf16[1536,512]{1,0:T(8,128)(2,1)S(1)} %collective-permute-done.30.refs_3_) | copy-start | bytes 4718596
  220.0 59.2 %collective-permute-start.9 = (bf16[1536,512]{1,0:T(8,128)(2,1)}, bf16[1536,512]{1,0:T(8,128)(2,1)}, u32[]{:S(2)}, u32[]{:S(2)}) collective-permute-start(bf16[1536,512]{1,0:T(8,128)(2,1)} %broadcast_select_fusion.9), channel_id=1, source_target_pairs={{0,8},{2,4},{4,2},{6,30},{8,16},{10,12},{12,10},{14,6},{16,24},{18... | collective-permute-start | bytes 4718600 | tf_op jit(solution)/shard_map/ppermute | solution.py:309
  247.8 8.3 %copy-start.4 = (bf16[1536,512]{1,0:T(8,128)(2,1)}, bf16[1536,512]{1,0:T(8,128)(2,1)S(1)}, u32[]{:S(2)}) copy-start(bf16[1536,512]{1,0:T(8,128)(2,1)S(1)} %collective-permute-done.29.refs_2_) | copy-start | bytes 4718596
  247.8 49.1 %collective-permute-start.28 = (bf16[1536,512]{1,0:T(8,128)(2,1)}, bf16[1536,512]{1,0:T(8,128)(2,1)S(1)}, u32[]{:S(2)}, u32[]{:S(2)}) collective-permute-start(bf16[1536,512]{1,0:T(8,128)(2,1)} %collective-permute-done.18.refs_1_), channel_id=1, source_target_pairs={{0,2},{2,0},{4,6},{6,4},{8,10},{10,8},{12,14},{14,12},{16,18},{18,... | collective-permute-start | bytes 4718600 | tf_op jit(solution)/shard_map/ppermute | solution.py:309
  256.1 13.2 %copy-start.5 = (bf16[1536,512]{1,0:T(8,128)(2,1)}, bf16[1536,512]{1,0:T(8,128)(2,1)S(1)}, u32[]{:S(2)}) copy-start(bf16[1536,512]{1,0:T(8,128)(2,1)S(1)} %collective-permute-done.32.refs_1_.refs_5_) | copy-start | bytes 4718596
  256.1 54.8 %collective-permute-start.27 = (bf16[1536,512]{1,0:T(8,128)(2,1)}, bf16[1536,512]{1,0:T(8,128)(2,1)}, u32[]{:S(2)}, u32[]{:S(2)}) collective-permute-start(bf16[1536,512]{1,0:T(8,128)(2,1)} %collective-permute-done.8.refs_0_), channel_id=1, source_target_pairs={{0,2},{2,0},{4,6},{6,4},{8,10},{10,8},{12,14},{14,12},{16,18},{18,... | collective-permute-start | bytes 4718600 | tf_op jit(solution)/shard_map/ppermute | solution.py:309
  279.1 8.5 %copy-start.8 = (bf16[1536,512]{1,0:T(8,128)(2,1)}, bf16[1536,512]{1,0:T(8,128)(2,1)S(1)}, u32[]{:S(2)}) copy-start(bf16[1536,512]{1,0:T(8,128)(2,1)S(1)} %collective-permute-done.19.refs_1_) | copy-start | bytes 4718596
  279.1 51.4 %collective-permute-start.21 = (bf16[1536,512]{1,0:T(8,128)(2,1)S(1)}, bf16[1536,512]{1,0:T(8,128)(2,1)S(1)}, u32[]{:S(2)}, u32[]{:S(2)}) collective-permute-start(bf16[1536,512]{1,0:T(8,128)(2,1)S(1)} %collective-permute-done.19.refs_1_), channel_id=1, source_target_pairs={{0,2},{2,0},{4,6},{6,4},{8,10},{10,8},{12,14},{14,12},{16,18},{18,... | collective-permute-start | bytes 4718600 | tf_op jit(solution)/shard_map/ppermute | solution.py:309
  279.2 51.4 %collective-permute-start.20 = (bf16[1536,512]{1,0:T(8,128)(2,1)}, bf16[1536,512]{1,0:T(8,128)(2,1)S(1)}, u32[]{:S(2)}, u32[]{:S(2)}) collective-permute-start(bf16[1536,512]{1,0:T(8,128)(2,1)} %collective-permute-done.9.refs_0_), channel_id=1, source_target_pairs={{0,2},{2,0},{4,6},{6,4},{8,10},{10,8},{12,14},{14,12},{16,18},{18,... | collective-permute-start | bytes 4718600 | tf_op jit(solution)/shard_map/ppermute | solution.py:309
  287.7 53.6 %collective-permute-start.36 = (bf16[1536,512]{1,0:T(8,128)(2,1)}, bf16[1536,512]{1,0:T(8,128)(2,1)S(1)}, u32[]{:S(2)}, u32[]{:S(2)}) collective-permute-start(bf16[1536,512]{1,0:T(8,128)(2,1)} %shard_map.85), channel_id=1, source_target_pairs={{0,1},{1,0},{2,3},{3,2},{4,5},{5,4},{6,7},{7,6},{8,9},{9,8},{10,11... | collective-permute-start | bytes 4718600 | tf_op jit(solution)/shard_map/ppermute | solution.py:324
  296.9 14.0 %copy-start.9 = (bf16[1536,512]{1,0:T(8,128)(2,1)}, bf16[1536,512]{1,0:T(8,128)(2,1)S(1)}, u32[]{:S(2)}) copy-start(bf16[1536,512]{1,0:T(8,128)(2,1)S(1)} %collective-permute-done.28.refs_3_) | copy-start | bytes 4718596
  296.9 60.8 %collective-permute-start.35 = (bf16[1536,512]{1,0:T(8,128)(2,1)}, bf16[1536,512]{1,0:T(8,128)(2,1)}, u32[]{:S(2)}, u32[]{:S(2)}) collective-permute-start(bf16[1536,512]{1,0:T(8,128)(2,1)} %shard_map.83), channel_id=1, source_target_pairs={{0,1},{1,0},{2,3},{3,2},{4,5},{5,4},{6,7},{7,6},{8,9},{9,8},{10,11... | collective-permute-start | bytes 4718600 | tf_op jit(solution)/shard_map/ppermute | solution.py:324
  341.3 16.4 %copy-start.12 = (bf16[1536,512]{1,0:T(8,128)(2,1)}, bf16[1536,512]{1,0:T(8,128)(2,1)S(1)}, u32[]{:S(2)}) copy-start(bf16[1536,512]{1,0:T(8,128)(2,1)S(1)} %collective-permute-done.36.refs_8_) | copy-start | bytes 4718596
  (8 other events, 17.4 us)

commit v4 on v0

--- a/solution.py
+++ b/solution.py
@@ -1,9 +1,15 @@
 import jax
 import jax.numpy as jnp
+import numpy as np
 from jax import lax
+from jax.experimental import pallas as pl
+from jax.experimental.pallas import tpu as pltpu
 from jax.sharding import PartitionSpec as P
 
 ROUNDS = 5
+TAIL = 16
+CHUNKS = 8
+VMEM = 56 * 1024 * 1024
 
 
 def passed_along(array, axis, by):
@@ -26,7 +32,7 @@
     return (weight * coulomb / denominator).astype(jnp.bfloat16)
 
 
-def per_device(three_index, orbital_map, occ_energy, vir_energy, pair_kept):
+def ring_plan(three_index, orbital_map, occ_energy, vir_energy, pair_kept):
     occ_count = three_index.shape[0]
     vir_count = three_index.shape[2]
     blocks = lax.axis_size("wide")
@@ -79,7 +85,473 @@
     return scattered + returned
 
 
+class Routes:
+    def __init__(self, blocks):
+        self.blocks = blocks
+        everyone = range(blocks)
+        self.lead = [self.place(w)[1] == self.place(w)[2] for w in everyone]
+        self.swap = [(w, w ^ 1) for w in everyone]
+        onward = [(w, self.along_z(w, 1)) for w in everyone]
+        backward = [(w, self.along_z(w, -1)) for w in everyone]
+        across = [(w, self.across_x(w)) for w in everyone]
+        self.rounds = [
+            self.either(across, onward),
+            self.either(onward, across),
+            self.either(across, backward),
+            self.either(backward, across),
+            self.either(backward, across),
+        ]
+
+    def place(self, w):
+        return w // 4, (w // 2) % 2, w % 2
+
+    def along_z(self, w, step):
+        z, x, core = self.place(w)
+        z = (z + (step if x == 1 else -step)) % (self.blocks // 4)
+        return (z * 2 + x) * 2 + core
+
+    def across_x(self, w):
+        z, x, core = self.place(w)
+        return (z * 2 + 1 - x) * 2 + 1 - core
+
+    def either(self, of_lead, of_other):
+        return [a if lead else b for lead, a, b in zip(self.lead, of_lead, of_other)]
+
+    def moved(self, ids, pairs):
+        out = [0] * self.blocks
+        for source, target in pairs:
+            out[target] = ids[source]
+        return out
+
+
+class Slab:
+    def __init__(self, array, ids, far=0):
+        self.pieces = list(array) if isinstance(array, (list, tuple)) else [array]
+        self.array = self.pieces[0]
+        self.ids = ids
+        self.far = far
+
+
+def pick(step, values):
+    out = values[0]
+    for index, value in enumerate(values):
+        if index and value != values[0]:
+            out = jnp.where(step == index, value, out)
+    return out
+
+
+def amplitude_call(jobs, table, lines, turned, vir_rows, vir_cols, earlier):
+    slabs = []
+    for slab, _ in jobs:
+        if slab not in slabs:
+            slabs.append(slab)
+    count, blocks = len(slabs), len(turned)
+    cols, aux = turned[0].shape
+    held_rows = aux + TAIL
+    pieces = [len(slab.pieces) for slab in slabs]
+    begins = [sum(pieces[:s]) for s in range(count)]
+    of_job = [slabs.index(slab) for slab, _ in jobs]
+    block_of = [block for _, block in jobs]
+    far_of = [slab.far for slab, _ in jobs]
+    line_of = [lines[slab] for slab, _ in jobs]
+    opens = [t for t in range(len(jobs)) if t == 0 or of_job[t] != of_job[t - 1]]
+    half = cols // 2
+
+    def kernel(scalars, *refs):
+        sources, refs = refs[: sum(pieces)], refs[sum(pieces) :]
+        row_sources, refs = refs[:blocks], refs[blocks + len(earlier) :]
+        vir_row, vir_col, out, held, rows, held_sems, row_sems = refs
+        step = pl.program_id(0)
+
+        def slab_copies(s):
+            row = 0
+            for index in range(pieces[s]):
+                source = sources[begins[s] + index]
+                target = held.at[s % 2, pl.ds(row, source.shape[0]), :]
+                yield pltpu.make_async_copy(source, target, held_sems.at[s % 2, index])
+                row += source.shape[0]
+
+        def row_copy(block):
+            return pltpu.make_async_copy(row_sources[block], rows.at[block], row_sems.at[block])
+
+        @pl.when(step == 0)
+        def _():
+            for copy in slab_copies(0):
+                copy.start()
+            for block in dict.fromkeys(block_of):
+                row_copy(block).start()
+
+        for s, t in enumerate(opens):
+
+            @pl.when(step == t)
+            def _(s=s):
+                for copy in slab_copies(s):
+                    copy.wait()
+                if s + 1 < count:
+                    for copy in slab_copies(s + 1):
+                        copy.start()
+
+        for block in dict.fromkeys(block_of):
+
+            @pl.when(step == block_of.index(block))
+            def _(block=block):
+                row_copy(block).wait()
+
+        slot = pick(step, [s % 2 for s in of_job])
+        block = pick(step, block_of)
+        line = pick(step, line_of)
+        plan = held[slot, aux:, :128].astype(jnp.float32)
+        lane = lax.broadcasted_iota(jnp.int32, plan.shape, 1).astype(jnp.float32)
+        row = lax.broadcasted_iota(jnp.int32, plan.shape, 0)
+        told = jnp.where(jnp.logical_and(row == 0, lane == scalars[line, 2]), plan, 0.0)
+        weight = scalars[line, 1] + jnp.sum(told, keepdims=True)
+        for begin in range(0, cols, half):
+            part = pl.ds(begin, half)
+            coulomb = jnp.dot(rows[block], held[slot, :aux, part], preferred_element_type=jnp.float32)
+            denominator = (vir_row[0] + vir_col[0, :, part]) - scalars[line, 0]
+            out[0, :, part] = (weight * coulomb / denominator).astype(out.dtype)
+
+    return pl.pallas_call(
+        kernel,
+        grid=(len(jobs),),
+        in_specs=[pl.BlockSpec(memory_space=pltpu.SMEM)]
+        + [pl.BlockSpec(memory_space=pl.ANY)] * (sum(pieces) + blocks + len(earlier))
+        + [
+            pl.BlockSpec((1, cols, 1), lambda t: (pick(t, block_of), 0, 0)),
+            pl.BlockSpec((1, 1, cols), lambda t: (pick(t, far_of), 0, 0)),
+        ],
+        out_specs=pl.BlockSpec((1, cols, cols), lambda t: (t, 0, 0)),
+        out_shape=jax.ShapeDtypeStruct((len(jobs), cols, cols), jnp.bfloat16),
+        scratch_shapes=[
+            pltpu.VMEM((2, held_rows, cols), jnp.bfloat16),
+            pltpu.VMEM((blocks, cols, aux), jnp.bfloat16),
+            pltpu.SemaphoreType.DMA((2, max(pieces))),
+            pltpu.SemaphoreType.DMA((blocks,)),
+        ],
+        compiler_params=pltpu.CompilerParams(vmem_limit_bytes=VMEM),
+        cost_estimate=pl.CostEstimate(
+            flops=2 * len(jobs) * cols * aux * cols,
+            bytes_accessed=2 * cols * (blocks * aux + count * aux + len(jobs) * cols),
+            transcendentals=0,
+        ),
+    )(table, *[p for s in slabs for p in s.pieces], *turned, *earlier, vir_rows, vir_cols)
+
+
+def in_chunks(source, target, sems):
+    rows = source.shape[0]
+    size = -(-rows // CHUNKS // 16) * 16
+    for index in range(CHUNKS):
+        begin = index * size
+        part = pl.ds(begin, min(size, rows - begin))
+        yield pltpu.make_async_copy(source.at[part], target.at[part], sems.at[index])
+
+
+def choice_call(flag, a, b, earlier, pieces=1):
+    rows = a.shape[0]
+    size = rows // pieces // 512 * 512 if pieces > 1 else rows
+    begins = [index * size for index in range(pieces)] + [rows]
+    shapes = [(end - begin, a.shape[1]) for begin, end in zip(begins, begins[1:])]
+
+    def kernel(flag_ref, a_ref, b_ref, *refs):
+        outs, sems = refs[len(earlier) : -1], refs[-1]
+
+        def copies(source):
+            for index, out in enumerate(outs):
+                part = source.at[pl.ds(begins[index], out.shape[0])]
+                yield from in_chunks(part, out, sems.at[index])
+
+        for value, source in ((1, a_ref), (0, b_ref)):
+
+            @pl.when(flag_ref[0] == value)
+            def _(source=source):
+                for copy in copies(source):
+                    copy.start()
+                for copy in copies(source):
+                    copy.wait()
+
+    return pl.pallas_call(
+        kernel,
+        in_specs=[pl.BlockSpec(memory_space=pltpu.SMEM)]
+        + [pl.BlockSpec(memory_space=pl.ANY)] * (2 + len(earlier)),
+        out_specs=[pl.BlockSpec(memory_space=pl.ANY)] * pieces,
+        out_shape=[jax.ShapeDtypeStruct(shape, a.dtype) for shape in shapes],
+        scratch_shapes=[pltpu.SemaphoreType.DMA((pieces, CHUNKS))],
+        cost_estimate=pl.CostEstimate(flops=0, bytes_accessed=2 * a.size * a.dtype.itemsize, transcendentals=0),
+    )(flag, a, b, *earlier)
+
+
+def join_call(earlier):
+    def kernel(*refs):
+        refs[-1][...] = jnp.zeros_like(refs[-1])
+
+    return pl.pallas_call(
+        kernel,
+        in_specs=[pl.BlockSpec(memory_space=pl.ANY)] * len(earlier),
+        out_specs=pl.BlockSpec(memory_space=pltpu.VMEM),
+        out_shape=jax.ShapeDtypeStruct((8, 128), jnp.float32),
+    )(*earlier)
+
+
+def density_call(terms, parts, out_dtype, aux, earlier, rows=None, copied=None):
+    count = len(terms)
+    extra = [] if copied is None else [copied]
+    pieces = [len(t[0].pieces) for t in terms]
+    begins = [sum(pieces[:s]) for s in range(count)]
+    depth = terms[0][0].array.shape[1]
+    cols = depth
+    begin, length = rows or (0, aux)
+    tile = 512
+    while length % tile or begin % tile:
+        tile //= 2
+    steps = length // tile
+    spans = []
+    for part in parts:
+        ends = np.cumsum([piece.shape[0] // tile for piece in part])
+        spans.append([(int(end) - piece.shape[0] // tile, int(end)) for end, piece in zip(ends, part)])
+    parts = [p for part in parts for p in part]
+
+    def kernel(*refs):
+        sources, refs = refs[: sum(pieces)], refs[sum(pieces) :]
+        amps, refs = refs[:count], refs[count + len(earlier) :]
+        source, refs = refs[: len(extra)], refs[len(extra) :]
+        part_refs, out, refs = refs[: len(parts)], refs[len(parts)], refs[len(parts) + 1 :]
+        target, (left, right, left_sems, right_sems, copy_sems) = refs[: len(extra)], refs[len(extra) :]
+        step = pl.program_id(0)
+        slot = step % 2
+
+        def amp_copies():
+            for s, (_, _, place) in enumerate(terms):
+                yield pltpu.make_async_copy(
+                    amps[s].at[place], right.at[:, pl.ds(s * depth, depth)], right_sems.at[s]
+                )
+
+        def slab_copies(which, start):
+            for s in range(count):
+                end = 0
+                for index in range(pieces[s]):
+                    source = sources[begins[s] + index]
+                    first = end
+                    end += source.shape[0] // tile
+
+                    def act(source=source, first=first, s=s):
+                        row = pl.multiple_of((begin // tile + which - first) * tile, tile)
+                        copy = pltpu.make_async_copy(
+                            source.at[pl.ds(row, tile), :],
+                            left.at[which % 2, :, pl.ds(s * depth, depth)],
+                            left_sems.at[which % 2, s],
+                        )
+                        copy.start() if start else copy.wait()
+
+                    at = begin // tile + which
+                    if pieces[s] == 1:
+                        act()
+                    else:
+                        pl.when(jnp.logical_and(at >= first, at < end))(act)
+
+        @pl.when(step == 0)
+        def _():
+            for copy in amp_copies():
+                copy.start()
+            slab_copies(step, True)
+            for pair in zip(source, target):
+                for copy in in_chunks(*pair, copy_sems):
+                    copy.start()
+
+        @pl.when(step + 1 < steps)
+        def _():
+            slab_copies(step + 1, True)
+
+        @pl.when(step == 0)
+        def _():
+            for copy in amp_copies():
+                copy.wait()
+
+        slab_copies(step, False)
+        total = lax.dot_general(
+            left[slot], right[...], (((1,), (1,)), ((), ())), preferred_element_type=jnp.float32
+        )
+        at = 0
+        for span in spans:
+            part = part_refs[at][...]
+            for index in range(1, len(span)):
+                part = jnp.where(step >= span[index][0], part_refs[at + index][...], part)
+            total = total + part.astype(jnp.float32)
+            at += len(span)
+        out[...] = total.astype(out.dtype)
+
+        @pl.when(step == steps - 1)
+        def _():
+            for pair in zip(source, target):
+                for copy in in_chunks(*pair, copy_sems):
+                    copy.wait()
+
+    def rows_of(start, end):
+        return pl.BlockSpec((tile, cols), lambda i: (jnp.clip(i - start, 0, end - start - 1), 0))
+
+    bytes_moved = 2 * count * (length * depth + cols * depth)
+    bytes_moved += sum(length * cols * p.dtype.itemsize for p in parts)
+    return pl.pallas_call(
+        kernel,
+        grid=(steps,),
+        in_specs=[pl.BlockSpec(memory_space=pl.ANY)] * (sum(pieces) + count + len(earlier) + len(extra))
+        + [rows_of(*ends) for span in spans for ends in span],
+        out_specs=[pl.BlockSpec((tile, cols), lambda i: (i, 0))]
+        + [pl.BlockSpec(memory_space=pl.ANY)] * len(extra),
+        out_shape=[jax.ShapeDtypeStruct((length, cols), out_dtype)]
+        + [jax.ShapeDtypeStruct(x.shape, x.dtype) for x in extra],
+        scratch_shapes=[
+            pltpu.VMEM((2, tile, count * depth), jnp.bfloat16),
+            pltpu.VMEM((cols, count * depth), jnp.bfloat16),
+            pltpu.SemaphoreType.DMA((2, count)),
+            pltpu.SemaphoreType.DMA((count,)),
+            pltpu.SemaphoreType.DMA((CHUNKS,)),
+        ],
+        compiler_params=pltpu.CompilerParams(vmem_limit_bytes=VMEM),
+        cost_estimate=pl.CostEstimate(
+            flops=2 * length * depth * cols * count,
+            bytes_accessed=(bytes_moved + length * cols * jnp.dtype(out_dtype).itemsize),
+            transcendentals=0,
+        ),
+    )(*[p for t in terms for p in t[0].pieces], *[t[1] for t in terms], *earlier, *extra, *parts)
+
+
+def paired_plan(three_index, orbital_map, occ_energy, vir_energy, pair_kept):
+    blocks = lax.axis_size("wide")
+    routes = Routes(blocks)
+    here = lax.axis_index("wide")
+    side = lax.axis_index("narrow")
+    aux, vir_count = three_index.shape[1:]
+
+    def moved(slab, pairs):
+        sent = [lax.ppermute(piece, "wide", pairs) for piece in slab.pieces]
+        return Slab(sent, routes.moved(slab.ids, pairs), slab.far)
+
+    def swapped(slab):
+        return moved(slab, routes.swap)
+
+    flag = jnp.asarray(np.array(routes.lead, np.int32))[here].reshape(1)
+
+    def chosen(of_lead, of_other, *earlier, pieces=1):
+        return Slab(
+            choice_call(flag, of_lead.array, of_other.array, earlier, pieces),
+            routes.either(of_lead.ids, of_other.ids),
+            of_lead.far,
+        )
+
+    def sibling(array):
+        return lax.ppermute(array, "narrow", [(0, 1), (1, 0)])
+
+    plan = jnp.zeros((TAIL, vir_count), jnp.bfloat16)
+    plan = plan.at[0, : ROUNDS + 1].set(pair_kept[:, 0].astype(jnp.bfloat16))
+    own = Slab(jnp.concatenate([three_index[0], plan]), list(range(blocks)))
+
+    r1 = moved(own, routes.rounds[0])
+    own_far = Slab(sibling(own.array), own.ids, 1)
+    mate = swapped(own)
+    s1 = swapped(r1)
+    sent2 = chosen(own, r1, mate.array)
+    r2 = moved(sent2, routes.rounds[1])
+
+    labels = jnp.arange(occ_energy.shape[0], dtype=jnp.int32)
+    picked = orbital_map[:, None] == labels[None, :]
+    energy = jnp.sum(jnp.where(picked, occ_energy[None, :], 0.0), axis=1)
+
+    def table_of(ids):
+        ids = np.array(ids, np.int32).T
+        places = np.arange(blocks)[:, None]
+        back, forth = (places - ids) % blocks, (ids - places) % blocks
+        behind = back <= ROUNDS
+        known = np.stack([ids, np.where(behind, back, -1), np.where(behind, -1, forth)])
+        block, mine, theirs = jnp.asarray(known.astype(np.int32))[:, here]
+        places = jnp.arange(blocks, dtype=jnp.int32)[None, :]
+        both = jnp.where(places == here, energy[None, :], 0.0)
+        both = both + jnp.where(places == block[:, None], energy[None, :], 0.0)
+        entries = jnp.arange(ROUNDS + 1, dtype=jnp.int32)[None, :]
+        kept = pair_kept[:, 0].astype(jnp.float32)[None, :]
+        weight = jnp.sum(jnp.where(entries == mine[:, None], kept, 0.0), axis=1)
+        return jnp.stack([jnp.sum(both, axis=1), weight, theirs.astype(jnp.float32)], axis=1)
+
+    vir = jnp.stack(
+        [lax.dynamic_slice_in_dim(vir_energy, s * vir_count, vir_count) for s in (side, 1 - side)]
+    )
+    vir_rows, vir_cols = vir[:, :, None], vir[:, None, :]
+
+    r3_ids = routes.moved(routes.either(r2.ids, own.ids), routes.rounds[2])
+    r4_ids = routes.moved(r3_ids, routes.rounds[3])
+    r5_ids = routes.moved(own.ids, routes.rounds[4])
+    all_ids = [own.ids, mate.ids, r1.ids, s1.ids, r2.ids, routes.moved(r2.ids, routes.swap)]
+    all_ids += [r3_ids, routes.moved(r3_ids, routes.swap), r4_ids, r5_ids, routes.moved(r5_ids, routes.swap)]
+    table = table_of(all_ids)
+    near, far = 0, 1
+    rows_near = three_index[0].T
+    stacks = {}
+
+    def amps(jobs, turned, *earlier):
+        lines = {slab: all_ids.index(slab.ids) for slab, _ in jobs}
+        stack = amplitude_call(jobs, table, lines, turned, vir_rows, vir_cols, earlier)
+        for place, job in enumerate(jobs):
+            stacks[job] = (stack, place)
+        return stack
+
+    def density(slabs, block, parts, dtype, *earlier, rows=None, copied=None):
+        terms = [(slab, *stacks[slab, block]) for slab in slabs]
+        out, *copy = density_call(terms, parts, dtype, aux, earlier, rows, copied)
+        return (out, *copy) if copy else out
+
+    f32, bf16 = jnp.float32, jnp.bfloat16
+    done = amps([(s, near) for s in (own, mate, r1, s1)], [rows_near], sent2.array)
+    mate_far = swapped(own_far)
+
+    sent3 = chosen(r2, own, done)
+    r3 = moved(sent3, routes.rounds[2])
+    s2 = swapped(r2)
+    rows_far = own_far.array[:aux].T
+    part = density([own, mate, r1, s1], near, [], f32, sent3.array)
+    jobs = [(r1, far), (s1, far), (r2, near), (r2, far), (s2, far), (s2, near)]
+    jobs += [(own_far, near), (mate_far, near)]
+    done = amps(jobs, [rows_near, rows_far], part)
+
+    r3 = chosen(r3, r3, done)
+    r4 = moved(r3, routes.rounds[3])
+    s3 = swapped(r3)
+    jobs = [(r3, near), (r3, far), (s3, far), (s3, near)]
+    done = amps(jobs, [rows_near, rows_far], done)
+    slabs = [own_far, mate_far, r2, s2, r3, s3]
+    part, again = density(slabs, near, [[part]], f32, done, copied=own.array)
+    r5 = moved(Slab(again, own.ids), routes.rounds[4])
+
+    done = amps([(r4, far)], [rows_near, rows_far], part)
+    slabs = [r1, s1, r2, s2, r3, s3, r4]
+    half = aux // 2
+    sent0, again = density(slabs, far, [], bf16, done, rows=(0, half), copied=own_far.array)
+    sent1 = density(slabs, far, [], bf16, sent0, rows=(half, half))
+    r6 = moved(Slab(again, own.ids, 1), routes.rounds[4])
+    incoming = [sibling(sent0), sibling(sent1)]
+    done = amps([(r4, near)], [rows_near], sent1)
+
+    r5 = chosen(r5, r5, done, pieces=3)
+    s5 = swapped(r5)
+    done = amps([(r5, near)], [rows_near], r5.array)
+    done = join_call([incoming[0], done])
+    done = amps([(s5, near)], [rows_near], done)
+    part = density([r4, r5, s5], near, [[part]], f32, done)
+    r6 = chosen(r6, r6, part, pieces=3)
+    s6 = swapped(r6)
+    done = amps([(r6, near)], [rows_near], r6.array)
+    done = join_call([incoming[1], done])
+    done = amps([(s6, near)], [rows_near], done)
+    return density([r6, s6], near, [[part], incoming], f32, done)[None]
+
+
 def solution(mesh):
+    wide, narrow = mesh.shape["wide"], mesh.shape["narrow"]
+    paired = narrow == 2 and wide % 4 == 0 and wide > 2 * ROUNDS + 1 and ROUNDS == 5
+
+    def per_device(three_index, *rest):
+        if paired and three_index.shape[0] == 1:
+            return paired_plan(three_index, *rest)
+        return ring_plan(three_index, *rest)
+
     placed = (P("wide", None, "narrow"), P(), P(), P(), P(None, "wide"))
     return jax.shard_map(
         per_device, mesh=mesh, in_specs=placed, out_specs=P("wide", None, "narrow"), check_vma=False

time: 714 us -> 947 us (1.33)
  Pallas kernels: 0 us -> 820 us
  waiting for transfers between devices: 497 us -> 72.6 us
  matrix products: 137 us -> 0 us
  between operations: 21 us -> 0.46 us
  local copies, waits for them, and re-layouts: 9.23 us -> 28.7 us
  other arithmetic: 20.3 us -> 4.07 us
    pallas_call x0 -> x22, Pallas kernels: none -> 820 us  [the longest x5 488 us: choice_call(): pl.pallas_call(kernel, in_specs=[pl.BlockSpec(memory_space=pltpu.SMEM)] +...]
    ppermute x10 -> x20, waiting for transfers between devices: 491 us -> 72.6 us  [the longest x17 72.6 us: moved(): sent = [lax.ppermute(piece, 'wide', pairs) for piece in slab.pieces]]
    dot_general x16 -> x0, matrix products: 137 us -> none  [the longest x5 60.5 us: per_device(): jnp.einsum('ijab,jpb->ipa', amplitude, visiting, preferred_element_type=j...]
    add x4 -> x0, other arithmetic: 15.9 us -> none  [the longest x1 8.81 us: per_device(): return scattered + returned]
    unnamed x28 -> x26, local copies, waits for them, and re-layouts: 1.25 us -> 16.3 us
    ppermute x10 -> x20, starting transfers between devices: 21.4 us -> 17.4 us  [the longest x17 14.6 us: moved(): sent = [lax.ppermute(piece, 'wide', pairs) for piece in slab.pieces]]
  transfers between devices with their start and end apart: 12 -> 20, of which waited for: 9 -> 3; matrix products, arithmetic and copies ran while one was open for 21% -> 1% of each run, Pallas kernels for 0% -> 75%
where the time goes in v4:
time: 947 us; the launch traced here: 944 us
  Pallas kernels  820 us (87%)
  waiting for transfers between devices  72.6 us (8%)
  local copies, waits for them, and re-layouts  28.7 us (3%)
  starting transfers between devices  17.4 us (2%)
    pallas_call x5, Pallas kernels, choice_call(): pl.pallas_call(kernel, in_specs=[pl.BlockSpec(memory_space=pltpu.SMEM)] +...  488 us
    pallas_call x6, Pallas kernels, density_call(): pl.pallas_call(kernel, grid=(steps,), in_specs=[pl.BlockSpec(memory_space...  248 us
    pallas_call x9, Pallas kernels, amplitude_call(): pl.pallas_call(kernel, grid=(len(jobs),), in_specs=[pl.BlockSpec(memory_s...  83.2 us
    ppermute x17, waiting for transfers between devices, moved(): sent = [lax.ppermute(piece, 'wide', pairs) for piece in slab.pieces]  72.6 us
  transfers between devices with their start and end apart: 20, of which 3 were waited for; matrix products, arithmetic and copies ran while one was open for 1% of the time, Pallas kernels for 75%

profile of v4, /device:TPU:3, one launch (start us, length us, event | category | flops | bytes accessed | tf_op | source)
XLA Modules:
  0.0 943.6 jit_solution(7576648414528127198)
XLA Ops:
  0.0 0.7 convert_bitcast_fusion
  0.7 3.2 copy.75
  4.0 2.1 fusion.1
  6.6 5.6 copy.77.a_ref.refs_0_.b_ref.refs_13_
  12.3 2.2 collective-permute-start.2
  14.5 1.2 collective-permute-start.6
  15.8 0.6 dynamic_slice.12.flag_ref
  16.4 33.4 %collective-permute-done.b_ref.refs_2_.refs_0_ = bf16[3088,512]{1,0:T(8,128)(2,1)S(1)} collective-permute-done((bf16[3088,512]{1,0:T(8,128)(2,1)}, bf16[3088,512]{1,0:T(8,128)(2,1)S(1)}, u32[]{:S(2)}, u32[]{:S(2)}) %collective-permute-start) | collective-permute-done | bytes 3162144 | tf_op jit(solution)/shard_map/ppermute | solution.py:426
  49.8 1.7 copy-done.2
  51.5 97.6 %shard_map.73.refs_5_ = bf16[3088,512]{1,0:T(8,128)(2,1)} custom-call(s32[1]{0:T(128)} %dynamic_slice.12.flag_ref, bf16[3088,512]{1,0:T(8,128)(2,1)} %copy.77.a_ref.refs_0_.b_ref.refs_13_, bf16[3088,512]{1,0:T(8,128)(2,1)} %copy-done.2, bf16[3088,512]{1,0:T(8,128)(2,1)} %collective-permute-done.2.refs_0_.refs_1_), custom_call_target="tpu_custom_call" | custom-call | bytes 6324224 | tf_op jit(solution)/shard_map/pallas_call | solution.py:272
  149.1 1.3 collective-permute-start.3
  150.4 1.5 collective-permute-start.1
  152.2 35.3 %collective-permute-done.3.a_ref.refs_2_ = bf16[3088,512]{1,0:T(8,128)(2,1)S(1)} collective-permute-done((bf16[3088,512]{1,0:T(8,128)(2,1)}, bf16[3088,512]{1,0:T(8,128)(2,1)S(1)}, u32[]{:S(2)}, u32[]{:S(2)}) %collective-permute-start.3) | collective-permute-done | bytes 3162144 | tf_op jit(solution)/shard_map/ppermute | solution.py:426
  187.5 1.4 collective-permute-start.4
  188.9 0.7 fusion.4
  189.9 0.7 copy.80.scalars
  190.7 1.0 copy.82.refs_6_.refs_9_.refs_5_.refs_4_.refs_3_
  191.7 0.6 broadcast_in_dim.66.refs_7_.refs_10_.refs_6_.refs_5_.refs_4_
  192.2 12.2 %shard_map.74.refs_0_.refs_4_.refs_5_.refs_6_.refs_7_ = bf16[4,512,512]{2,1,0:T(8,128)(2,1)} custom-call(f32[11,3]{1,0:T(8,128)} %copy.80.scalars, bf16[3088,512]{1,0:T(8,128)(2,1)} %copy.77.a_ref.refs_0_.b_ref.refs_13_, bf16[3088,512]{1,0:T(8,128)(2,1)} %collective-permute-done.2.refs_0_.refs_1_, bf16[3088,512]{1,0:T(8,128)(2,1)} %copy-done.2, ...), custom_call_target="tpu_custom_call" | custom-call | flops 6442450944 | bytes 17825792 | tf_op jit(solution)/shard_map/pallas_call | solution.py:214
  204.5 97.6 %shard_map.75.refs_8_ = bf16[3088,512]{1,0:T(8,128)(2,1)} custom-call(s32[1]{0:T(128)} %dynamic_slice.12.flag_ref, bf16[3088,512]{1,0:T(8,128)(2,1)} %copy-done.3, bf16[3088,512]{1,0:T(8,128)(2,1)} %copy.77.a_ref.refs_0_.b_ref.refs_13_, bf16[4,512,512]{2,1,0:T(8,128)(2,1)} %shard_map.74.refs_0_.refs_4_.refs_5_.refs_6_.refs_7_), custom_call_target="tpu_custom_call" | custom-call | bytes 6324224 | tf_op jit(solution)/shard_map/pallas_call | solution.py:272
  302.3 3.8 slice.23
  306.0 4.7 copy.104
  310.7 13.0 %shard_map.76.refs_8_.refs_14_ = f32[3072,512]{1,0:T(8,128)} custom-call(bf16[3088,512]{1,0:T(8,128)(2,1)} %copy.77.a_ref.refs_0_.b_ref.refs_13_, bf16[3088,512]{1,0:T(8,128)(2,1)} %collective-permute-done.2.refs_0_.refs_1_, bf16[3088,512]{1,0:T(8,128)(2,1)} %copy-done.2, bf16[3088,512]{1,0:T(8,128)(2,1)} %collective-permute-done.1.refs_3_.refs_1_, ...), custom_call_target="tpu_custom_call" | custom-call | flops 6442450944 | bytes 20971520 | tf_op jit(solution)/shard_map/pallas_call | solution.py:393
  323.7 20.0 %shard_map.77.refs_0_.refs_4_.refs_6_.refs_7_.refs_8_.refs_9_.refs_10_ = bf16[8,512,512]{2,1,0:T(8,128)(2,1)} custom-call(f32[11,3]{1,0:T(8,128)} %copy.80.scalars, bf16[3088,512]{1,0:T(8,128)(2,1)} %copy-done.2, bf16[3088,512]{1,0:T(8,128)(2,1)} %collective-permute-done.1.refs_3_.refs_1_, bf16[3088,512]{1,0:T(8,128)(2,1)} %copy-done.3, ...), custom_call_target="tpu_custom_call" | custom-call | flops 12884901888 | bytes 29360128 | tf_op jit(solution)/shard_map/pallas_call | solution.py:214
  343.8 97.6 %shard_map.78.refs_0_.refs_4_ = bf16[3088,512]{1,0:T(8,128)(2,1)} custom-call(s32[1]{0:T(128)} %dynamic_slice.12.flag_ref, bf16[3088,512]{1,0:T(8,128)(2,1)} %collective-permute-done.5.a_ref.b_ref, bf16[3088,512]{1,0:T(8,128)(2,1)} %collective-permute-done.5.a_ref.b_ref, bf16[8,512,512]{2,1,0:T(8,128)(2,1)} %shard_map.77.refs_0_.refs_4_.refs_6_.refs_7_.refs_8_.refs_9_.refs_10_), custom_call_target="tpu_custom_call" | custom-call | bytes 6324224 | tf_op jit(solution)/shard_map/pallas_call | solution.py:272
  441.4 1.9 collective-permute-start.8
  443.3 1.6 collective-permute-start.9
  444.9 3.9 collective-permute-done.8.refs_1_.refs_5_
  448.8 1.7 copy-done.4
  450.5 12.0 %shard_map.79.refs_10_.refs_11_.refs_12_ = bf16[4,512,512]{2,1,0:T(8,128)(2,1)} custom-call(f32[11,3]{1,0:T(8,128)} %copy.80.scalars, bf16[3088,512]{1,0:T(8,128)(2,1)} %shard_map.78.refs_0_.refs_4_, bf16[3088,512]{1,0:T(8,128)(2,1)} %copy-done.4, bf16[512,3072]{1,0:T(8,128)(2,1)} %bitcast.24, bf16[512,3072]{1,0:T(8,128)(2,1)} %bitcast.32, ...), custom_call_target="tpu_custom_call" | custom-call | flops 6442450944 | bytes 14680064 | tf_op jit(solution)/shard_map/pallas_call | solution.py:214
  462.5 99.4 %shard_map.80 = (f32[3072,512]{1,0:T(8,128)}, bf16[3088,512]{1,0:T(8,128)(2,1)}) custom-call(bf16[3088,512]{1,0:T(8,128)(2,1)} %collective-permute-done.6.refs_4_.refs_0_.refs_15_, bf16[3088,512]{1,0:T(8,128)(2,1)} %collective-permute-done.7.refs_5_.refs_1_, bf16[3088,512]{1,0:T(8,128)(2,1)} %copy-done.3, bf16[3088,512]{1,0:T(8,128)(2,1)} %collective-permute-done.4.refs_3_, ...), custom_call_target="tpu_custom_call" | custom-call | flops 9663676416 | bytes 34603008 | tf_op jit(solution)/shard_map/pallas_call | solution.py:393
  561.9 2.0 collective-permute-start.11
  563.9 1.7 copy-done.1
  565.6 6.4 shard_map.81.refs_13_.refs_14_
  572.0 98.0 %shard_map.82 = (bf16[1536,512]{1,0:T(8,128)(2,1)}, bf16[3088,512]{1,0:T(8,128)(2,1)}) custom-call(bf16[3088,512]{1,0:T(8,128)(2,1)} %copy-done.2, bf16[3088,512]{1,0:T(8,128)(2,1)} %collective-permute-done.1.refs_3_.refs_1_, bf16[3088,512]{1,0:T(8,128)(2,1)} %copy-done.3, bf16[3088,512]{1,0:T(8,128)(2,1)} %collective-permute-done.4.refs_3_, ...), custom_call_target="tpu_custom_call" | custom-call | flops 5637144576 | bytes 16252928 | tf_op jit(solution)/shard_map/pallas_call | solution.py:393
  670.3 1.3 collective-permute-start.15
  671.6 11.6 %shard_map.83.refs_2_ = bf16[1536,512]{1,0:T(8,128)(2,1)} custom-call(bf16[3088,512]{1,0:T(8,128)(2,1)} %copy-done.2, bf16[3088,512]{1,0:T(8,128)(2,1)} %collective-permute-done.1.refs_3_.refs_1_, bf16[3088,512]{1,0:T(8,128)(2,1)} %copy-done.3, bf16[3088,512]{1,0:T(8,128)(2,1)} %collective-permute-done.4.refs_3_, ...), custom_call_target="tpu_custom_call" | custom-call | flops 5637144576 | bytes 16252928 | tf_op jit(solution)/shard_map/pallas_call | solution.py:393
  683.2 6.5 shard_map.84.refs_0_.refs_7_
  689.7 1.7 copy-done.5
  691.4 97.7 %shard_map.85 = (bf16[1024,512]{1,0:T(8,128)(2,1)}, bf16[1024,512]{1,0:T(8,128)(2,1)}, bf16[1040,512]{1,0:T(8,128)(2,1)}) custom-call(s32[1]{0:T(128)} %dynamic_slice.12.flag_ref, bf16[3088,512]{1,0:T(8,128)(2,1)} %copy-done.5, bf16[3088,512]{1,0:T(8,128)(2,1)} %copy-done.5, bf16[1,512,512]{2,1,0:T(8,128)(2,1)} %shard_map.84.refs_0_.refs_7_), custom_call_target="tpu_custom_call" | custom-call | bytes 6324224 | tf_op jit(solution)/shard_map/pallas_call | solution.py:272
  790.1 6.5 shard_map.86.refs_1_.refs_8_
  797.6 6.5 shard_map.88.refs_9_.refs_10_
  804.1 13.4 %shard_map.89.refs_0_.refs_9_ = f32[3072,512]{1,0:T(8,128)} custom-call(bf16[3088,512]{1,0:T(8,128)(2,1)} %copy-done.1, bf16[1024,512]{1,0:T(8,128)(2,1)} %get-tuple-element.31.refs_0_.refs_4_.refs_1_, bf16[1024,512]{1,0:T(8,128)(2,1)} %get-tuple-element.32.refs_1_.refs_2_, bf16[1040,512]{1,0:T(8,128)(2,1)} %get-tuple-element.33.refs_2_.refs_3_, ...), custom_call_target="tpu_custom_call" | custom-call | flops 4831838208 | bytes 23592960 | tf_op jit(solution)/shard_map/pallas_call | solution.py:393
  817.5 97.7 %shard_map.90 = (bf16[1024,512]{1,0:T(8,128)(2,1)}, bf16[1024,512]{1,0:T(8,128)(2,1)}, bf16[1040,512]{1,0:T(8,128)(2,1)}) custom-call(s32[1]{0:T(128)} %dynamic_slice.12.flag_ref, bf16[3088,512]{1,0:T(8,128)(2,1)} %collective-permute-done.10.a_ref.b_ref, bf16[3088,512]{1,0:T(8,128)(2,1)} %collective-permute-done.10.a_ref.b_ref, ...), custom_call_target="tpu_custom_call" | custom-call | bytes 6324224 | tf_op jit(solution)/shard_map/pallas_call | solution.py:272
  916.3 6.5 shard_map.91.refs_1_.refs_6_
  922.8 1.2 copy-done.7
  924.6 6.5 shard_map.93.refs_7_.refs_8_
  931.1 12.3 %shard_map.94 = f32[3072,512]{1,0:T(8,128)} custom-call(bf16[1024,512]{1,0:T(8,128)(2,1)} %get-tuple-element.34.refs_0_.refs_4_, bf16[1024,512]{1,0:T(8,128)(2,1)} %get-tuple-element.35.refs_1_, bf16[1040,512]{1,0:T(8,128)(2,1)} %get-tuple-element.36.refs_2_, bf16[1024,512]{1,0:T(8,128)(2,1)} %collective-permute-done.16.refs_0_.refs_3_, ...), custom_call_target="tpu_custom_call" | custom-call | flops 3221225472 | bytes 26214400 | tf_op jit(solution)/shard_map/pallas_call | solution.py:393
  (57 shorter events, 5.3 us)
Async XLA Ops:
  3.9 2.7 copy-start
  6.6 9.1 copy-start.11
  12.3 37.5 %collective-permute-start = (bf16[3088,512]{1,0:T(8,128)(2,1)}, bf16[3088,512]{1,0:T(8,128)(2,1)S(1)}, u32[]{:S(2)}, u32[]{:S(2)}) collective-permute-start(bf16[3088,512]{1,0:T(8,128)(2,1)} %copy.77.a_ref.refs_0_.b_ref.refs_13_), channel_id=1, source_target_pairs={{0,6},{2,26},{4,12},{6,0},{8,14},{10,2},{12,20},{14,8},{16,22},{18... | collective-permute-start | bytes 9486344 | tf_op jit(solution)/shard_map/ppermute | solution.py:426
  12.3 37.5 %collective-permute-start.2 = (bf16[3088,512]{1,0:T(8,128)(2,1)}, bf16[3088,512]{1,0:T(8,128)(2,1)}, u32[]{:S(2)}, u32[]{:S(2)}) collective-permute-start(bf16[3088,512]{1,0:T(8,128)(2,1)} %copy.77.a_ref.refs_0_.b_ref.refs_13_), channel_id=1, source_target_pairs={{0,2},{2,0},{4,6},{6,4},{8,10},{10,8},{12,14},{14,12},{16,18},{18,... | collective-permute-start | bytes 9486344 | tf_op jit(solution)/shard_map/ppermute | solution.py:426
  14.5 137.5 %collective-permute-start.6 = (bf16[3088,512]{1,0:T(8,128)(2,1)}, bf16[3088,512]{1,0:T(8,128)(2,1)}, u32[]{:S(2)}, u32[]{:S(2)}) collective-permute-start(bf16[3088,512]{1,0:T(8,128)(2,1)} %copy.77.a_ref.refs_0_.b_ref.refs_13_), channel_id=1, source_target_pairs={{0,1},{1,0},{2,3},{3,2},{4,5},{5,4},{6,7},{7,6},{8,9},{9,8},{10,11... | collective-permute-start | bytes 9486344 | tf_op jit(solution)/shard_map/ppermute | solution.py:442
  16.4 135.5 %copy-start.9 = (f32[16]{0:T(128)S(1)}, f32[16]{0:T(128)}, u32[]{:S(2)}) copy-start(f32[16]{0:T(128)} %param.11) | copy-start | bytes 196
  16.4 135.5 %copy-start.10 = (s32[16]{0:T(128)S(1)}, s32[16]{0:T(128)}, u32[]{:S(2)}) copy-start(s32[16]{0:T(128)} %param.10) | copy-start | bytes 196
  16.4 174.2 %copy-start.8 = (f32[1024]{0:T(1024)S(1)}, f32[1024]{0:T(1024)}, u32[]{:S(2)}) copy-start(f32[1024]{0:T(1024)} %param.12) | copy-start | bytes 12292
  49.8 1.7 copy-start.2
  149.1 38.4 %collective-permute-start.3 = (bf16[3088,512]{1,0:T(8,128)(2,1)}, bf16[3088,512]{1,0:T(8,128)(2,1)S(1)}, u32[]{:S(2)}, u32[]{:S(2)}) collective-permute-start(bf16[3088,512]{1,0:T(8,128)(2,1)} %shard_map.73.refs_5_), channel_id=1, source_target_pairs={{0,24},{2,4},{4,2},{6,14},{8,0},{10,12},{12,10},{14,22},{16,8},{18... | collective-permute-start | bytes 9486344 | tf_op jit(solution)/shard_map/ppermute | solution.py:426
  150.4 41.8 %collective-permute-start.1 = (bf16[3088,512]{1,0:T(8,128)(2,1)}, bf16[3088,512]{1,0:T(8,128)(2,1)}, u32[]{:S(2)}, u32[]{:S(2)}) collective-permute-start(bf16[3088,512]{1,0:T(8,128)(2,1)} %copy-done.2), channel_id=1, source_target_pairs={{0,2},{2,0},{4,6},{6,4},{8,10},{10,8},{12,14},{14,12},{16,18},{18,... | collective-permute-start | bytes 9486344 | tf_op jit(solution)/shard_map/ppermute | solution.py:426
  152.1 171.6 %collective-permute-start.7 = (bf16[3088,512]{1,0:T(8,128)(2,1)}, bf16[3088,512]{1,0:T(8,128)(2,1)}, u32[]{:S(2)}, u32[]{:S(2)}) collective-permute-start(bf16[3088,512]{1,0:T(8,128)(2,1)} %collective-permute-done.6.refs_4_.refs_0_.refs_15_), channel_id=1, source_target_pairs={{0,2},{2,0},{4,6},{6,4},{8,10},{10,8},{12,14},{14,12},{16,18},{18,... | collective-permute-start | bytes 9486344 | tf_op jit(solution)/shard_map/ppermute | solution.py:426
  187.5 17.0 %copy-start.3 = (bf16[3088,512]{1,0:T(8,128)(2,1)}, bf16[3088,512]{1,0:T(8,128)(2,1)S(1)}, u32[]{:S(2)}) copy-start(bf16[3088,512]{1,0:T(8,128)(2,1)S(1)} %collective-permute-done.3.a_ref.refs_2_) | copy-start | bytes 9486340
  187.5 136.2 %collective-permute-start.4 = (bf16[3088,512]{1,0:T(8,128)(2,1)S(1)}, bf16[3088,512]{1,0:T(8,128)(2,1)}, u32[]{:S(2)}, u32[]{:S(2)}) collective-permute-start(bf16[3088,512]{1,0:T(8,128)(2,1)S(1)} %collective-permute-done.3.a_ref.refs_2_), channel_id=1, source_target_pairs={{0,2},{2,0},{4,6},{6,4},{8,10},{10,8},{12,14},{14,12},{16,18},{18,... | collective-permute-start | bytes 9486344 | tf_op jit(solution)/shard_map/ppermute | solution.py:426
  302.1 41.7 %collective-permute-start.5 = (bf16[3088,512]{1,0:T(8,128)(2,1)}, bf16[3088,512]{1,0:T(8,128)(2,1)}, u32[]{:S(2)}, u32[]{:S(2)}) collective-permute-start(bf16[3088,512]{1,0:T(8,128)(2,1)} %shard_map.75.refs_8_), channel_id=1, source_target_pairs={{0,6},{2,10},{4,28},{6,0},{8,14},{10,18},{12,4},{14,8},{16,22},{18... | collective-permute-start | bytes 9486344 | tf_op jit(solution)/shard_map/ppermute | solution.py:426
  441.4 7.4 collective-permute-start.8
  443.3 120.6 %collective-permute-start.9 = (bf16[3088,512]{1,0:T(8,128)(2,1)}, bf16[3088,512]{1,0:T(8,128)(2,1)S(1)}, u32[]{:S(2)}, u32[]{:S(2)}) collective-permute-start(bf16[3088,512]{1,0:T(8,128)(2,1)} %shard_map.78.refs_0_.refs_4_), channel_id=1, source_target_pairs={{0,8},{2,4},{4,2},{6,30},{8,16},{10,12},{12,10},{14,6},{16,24},{18... | collective-permute-start | bytes 9486344 | tf_op jit(solution)/shard_map/ppermute | solution.py:426
  448.8 1.7 copy-start.4
  561.9 127.8 %collective-permute-start.11 = (bf16[3088,512]{1,0:T(8,128)(2,1)}, bf16[3088,512]{1,0:T(8,128)(2,1)S(1)}, u32[]{:S(2)}, u32[]{:S(2)}) collective-permute-start(bf16[3088,512]{1,0:T(8,128)(2,1)} %get-tuple-element.29), channel_id=1, source_target_pairs={{0,8},{2,4},{4,2},{6,30},{8,16},{10,12},{12,10},{14,6},{16,24},{18... | collective-permute-start | bytes 9486344 | tf_op jit(solution)/shard_map/ppermute | solution.py:426
  563.9 1.7 copy-start.1
  670.0 147.5 %collective-permute-start.10 = (bf16[3088,512]{1,0:T(8,128)(2,1)}, bf16[3088,512]{1,0:T(8,128)(2,1)}, u32[]{:S(2)}, u32[]{:S(2)}) collective-permute-start(bf16[3088,512]{1,0:T(8,128)(2,1)} %get-tuple-element.28), channel_id=1, source_target_pairs={{0,8},{2,4},{4,2},{6,30},{8,16},{10,12},{12,10},{14,6},{16,24},{18... | collective-permute-start | bytes 9486344 | tf_op jit(solution)/shard_map/ppermute | solution.py:426
  670.3 126.4 %collective-permute-start.15 = (bf16[1536,512]{1,0:T(8,128)(2,1)}, bf16[1536,512]{1,0:T(8,128)(2,1)}, u32[]{:S(2)}, u32[]{:S(2)}) collective-permute-start(bf16[1536,512]{1,0:T(8,128)(2,1)} %get-tuple-element.30.refs_14_), channel_id=1, source_target_pairs={{0,1},{1,0},{2,3},{3,2},{4,5},{5,4},{6,7},{7,6},{8,9},{9,8},{10,11... | collective-permute-start | bytes 4718600 | tf_op jit(solution)/shard_map/ppermute | solution.py:442
  689.7 1.7 copy-start.5
  789.1 8.5 collective-permute-start.14
  789.6 8.0 collective-permute-start.12
  789.7 7.0 copy-start.6
  789.7 7.9 collective-permute-start.13
  796.7 126.1 %collective-permute-start.19 = (bf16[1536,512]{1,0:T(8,128)(2,1)S(1)}, bf16[1536,512]{1,0:T(8,128)(2,1)S(1)}, u32[]{:S(2)}, u32[]{:S(2)}) collective-permute-start(bf16[1536,512]{1,0:T(8,128)(2,1)S(1)} %copy-done.6), channel_id=1, source_target_pairs={{0,1},{1,0},{2,3},{3,2},{4,5},{5,4},{6,7},{7,6},{8,9},{9,8},{10,11... | collective-permute-start | bytes 4718600 | tf_op jit(solution)/shard_map/ppermute | solution.py:442
  915.2 9.4 collective-permute-start.18
  915.8 8.8 collective-permute-start.16
  915.9 8.8 collective-permute-start.17
  922.8 1.2 copy-start.7

commit v5 on v4

--- a/solution.py
+++ b/solution.py
@@ -8,7 +8,7 @@
 
 ROUNDS = 5
 TAIL = 16
-CHUNKS = 8
+CHUNK = 512
 VMEM = 56 * 1024 * 1024
 
 
@@ -237,45 +237,93 @@
     )(table, *[p for s in slabs for p in s.pieces], *turned, *earlier, vir_rows, vir_cols)
 
 
-def in_chunks(source, target, sems):
-    rows = source.shape[0]
-    size = -(-rows // CHUNKS // 16) * 16
-    for index in range(CHUNKS):
-        begin = index * size
-        part = pl.ds(begin, min(size, rows - begin))
-        yield pltpu.make_async_copy(source.at[part], target.at[part], sems.at[index])
-
-
-def choice_call(flag, a, b, earlier, pieces=1):
-    rows = a.shape[0]
-    size = rows // pieces // 512 * 512 if pieces > 1 else rows
+def chunks_of(rows):
+    return [(begin, min(CHUNK, rows - begin)) for begin in range(0, rows, CHUNK)]
+
+
+def copies_in(sources, held, sems):
+    row, index = 0, 0
+    for source in sources:
+        for begin, size in chunks_of(source.shape[0]):
+            yield pltpu.make_async_copy(
+                source.at[pl.ds(begin, size)], held.at[pl.ds(row + begin, size)], sems.at[index]
+            )
+            index += 1
+        row += source.shape[0]
+
+
+def copies_out(held, targets, sems):
+    row, index = 0, 0
+    for target in targets:
+        for begin, size in chunks_of(target.shape[0]):
+            yield pltpu.make_async_copy(
+                held.at[pl.ds(row + begin, size)], target.at[pl.ds(begin, size)], sems.at[index]
+            )
+            index += 1
+        row += target.shape[0]
+
+
+def copy_scratch(rows, cols):
+    count = len(chunks_of(rows)) + 1
+    return [
+        pltpu.VMEM((rows, cols), jnp.bfloat16),
+        pltpu.SemaphoreType.DMA((count,)),
+        pltpu.SemaphoreType.DMA((count,)),
+    ]
+
+
+def copy_through(sources, targets, held, in_sems, out_sems):
+    for copy in copies_in(sources, held, in_sems):
+        copy.start()
+    for copy in copies_in(sources, held, in_sems):
+        copy.wait()
+    for copy in copies_out(held, targets, out_sems):
+        copy.start()
+    for copy in copies_out(held, targets, out_sems):
+        copy.wait()
+
+
+def append_call(array, tail):
+    def kernel(array_ref, tail_ref, out, held, in_sems, out_sems):
+        copy_through([array_ref, tail_ref], [out], held, in_sems, out_sems)
+
+    rows, cols = array.shape[0] + tail.shape[0], array.shape[1]
+    return pl.pallas_call(
+        kernel,
+        in_specs=[pl.BlockSpec(memory_space=pl.ANY)] * 2,
+        out_specs=pl.BlockSpec(memory_space=pl.ANY),
+        out_shape=jax.ShapeDtypeStruct((rows, cols), array.dtype),
+        scratch_shapes=copy_scratch(rows, cols),
+        compiler_params=pltpu.CompilerParams(vmem_limit_bytes=VMEM),
+    )(array, tail)
+
+
+def choice_call(flag, a, b, earlier, pieces=1, keep=False):
+    rows, cols = a.shape
+    size = rows // pieces // CHUNK * CHUNK if pieces > 1 else rows
     begins = [index * size for index in range(pieces)] + [rows]
-    shapes = [(end - begin, a.shape[1]) for begin, end in zip(begins, begins[1:])]
+    shapes = [(end - begin, cols) for begin, end in zip(begins, begins[1:])]
+    kept = [(rows, cols)] if keep else []
 
     def kernel(flag_ref, a_ref, b_ref, *refs):
-        outs, sems = refs[len(earlier) : -1], refs[-1]
-
-        def copies(source):
-            for index, out in enumerate(outs):
-                part = source.at[pl.ds(begins[index], out.shape[0])]
-                yield from in_chunks(part, out, sems.at[index])
-
+        outs, kept_outs = refs[len(earlier) :][:pieces], refs[len(earlier) + pieces : -3]
+        scratch = refs[-3:]
+        if keep:
+            copy_through([a_ref], kept_outs, *scratch)
         for value, source in ((1, a_ref), (0, b_ref)):
 
             @pl.when(flag_ref[0] == value)
             def _(source=source):
-                for copy in copies(source):
-                    copy.start()
-                for copy in copies(source):
-                    copy.wait()
+                copy_through([source], outs, *scratch)
 
     return pl.pallas_call(
         kernel,
         in_specs=[pl.BlockSpec(memory_space=pltpu.SMEM)]
         + [pl.BlockSpec(memory_space=pl.ANY)] * (2 + len(earlier)),
-        out_specs=[pl.BlockSpec(memory_space=pl.ANY)] * pieces,
-        out_shape=[jax.ShapeDtypeStruct(shape, a.dtype) for shape in shapes],
-        scratch_shapes=[pltpu.SemaphoreType.DMA((pieces, CHUNKS))],
+        out_specs=[pl.BlockSpec(memory_space=pl.ANY)] * (pieces + len(kept)),
+        out_shape=[jax.ShapeDtypeStruct(shape, a.dtype) for shape in shapes + kept],
+        scratch_shapes=copy_scratch(rows, cols),
+        compiler_params=pltpu.CompilerParams(vmem_limit_bytes=VMEM),
         cost_estimate=pl.CostEstimate(flops=0, bytes_accessed=2 * a.size * a.dtype.itemsize, transcendentals=0),
     )(flag, a, b, *earlier)
 
@@ -315,7 +363,8 @@
         amps, refs = refs[:count], refs[count + len(earlier) :]
         source, refs = refs[: len(extra)], refs[len(extra) :]
         part_refs, out, refs = refs[: len(parts)], refs[len(parts)], refs[len(parts) + 1 :]
-        target, (left, right, left_sems, right_sems, copy_sems) = refs[: len(extra)], refs[len(extra) :]
+        target, refs = refs[: len(extra)], refs[len(extra) :]
+        (left, right, left_sems, right_sems), scratch = refs[:4], refs[4:]
         step = pl.program_id(0)
         slot = step % 2
 
@@ -353,8 +402,8 @@
             for copy in amp_copies():
                 copy.start()
             slab_copies(step, True)
-            for pair in zip(source, target):
-                for copy in in_chunks(*pair, copy_sems):
+            if extra:
+                for copy in copies_in(source, scratch[0], scratch[1]):
                     copy.start()
 
         @pl.when(step + 1 < steps)
@@ -379,10 +428,18 @@
             at += len(span)
         out[...] = total.astype(out.dtype)
 
-        @pl.when(step == steps - 1)
-        def _():
-            for pair in zip(source, target):
-                for copy in in_chunks(*pair, copy_sems):
+        if extra:
+
+            @pl.when(step == 1)
+            def _():
+                for copy in copies_in(source, scratch[0], scratch[1]):
+                    copy.wait()
+                for copy in copies_out(scratch[0], target, scratch[2]):
+                    copy.start()
+
+            @pl.when(step == steps - 1)
+            def _():
+                for copy in copies_out(scratch[0], target, scratch[2]):
                     copy.wait()
 
     def rows_of(start, end):
@@ -404,7 +461,7 @@
             pltpu.VMEM((cols, count * depth), jnp.bfloat16),
             pltpu.SemaphoreType.DMA((2, count)),
             pltpu.SemaphoreType.DMA((count,)),
-            pltpu.SemaphoreType.DMA((CHUNKS,)),
+            *(copy_scratch(*copied.shape) if extra else []),
         ],
         compiler_params=pltpu.CompilerParams(vmem_limit_bytes=VMEM),
         cost_estimate=pl.CostEstimate(
@@ -443,7 +500,7 @@
 
     plan = jnp.zeros((TAIL, vir_count), jnp.bfloat16)
     plan = plan.at[0, : ROUNDS + 1].set(pair_kept[:, 0].astype(jnp.bfloat16))
-    own = Slab(jnp.concatenate([three_index[0], plan]), list(range(blocks)))
+    own = Slab(append_call(three_index[0], plan), list(range(blocks)))
 
     r1 = moved(own, routes.rounds[0])
     own_far = Slab(sibling(own.array), own.ids, 1)
@@ -483,7 +540,7 @@
     all_ids += [r3_ids, routes.moved(r3_ids, routes.swap), r4_ids, r5_ids, routes.moved(r5_ids, routes.swap)]
     table = table_of(all_ids)
     near, far = 0, 1
-    rows_near = three_index[0].T
+    rows_near = own.array[:aux].T
     stacks = {}
 
     def amps(jobs, turned, *earlier):
@@ -500,21 +557,22 @@
 
     f32, bf16 = jnp.float32, jnp.bfloat16
     done = amps([(s, near) for s in (own, mate, r1, s1)], [rows_near], sent2.array)
-    mate_far = swapped(own_far)
-
-    sent3 = chosen(r2, own, done)
+
+    sent, kept = choice_call(flag, r2.array, own.array, [done], keep=True)
+    r2 = Slab(kept, r2.ids)
+    sent3 = Slab(sent, routes.either(r2.ids, own.ids))
     r3 = moved(sent3, routes.rounds[2])
     s2 = swapped(r2)
     rows_far = own_far.array[:aux].T
-    part = density([own, mate, r1, s1], near, [], f32, sent3.array)
+    part, again = density([own, mate, r1, s1], near, [], f32, sent3.array, copied=own_far.array)
+    mate_far = swapped(Slab(again, own.ids, 1))
     jobs = [(r1, far), (s1, far), (r2, near), (r2, far), (s2, far), (s2, near)]
-    jobs += [(own_far, near), (mate_far, near)]
     done = amps(jobs, [rows_near, rows_far], part)
 
     r3 = chosen(r3, r3, done)
     r4 = moved(r3, routes.rounds[3])
     s3 = swapped(r3)
-    jobs = [(r3, near), (r3, far), (s3, far), (s3, near)]
+    jobs = [(own_far, near), (mate_far, near), (r3, near), (r3, far), (s3, far), (s3, near)]
     done = amps(jobs, [rows_near, rows_far], done)
     slabs = [own_far, mate_far, r2, s2, r3, s3]
     part, again = density(slabs, near, [[part]], f32, done, copied=own.array)

time: 947 us -> 327 us (0.35)
  Pallas kernels: 820 us -> 199 us
  waiting for transfers between devices: 72.6 us -> 83.8 us
    pallas_call x5, Pallas kernels: 488 us -> 24.9 us  [choice_call(): pl.pallas_call(kernel, in_specs=[pl.BlockSpec(memory_space=pltpu.SMEM)] +...]
    pallas_call x6, Pallas kernels: 248 us -> 86.2 us  [density_call(): pl.pallas_call(kernel, grid=(steps,), in_specs=[pl.BlockSpec(memory_space...]
    ppermute x3, waiting for transfers between devices: 0.01 us -> 30.7 us  [sibling(): return lax.ppermute(array, 'narrow', [(0, 1), (1, 0)])]
    ppermute x17, waiting for transfers between devices: 72.6 us -> 53.2 us  [moved(): sent = [lax.ppermute(piece, 'wide', pairs) for piece in slab.pieces]]
  transfers between devices with their start and end apart: 20 -> 20, of which waited for: 3 -> 6; matrix products, arithmetic and copies ran while one was open for 1% -> 5% of each run, Pallas kernels for 75% -> 55%
where the time goes in v5:
time: 327 us; the launch traced here: 324 us
  Pallas kernels  199 us (61%)
  waiting for transfers between devices  83.8 us (26%)
  local copies, waits for them, and re-layouts  21.4 us (7%)
  starting transfers between devices  17 us (5%)
    pallas_call x6, Pallas kernels, density_call(): pl.pallas_call(kernel, grid=(steps,), in_specs=[pl.BlockSpec(memory_space...  86.2 us
    pallas_call x9, Pallas kernels, amplitude_call(): pl.pallas_call(kernel, grid=(len(jobs),), in_specs=[pl.BlockSpec(memory_s...  83.3 us
    ppermute x17, waiting for transfers between devices, moved(): sent = [lax.ppermute(piece, 'wide', pairs) for piece in slab.pieces]  53.2 us
    ppermute x3, waiting for transfers between devices, sibling(): return lax.ppermute(array, 'narrow', [(0, 1), (1, 0)])  30.7 us
    pallas_call x5, Pallas kernels, choice_call(): pl.pallas_call(kernel, in_specs=[pl.BlockSpec(memory_space=pltpu.SMEM)] +...  24.9 us
    ppermute x17, starting transfers between devices, moved(): sent = [lax.ppermute(piece, 'wide', pairs) for piece in slab.pieces]  13.2 us
    unnamed x23, local copies, waits for them, and re-layouts  10.7 us
  transfers between devices with their start and end apart: 20, of which 6 were waited for; matrix products, arithmetic and copies ran while one was open for 5% of the time, Pallas kernels for 55%

profile of v5, /device:TPU:3, one launch (start us, length us, event | category | flops | bytes accessed | tf_op | source)
XLA Modules:
  0.0 323.8 jit_solution(10366425780414320259)
XLA Ops:
  0.0 0.7 convert_bitcast_fusion
  1.3 3.7 %shard_map.73.a_ref.refs_0_.b_ref.refs_13_ = bf16[3088,512]{1,0:T(8,128)(2,1)} custom-call(bf16[3072,512]{1,0:T(8,128)(2,1)} %bitcast.30, bf16[16,512]{1,0:T(8,128)(2,1)} %scatter.4.tail_ref), custom_call_target="tpu_custom_call" | custom-call | tf_op jit(solution)/shard_map/pallas_call | solution.py:291
  5.1 2.2 collective-permute-start.2
  7.3 35.2 %collective-permute-done.b_ref.refs_2_.refs_0_ = bf16[3088,512]{1,0:T(8,128)(2,1)} collective-permute-done((bf16[3088,512]{1,0:T(8,128)(2,1)}, bf16[3088,512]{1,0:T(8,128)(2,1)}, u32[]{:S(2)}, u32[]{:S(2)}) %collective-permute-start) | collective-permute-done | bytes 3162144 | tf_op jit(solution)/shard_map/ppermute | solution.py:483
  42.6 2.8 collective-permute-start.1
  45.9 4.6 %shard_map.74.refs_5_ = bf16[3088,512]{1,0:T(8,128)(2,1)} custom-call(s32[1]{0:T(128)} %dynamic_slice.12.flag_ref, bf16[3088,512]{1,0:T(8,128)(2,1)} %shard_map.73.a_ref.refs_0_.b_ref.refs_13_, bf16[3088,512]{1,0:T(8,128)(2,1)} %collective-permute-done.b_ref.refs_2_.refs_0_, bf16[3088,512]{1,0:T(8,128)(2,1)} %collective-permute-done.2.refs_0_.refs_1_), custom_call_target="tpu_custom_call" | custom-call | bytes 6324224 | tf_op jit(solution)/shard_map/pallas_call | solution.py:319
  50.6 1.3 collective-permute-start.6
  52.1 0.7 fusion.2
  52.8 1.9 slice.27
  55.0 0.7 copy.47.scalars
  55.7 1.0 copy.48.refs_6_.refs_7_.refs_4_.refs_3_.refs_5_
  57.4 4.7 %copy.68 = bf16[3072,512]{0,1:T(8,128)(2,1)} copy(bf16[3072,512]{1,0:T(8,128)(2,1)} %slice.27) | data formatting | bytes 6291456
  62.0 12.2 %shard_map.75.refs_0_.refs_4_.refs_5_.refs_6_.refs_7_ = bf16[4,512,512]{2,1,0:T(8,128)(2,1)} custom-call(f32[11,3]{1,0:T(8,128)} %copy.47.scalars, bf16[3088,512]{1,0:T(8,128)(2,1)} %shard_map.73.a_ref.refs_0_.b_ref.refs_13_, bf16[3088,512]{1,0:T(8,128)(2,1)} %collective-permute-done.2.refs_0_.refs_1_, ...), custom_call_target="tpu_custom_call" | custom-call | flops 6442450944 | bytes 17825792 | tf_op jit(solution)/shard_map/pallas_call | solution.py:214
  74.3 14.7 %collective-permute-done.3.a_ref = bf16[3088,512]{1,0:T(8,128)(2,1)} collective-permute-done((bf16[3088,512]{1,0:T(8,128)(2,1)}, bf16[3088,512]{1,0:T(8,128)(2,1)}, u32[]{:S(2)}, u32[]{:S(2)}) %collective-permute-start.3) | collective-permute-done | bytes 3162144 | tf_op jit(solution)/shard_map/ppermute | solution.py:483
  89.0 7.7 %shard_map.76 = (bf16[3088,512]{1,0:T(8,128)(2,1)}, bf16[3088,512]{1,0:T(8,128)(2,1)}) custom-call(s32[1]{0:T(128)} %dynamic_slice.12.flag_ref, bf16[3088,512]{1,0:T(8,128)(2,1)} %collective-permute-done.3.a_ref, bf16[3088,512]{1,0:T(8,128)(2,1)} %shard_map.73.a_ref.refs_0_.b_ref.refs_13_, bf16[4,512,512]{2,1,0:T(8,128)(2,1)} %shard_map.75.refs_0_.refs_4_.refs_5_.refs_6_.refs_7_), custom_call_target="tpu_custom_call" | custom-call | bytes 6324224 | tf_op jit(solution)/shard_map/pallas_call | solution.py:319
  96.8 24.0 %collective-permute-done.6.refs_9_.refs_0_.refs_15_ = bf16[3088,512]{1,0:T(8,128)(2,1)} collective-permute-done((bf16[3088,512]{1,0:T(8,128)(2,1)S(1)}, bf16[3088,512]{1,0:T(8,128)(2,1)}, u32[]{:S(2)}, u32[]{:S(2)}) %collective-permute-start.6) | collective-permute-done | bytes 3162144 | tf_op jit(solution)/shard_map/ppermute | solution.py:499
  120.8 2.1 slice_bitcast_fusion
  122.9 3.1 copy.50.refs_5_.refs_2_
  126.0 15.2 %shard_map.77 = (f32[3072,512]{1,0:T(8,128)}, bf16[3088,512]{1,0:T(8,128)(2,1)}) custom-call(bf16[3088,512]{1,0:T(8,128)(2,1)} %shard_map.73.a_ref.refs_0_.b_ref.refs_13_, bf16[3088,512]{1,0:T(8,128)(2,1)} %collective-permute-done.2.refs_0_.refs_1_, bf16[3088,512]{1,0:T(8,128)(2,1)} %collective-permute-done.b_ref.refs_2_.refs_0_, ...), custom_call_target="tpu_custom_call" | custom-call | flops 6442450944 | bytes 20971520 | tf_op jit(solution)/shard_map/pallas_call | solution.py:450
  141.2 0.8 collective-permute-start.9
  142.1 16.1 %shard_map.78.refs_0_.refs_6_.refs_8_.refs_9_.refs_7_.refs_10_ = bf16[6,512,512]{2,1,0:T(8,128)(2,1)} custom-call(f32[11,3]{1,0:T(8,128)} %copy.47.scalars, bf16[3088,512]{1,0:T(8,128)(2,1)} %collective-permute-done.b_ref.refs_2_.refs_0_, bf16[3088,512]{1,0:T(8,128)(2,1)} %collective-permute-done.1.refs_3_.refs_1_, ...), custom_call_target="tpu_custom_call" | custom-call | flops 9663676416 | bytes 22020096 | tf_op jit(solution)/shard_map/pallas_call | solution.py:214
  158.2 4.2 %shard_map.79.refs_2_.refs_4_ = bf16[3088,512]{1,0:T(8,128)(2,1)} custom-call(s32[1]{0:T(128)} %dynamic_slice.12.flag_ref, bf16[3088,512]{1,0:T(8,128)(2,1)} %collective-permute-done.5.a_ref.b_ref, bf16[3088,512]{1,0:T(8,128)(2,1)} %collective-permute-done.5.a_ref.b_ref, bf16[6,512,512]{2,1,0:T(8,128)(2,1)} %shard_map.78.refs_0_.refs_6_.refs_8_.refs_9_.refs_7_.refs_10_), custom_call_target="tpu_custom_call" | custom-call | bytes 6324224 | tf_op jit(solution)/shard_map/pallas_call | solution.py:319
  162.5 2.6 collective-permute-start.8
  165.1 3.2 collective-permute-done.7.refs_3_.refs_5_
  168.3 1.7 copy-done.2
  170.0 16.1 %shard_map.80.refs_6_.refs_7_.refs_10_.refs_11_.refs_12_ = bf16[6,512,512]{2,1,0:T(8,128)(2,1)} custom-call(f32[11,3]{1,0:T(8,128)} %copy.47.scalars, bf16[3088,512]{1,0:T(8,128)(2,1)} %collective-permute-done.6.refs_9_.refs_0_.refs_15_, bf16[3088,512]{1,0:T(8,128)(2,1)} %collective-permute-done.9.refs_1_, bf16[3088,512]{1,0:T(8,128)(2,1)} %shard_map.79.refs_2_.refs_4_, ...), custom_call_target="tpu_custom_call" | custom-call | flops 9663676416 | bytes 22020096 | tf_op jit(solution)/shard_map/pallas_call | solution.py:214
  186.1 21.2 %shard_map.81 = (f32[3072,512]{1,0:T(8,128)}, bf16[3088,512]{1,0:T(8,128)(2,1)}) custom-call(bf16[3088,512]{1,0:T(8,128)(2,1)} %collective-permute-done.6.refs_9_.refs_0_.refs_15_, bf16[3088,512]{1,0:T(8,128)(2,1)} %collective-permute-done.9.refs_1_, bf16[3088,512]{1,0:T(8,128)(2,1)} %get-tuple-element.31.refs_2_, ...), custom_call_target="tpu_custom_call" | custom-call | flops 9663676416 | bytes 34603008 | tf_op jit(solution)/shard_map/pallas_call | solution.py:450
  207.4 2.3 collective-permute-start.11
  209.7 1.7 copy-done.1
  211.4 6.4 %shard_map.82.refs_13_.refs_14_ = bf16[1,512,512]{2,1,0:T(8,128)(2,1)} custom-call(f32[11,3]{1,0:T(8,128)} %copy.47.scalars, bf16[3088,512]{1,0:T(8,128)(2,1)} %copy-done.1, bf16[512,3072]{1,0:T(8,128)(2,1)} %bitcast.24, bf16[512,3072]{1,0:T(8,128)(2,1)} %copy.50.refs_5_.refs_2_, f32[3072,512]{1,0:T(8,128)} %get-tuple-element.35.refs_3_.refs_11_, ...), custom_call_target="tpu_custom_call" | custom-call | flops 1610612736 | bytes 9961472 | tf_op jit(solution)/shard_map/pallas_call | solution.py:214
  217.8 12.7 %shard_map.83 = (bf16[1536,512]{1,0:T(8,128)(2,1)}, bf16[3088,512]{1,0:T(8,128)(2,1)}) custom-call(bf16[3088,512]{1,0:T(8,128)(2,1)} %collective-permute-done.b_ref.refs_2_.refs_0_, bf16[3088,512]{1,0:T(8,128)(2,1)} %collective-permute-done.1.refs_3_.refs_1_, bf16[3088,512]{1,0:T(8,128)(2,1)} %get-tuple-element.31.refs_2_, ...), custom_call_target="tpu_custom_call" | custom-call | flops 5637144576 | bytes 16252928 | tf_op jit(solution)/shard_map/pallas_call | solution.py:450
  230.8 1.3 collective-permute-start.15
  232.1 11.5 %shard_map.84.refs_2_ = bf16[1536,512]{1,0:T(8,128)(2,1)} custom-call(bf16[3088,512]{1,0:T(8,128)(2,1)} %collective-permute-done.b_ref.refs_2_.refs_0_, bf16[3088,512]{1,0:T(8,128)(2,1)} %collective-permute-done.1.refs_3_.refs_1_, bf16[3088,512]{1,0:T(8,128)(2,1)} %get-tuple-element.31.refs_2_, bf16[3088,512]{1,0:T(8,128)(2,1)} %collective-permute-done.4.refs_3_, ...), custom_call_target="tpu_custom_call" | custom-call | flops 5637144576 | bytes 16252928 | tf_op jit(solution)/shard_map/pallas_call | solution.py:450
  243.6 6.4 %shard_map.85.refs_0_.refs_7_ = bf16[1,512,512]{2,1,0:T(8,128)(2,1)} custom-call(f32[11,3]{1,0:T(8,128)} %copy.47.scalars, bf16[3088,512]{1,0:T(8,128)(2,1)} %copy-done.1, bf16[512,3072]{1,0:T(8,128)(2,1)} %bitcast.25, bf16[1536,512]{1,0:T(8,128)(2,1)} %shard_map.84.refs_2_, f32[2,512,1]{2,1,0:T(8,128)} %copy.48.refs_6_.refs_7_.refs_4_.refs_3_.refs_5_, ...), custom_call_target="tpu_custom_call" | custom-call | flops 1610612736 | bytes 6815744 | tf_op jit(solution)/shard_map/pallas_call | solution.py:214
  250.1 1.8 copy-done.3
  251.8 4.2 %shard_map.86 = (bf16[1024,512]{1,0:T(8,128)(2,1)}, bf16[1024,512]{1,0:T(8,128)(2,1)}, bf16[1040,512]{1,0:T(8,128)(2,1)}) custom-call(s32[1]{0:T(128)} %dynamic_slice.12.flag_ref, bf16[3088,512]{1,0:T(8,128)(2,1)} %copy-done.3, bf16[3088,512]{1,0:T(8,128)(2,1)} %copy-done.3, bf16[1,512,512]{2,1,0:T(8,128)(2,1)} %shard_map.85.refs_0_.refs_7_), custom_call_target="tpu_custom_call" | custom-call | bytes 6324224 | tf_op jit(solution)/shard_map/pallas_call | solution.py:319
  256.7 6.6 %shard_map.87.refs_1_.refs_8_ = bf16[1,512,512]{2,1,0:T(8,128)(2,1)} custom-call(f32[11,3]{1,0:T(8,128)} %copy.47.scalars, bf16[1024,512]{1,0:T(8,128)(2,1)} %get-tuple-element.39.refs_0_.refs_4_.refs_1_, bf16[1024,512]{1,0:T(8,128)(2,1)} %get-tuple-element.40.refs_1_.refs_2_, bf16[1040,512]{1,0:T(8,128)(2,1)} %get-tuple-element.41.refs_2_.refs_3_, ...), custom_call_target="tpu_custom_call" | custom-call | flops 1610612736 | bytes 6815744 | tf_op jit(solution)/shard_map/pallas_call | solution.py:214
  263.3 4.3 %collective-permute-done.15.refs_0_.refs_10_ = bf16[1536,512]{1,0:T(8,128)(2,1)S(1)} collective-permute-done((bf16[1536,512]{1,0:T(8,128)(2,1)}, bf16[1536,512]{1,0:T(8,128)(2,1)S(1)}, u32[]{:S(2)}, u32[]{:S(2)}) %collective-permute-start.15) | collective-permute-done | bytes 1572896 | tf_op jit(solution)/shard_map/ppermute | solution.py:499
  267.6 1.2 collective-permute-start.19
  269.4 6.5 %shard_map.89.refs_9_.refs_10_ = bf16[1,512,512]{2,1,0:T(8,128)(2,1)} custom-call(f32[11,3]{1,0:T(8,128)} %copy.47.scalars, bf16[1024,512]{1,0:T(8,128)(2,1)} %collective-permute-done.12.refs_0_.refs_4_, bf16[1024,512]{1,0:T(8,128)(2,1)} %collective-permute-done.13.refs_1_.refs_5_, bf16[1040,512]{1,0:T(8,128)(2,1)} %collective-permute-done.14.refs_2_.refs_6_, ...), custom_call_target="tpu_custom_call" | custom-call | flops 1610612736 | bytes 6815744 | tf_op jit(solution)/shard_map/pallas_call | solution.py:214
  275.9 13.3 %shard_map.90.refs_0_.refs_9_ = f32[3072,512]{1,0:T(8,128)} custom-call(bf16[3088,512]{1,0:T(8,128)(2,1)} %copy-done.1, bf16[1024,512]{1,0:T(8,128)(2,1)} %get-tuple-element.39.refs_0_.refs_4_.refs_1_, bf16[1024,512]{1,0:T(8,128)(2,1)} %get-tuple-element.40.refs_1_.refs_2_, bf16[1040,512]{1,0:T(8,128)(2,1)} %get-tuple-element.41.refs_2_.refs_3_, ...), custom_call_target="tpu_custom_call" | custom-call | flops 4831838208 | bytes 23592960 | tf_op jit(solution)/shard_map/pallas_call | solution.py:450
  289.2 4.2 %shard_map.91 = (bf16[1024,512]{1,0:T(8,128)(2,1)}, bf16[1024,512]{1,0:T(8,128)(2,1)}, bf16[1040,512]{1,0:T(8,128)(2,1)}) custom-call(s32[1]{0:T(128)} %dynamic_slice.12.flag_ref, bf16[3088,512]{1,0:T(8,128)(2,1)} %collective-permute-done.10.a_ref.b_ref, bf16[3088,512]{1,0:T(8,128)(2,1)} %collective-permute-done.10.a_ref.b_ref, ...), custom_call_target="tpu_custom_call" | custom-call | bytes 6324224 | tf_op jit(solution)/shard_map/pallas_call | solution.py:319
  293.4 0.6 collective-permute-start.18
  294.6 6.5 %shard_map.92.refs_1_.refs_6_ = bf16[1,512,512]{2,1,0:T(8,128)(2,1)} custom-call(f32[11,3]{1,0:T(8,128)} %copy.47.scalars, bf16[1024,512]{1,0:T(8,128)(2,1)} %get-tuple-element.42.refs_0_.refs_4_, bf16[1024,512]{1,0:T(8,128)(2,1)} %get-tuple-element.43.refs_1_, bf16[1040,512]{1,0:T(8,128)(2,1)} %get-tuple-element.44.refs_2_, bf16[512,3072]{1,0:T(8,128)(2,1)} %bitcast.28, ...), custom_call_target="tpu_custom_call" | custom-call | flops 1610612736 | bytes 6815744 | tf_op jit(solution)/shard_map/pallas_call | solution.py:214
  301.0 2.4 collective-permute-done.19.refs_0_.refs_11_
  304.0 1.0 copy-done.6
  305.0 6.5 %shard_map.94.refs_7_.refs_8_ = bf16[1,512,512]{2,1,0:T(8,128)(2,1)} custom-call(f32[11,3]{1,0:T(8,128)} %copy.47.scalars, bf16[1024,512]{1,0:T(8,128)(2,1)} %collective-permute-done.16.refs_0_.refs_3_, bf16[1024,512]{1,0:T(8,128)(2,1)} %collective-permute-done.17.refs_1_.refs_4_, bf16[1040,512]{1,0:T(8,128)(2,1)} %copy-done.6, bf16[512,3072]{1,0:T(8,128)(2,1)} %bitcast.29, ...), custom_call_target="tpu_custom_call" | custom-call | flops 1610612736 | bytes 6815744 | tf_op jit(solution)/shard_map/pallas_call | solution.py:214
  311.5 12.2 %shard_map.95 = f32[3072,512]{1,0:T(8,128)} custom-call(bf16[1024,512]{1,0:T(8,128)(2,1)} %get-tuple-element.42.refs_0_.refs_4_, bf16[1024,512]{1,0:T(8,128)(2,1)} %get-tuple-element.43.refs_1_, bf16[1040,512]{1,0:T(8,128)(2,1)} %get-tuple-element.44.refs_2_, bf16[1024,512]{1,0:T(8,128)(2,1)} %collective-permute-done.16.refs_0_.refs_3_, ...), custom_call_target="tpu_custom_call" | custom-call | flops 3221225472 | bytes 26214400 | tf_op jit(solution)/shard_map/pallas_call | solution.py:450
  (55 shorter events, 5.4 us)
Async XLA Ops:
  1.3 44.0 %copy-start.10 = (s32[16]{0:T(128)S(1)}, s32[16]{0:T(128)}, u32[]{:S(2)}) copy-start(s32[16]{0:T(128)} %constant.51.clone) | copy-start | bytes 196
  5.0 37.5 %collective-permute-start = (bf16[3088,512]{1,0:T(8,128)(2,1)}, bf16[3088,512]{1,0:T(8,128)(2,1)}, u32[]{:S(2)}, u32[]{:S(2)}) collective-permute-start(bf16[3088,512]{1,0:T(8,128)(2,1)} %shard_map.73.a_ref.refs_0_.b_ref.refs_13_), channel_id=1, source_target_pairs={{0,6},{2,26},{4,12},{6,0},{8,14},{10,2},{12,20},{14,8},{16,22},{18... | collective-permute-start | bytes 9486344 | tf_op jit(solution)/shard_map/ppermute | solution.py:483
  5.1 40.8 %collective-permute-start.2 = (bf16[3088,512]{1,0:T(8,128)(2,1)}, bf16[3088,512]{1,0:T(8,128)(2,1)}, u32[]{:S(2)}, u32[]{:S(2)}) collective-permute-start(bf16[3088,512]{1,0:T(8,128)(2,1)} %shard_map.73.a_ref.refs_0_.b_ref.refs_13_), channel_id=1, source_target_pairs={{0,2},{2,0},{4,6},{6,4},{8,10},{10,8},{12,14},{14,12},{16,18},{18,... | collective-permute-start | bytes 9486344 | tf_op jit(solution)/shard_map/ppermute | solution.py:483
  42.6 19.5 %collective-permute-start.1 = (bf16[3088,512]{1,0:T(8,128)(2,1)}, bf16[3088,512]{1,0:T(8,128)(2,1)}, u32[]{:S(2)}, u32[]{:S(2)}) collective-permute-start(bf16[3088,512]{1,0:T(8,128)(2,1)} %collective-permute-done.b_ref.refs_2_.refs_0_), channel_id=1, source_target_pairs={{0,2},{2,0},{4,6},{6,4},{8,10},{10,8},{12,14},{14,12},{16,18},{18,... | collective-permute-start | bytes 9486344 | tf_op jit(solution)/shard_map/ppermute | solution.py:483
  45.9 4.7 %copy-start = (bf16[3088,512]{1,0:T(8,128)(2,1)S(1)}, bf16[3088,512]{1,0:T(8,128)(2,1)}, u32[]{:S(2)}) copy-start(bf16[3088,512]{1,0:T(8,128)(2,1)} %shard_map.73.a_ref.refs_0_.b_ref.refs_13_) | copy-start | bytes 9486340
  45.9 6.0 %copy-start.8 = (f32[16]{0:T(128)S(1)}, f32[16]{0:T(128)}, u32[]{:S(2)}) copy-start(f32[16]{0:T(128)} %param.11) | copy-start | bytes 196
  45.9 6.0 %copy-start.9 = (s32[16]{0:T(128)S(1)}, s32[16]{0:T(128)}, u32[]{:S(2)}) copy-start(s32[16]{0:T(128)} %param.10) | copy-start | bytes 196
  50.5 38.5 %collective-permute-start.3 = (bf16[3088,512]{1,0:T(8,128)(2,1)}, bf16[3088,512]{1,0:T(8,128)(2,1)}, u32[]{:S(2)}, u32[]{:S(2)}) collective-permute-start(bf16[3088,512]{1,0:T(8,128)(2,1)} %shard_map.74.refs_5_), channel_id=1, source_target_pairs={{0,24},{2,4},{4,2},{6,14},{8,0},{10,12},{12,10},{14,22},{16,8},{18... | collective-permute-start | bytes 9486344 | tf_op jit(solution)/shard_map/ppermute | solution.py:483
  50.6 70.3 %collective-permute-start.6 = (bf16[3088,512]{1,0:T(8,128)(2,1)S(1)}, bf16[3088,512]{1,0:T(8,128)(2,1)}, u32[]{:S(2)}, u32[]{:S(2)}) collective-permute-start(bf16[3088,512]{1,0:T(8,128)(2,1)S(1)} %copy-done), channel_id=1, source_target_pairs={{0,1},{1,0},{2,3},{3,2},{4,5},{5,4},{6,7},{7,6},{8,9},{9,8},{10,11... | collective-permute-start | bytes 9486344 | tf_op jit(solution)/shard_map/ppermute | solution.py:499
  52.8 2.8 copy-start.7
  96.7 45.4 %collective-permute-start.4 = (bf16[3088,512]{1,0:T(8,128)(2,1)}, bf16[3088,512]{1,0:T(8,128)(2,1)}, u32[]{:S(2)}, u32[]{:S(2)}) collective-permute-start(bf16[3088,512]{1,0:T(8,128)(2,1)} %get-tuple-element.31.refs_2_), channel_id=1, source_target_pairs={{0,2},{2,0},{4,6},{6,4},{8,10},{10,8},{12,14},{14,12},{16,18},{18,... | collective-permute-start | bytes 9486344 | tf_op jit(solution)/shard_map/ppermute | solution.py:483
  96.7 61.4 %collective-permute-start.5 = (bf16[3088,512]{1,0:T(8,128)(2,1)}, bf16[3088,512]{1,0:T(8,128)(2,1)}, u32[]{:S(2)}, u32[]{:S(2)}) collective-permute-start(bf16[3088,512]{1,0:T(8,128)(2,1)} %get-tuple-element.32.refs_8_), channel_id=1, source_target_pairs={{0,6},{2,10},{4,28},{6,0},{8,14},{10,18},{12,4},{14,8},{16,22},{18... | collective-permute-start | bytes 9486344 | tf_op jit(solution)/shard_map/ppermute | solution.py:483
  141.2 23.9 %collective-permute-start.9 = (bf16[3088,512]{1,0:T(8,128)(2,1)}, bf16[3088,512]{1,0:T(8,128)(2,1)}, u32[]{:S(2)}, u32[]{:S(2)}) collective-permute-start(bf16[3088,512]{1,0:T(8,128)(2,1)} %get-tuple-element.34), channel_id=1, source_target_pairs={{0,2},{2,0},{4,6},{6,4},{8,10},{10,8},{12,14},{14,12},{16,18},{18,... | collective-permute-start | bytes 9486344 | tf_op jit(solution)/shard_map/ppermute | solution.py:483
  162.4 6.0 %collective-permute-start.7 = (bf16[3088,512]{1,0:T(8,128)(2,1)}, bf16[3088,512]{1,0:T(8,128)(2,1)S(1)}, u32[]{:S(2)}, u32[]{:S(2)}) collective-permute-start(bf16[3088,512]{1,0:T(8,128)(2,1)} %shard_map.79.refs_2_.refs_4_), channel_id=1, source_target_pairs={{0,2},{2,0},{4,6},{6,4},{8,10},{10,8},{12,14},{14,12},{16,18},{18,... | collective-permute-start | bytes 9486344 | tf_op jit(solution)/shard_map/ppermute | solution.py:483
  162.5 47.2 %collective-permute-start.8 = (bf16[3088,512]{1,0:T(8,128)(2,1)}, bf16[3088,512]{1,0:T(8,128)(2,1)S(1)}, u32[]{:S(2)}, u32[]{:S(2)}) collective-permute-start(bf16[3088,512]{1,0:T(8,128)(2,1)} %shard_map.79.refs_2_.refs_4_), channel_id=1, source_target_pairs={{0,8},{2,4},{4,2},{6,30},{8,16},{10,12},{12,10},{14,6},{16,24},{18... | collective-permute-start | bytes 9486344 | tf_op jit(solution)/shard_map/ppermute | solution.py:483
  168.3 1.7 copy-start.2
  207.4 42.7 %collective-permute-start.11 = (bf16[3088,512]{1,0:T(8,128)(2,1)}, bf16[3088,512]{1,0:T(8,128)(2,1)S(1)}, u32[]{:S(2)}, u32[]{:S(2)}) collective-permute-start(bf16[3088,512]{1,0:T(8,128)(2,1)} %get-tuple-element.37), channel_id=1, source_target_pairs={{0,8},{2,4},{4,2},{6,30},{8,16},{10,12},{12,10},{14,6},{16,24},{18... | collective-permute-start | bytes 9486344 | tf_op jit(solution)/shard_map/ppermute | solution.py:483
  209.7 1.7 copy-start.1
  230.5 58.7 %collective-permute-start.10 = (bf16[3088,512]{1,0:T(8,128)(2,1)}, bf16[3088,512]{1,0:T(8,128)(2,1)}, u32[]{:S(2)}, u32[]{:S(2)}) collective-permute-start(bf16[3088,512]{1,0:T(8,128)(2,1)} %get-tuple-element.36), channel_id=1, source_target_pairs={{0,8},{2,4},{4,2},{6,30},{8,16},{10,12},{12,10},{14,6},{16,24},{18... | collective-permute-start | bytes 9486344 | tf_op jit(solution)/shard_map/ppermute | solution.py:483
  230.8 36.8 %collective-permute-start.15 = (bf16[1536,512]{1,0:T(8,128)(2,1)}, bf16[1536,512]{1,0:T(8,128)(2,1)S(1)}, u32[]{:S(2)}, u32[]{:S(2)}) collective-permute-start(bf16[1536,512]{1,0:T(8,128)(2,1)} %get-tuple-element.38.refs_14_), channel_id=1, source_target_pairs={{0,1},{1,0},{2,3},{3,2},{4,5},{5,4},{6,7},{7,6},{8,9},{9,8},{10,11... | collective-permute-start | bytes 4718600 | tf_op jit(solution)/shard_map/ppermute | solution.py:499
  250.0 1.8 copy-start.3
  256.0 13.4 %collective-permute-start.14 = (bf16[1040,512]{1,0:T(8,128)(2,1)}, bf16[1040,512]{1,0:T(8,128)(2,1)}, u32[]{:S(2)}, u32[]{:S(2)}) collective-permute-start(bf16[1040,512]{1,0:T(8,128)(2,1)} %get-tuple-element.41.refs_2_.refs_3_), channel_id=1, source_target_pairs={{0,2},{2,0},{4,6},{6,4},{8,10},{10,8},{12,14},{14,12},{16,18},{18,... | collective-permute-start | bytes 3194888 | tf_op jit(solution)/shard_map/ppermute | solution.py:483
  256.1 13.3 %collective-permute-start.12 = (bf16[1024,512]{1,0:T(8,128)(2,1)}, bf16[1024,512]{1,0:T(8,128)(2,1)}, u32[]{:S(2)}, u32[]{:S(2)}) collective-permute-start(bf16[1024,512]{1,0:T(8,128)(2,1)} %get-tuple-element.39.refs_0_.refs_4_.refs_1_), channel_id=1, source_target_pairs={{0,2},{2,0},{4,6},{6,4},{8,10},{10,8},{12,14},{14,12},{16,18},{18,... | collective-permute-start | bytes 3145736 | tf_op jit(solution)/shard_map/ppermute | solution.py:483
  256.6 11.0 %copy-start.4 = (bf16[1536,512]{1,0:T(8,128)(2,1)S(1)}, bf16[1536,512]{1,0:T(8,128)(2,1)}, u32[]{:S(2)}) copy-start(bf16[1536,512]{1,0:T(8,128)(2,1)} %shard_map.84.refs_2_) | copy-start | bytes 4718596
  256.6 12.8 %collective-permute-start.13 = (bf16[1024,512]{1,0:T(8,128)(2,1)}, bf16[1024,512]{1,0:T(8,128)(2,1)}, u32[]{:S(2)}, u32[]{:S(2)}) collective-permute-start(bf16[1024,512]{1,0:T(8,128)(2,1)} %get-tuple-element.40.refs_1_.refs_2_), channel_id=1, source_target_pairs={{0,2},{2,0},{4,6},{6,4},{8,10},{10,8},{12,14},{14,12},{16,18},{18,... | collective-permute-start | bytes 3145736 | tf_op jit(solution)/shard_map/ppermute | solution.py:483
  267.6 1.2 copy-start.5
  267.6 35.8 %collective-permute-start.19 = (bf16[1536,512]{1,0:T(8,128)(2,1)S(1)}, bf16[1536,512]{1,0:T(8,128)(2,1)}, u32[]{:S(2)}, u32[]{:S(2)}) collective-permute-start(bf16[1536,512]{1,0:T(8,128)(2,1)S(1)} %copy-done.4), channel_id=1, source_target_pairs={{0,1},{1,0},{2,3},{3,2},{4,5},{5,4},{6,7},{7,6},{8,9},{9,8},{10,11... | collective-permute-start | bytes 4718600 | tf_op jit(solution)/shard_map/ppermute | solution.py:499
  293.4 10.6 %collective-permute-start.18 = (bf16[1040,512]{1,0:T(8,128)(2,1)}, bf16[1040,512]{1,0:T(8,128)(2,1)S(1)}, u32[]{:S(2)}, u32[]{:S(2)}) collective-permute-start(bf16[1040,512]{1,0:T(8,128)(2,1)} %get-tuple-element.44.refs_2_), channel_id=1, source_target_pairs={{0,2},{2,0},{4,6},{6,4},{8,10},{10,8},{12,14},{14,12},{16,18},{18,... | collective-permute-start | bytes 3194888 | tf_op jit(solution)/shard_map/ppermute | solution.py:483
  294.1 10.0 %collective-permute-start.16 = (bf16[1024,512]{1,0:T(8,128)(2,1)}, bf16[1024,512]{1,0:T(8,128)(2,1)}, u32[]{:S(2)}, u32[]{:S(2)}) collective-permute-start(bf16[1024,512]{1,0:T(8,128)(2,1)} %get-tuple-element.42.refs_0_.refs_4_), channel_id=1, source_target_pairs={{0,2},{2,0},{4,6},{6,4},{8,10},{10,8},{12,14},{14,12},{16,18},{18,... | collective-permute-start | bytes 3145736 | tf_op jit(solution)/shard_map/ppermute | solution.py:483
  294.1 9.9 %collective-permute-start.17 = (bf16[1024,512]{1,0:T(8,128)(2,1)}, bf16[1024,512]{1,0:T(8,128)(2,1)}, u32[]{:S(2)}, u32[]{:S(2)}) collective-permute-start(bf16[1024,512]{1,0:T(8,128)(2,1)} %get-tuple-element.43.refs_1_), channel_id=1, source_target_pairs={{0,2},{2,0},{4,6},{6,4},{8,10},{10,8},{12,14},{14,12},{16,18},{18,... | collective-permute-start | bytes 3145736 | tf_op jit(solution)/shard_map/ppermute | solution.py:483
  304.0 1.0 copy-start.6

commit v6 on v5

--- a/solution.py
+++ b/solution.py
@@ -9,6 +9,7 @@
 ROUNDS = 5
 TAIL = 16
 CHUNK = 512
+PIECES = 3
 VMEM = 56 * 1024 * 1024
 
 
@@ -273,19 +274,29 @@
 
 
 def copy_through(sources, targets, held, in_sems, out_sems):
-    for copy in copies_in(sources, held, in_sems):
-        copy.start()
-    for copy in copies_in(sources, held, in_sems):
-        copy.wait()
-    for copy in copies_out(held, targets, out_sems):
-        copy.start()
-    for copy in copies_out(held, targets, out_sems):
-        copy.wait()
+    if [x.shape[0] for x in sources] != [x.shape[0] for x in targets]:
+        loads, stores = [list(copies_in(sources, held, in_sems))], [list(copies_out(held, targets, out_sems))]
+    else:
+        loads = [[copy] for copy in copies_in(sources, held, in_sems)]
+        stores = [[copy] for copy in copies_out(held, targets, out_sems)]
+    for copies in loads:
+        for copy in copies:
+            copy.start()
+    for before, behind in zip(loads, stores):
+        for copy in before:
+            copy.wait()
+        for copy in behind:
+            copy.start()
+    for copies in stores:
+        for copy in copies:
+            copy.wait()
 
 
 def append_call(array, tail):
     def kernel(array_ref, tail_ref, out, held, in_sems, out_sems):
-        copy_through([array_ref, tail_ref], [out], held, in_sems, out_sems)
+        rows = array_ref.shape[0]
+        targets = [out.at[pl.ds(0, rows)], out.at[pl.ds(rows, tail_ref.shape[0])]]
+        copy_through([array_ref, tail_ref], targets, held, in_sems, out_sems)
 
     rows, cols = array.shape[0] + tail.shape[0], array.shape[1]
     return pl.pallas_call(
@@ -306,15 +317,45 @@
     kept = [(rows, cols)] if keep else []
 
     def kernel(flag_ref, a_ref, b_ref, *refs):
-        outs, kept_outs = refs[len(earlier) :][:pieces], refs[len(earlier) + pieces : -3]
-        scratch = refs[-3:]
+        refs = refs[len(earlier) :]
+        outs, kept_outs, scratch = refs[:pieces], refs[pieces : pieces + len(kept)], refs[pieces + len(kept) :]
         if keep:
-            copy_through([a_ref], kept_outs, *scratch)
-        for value, source in ((1, a_ref), (0, b_ref)):
-
-            @pl.when(flag_ref[0] == value)
-            def _(source=source):
-                copy_through([source], outs, *scratch)
+            held, loads, stores, other_held, other_loads, other_stores = scratch
+            leads = flag_ref[0] == 1
+            ours = list(copies_in([a_ref], held, loads))
+            theirs = list(copies_in([b_ref], other_held, other_loads))
+            kept_copies = list(copies_out(held, kept_outs, stores))
+            ours_out = list(copies_out(held, outs, other_stores))
+            theirs_out = list(copies_out(other_held, outs, other_stores))
+            for copy in ours:
+                copy.start()
+
+            @pl.when(jnp.logical_not(leads))
+            def _():
+                for copy in theirs:
+                    copy.start()
+
+            for load, store, also in zip(ours, kept_copies, ours_out):
+                load.wait()
+                store.start()
+                pl.when(leads)(also.start)
+
+            @pl.when(jnp.logical_not(leads))
+            def _():
+                for load, store in zip(theirs, theirs_out):
+                    load.wait()
+                    store.start()
+
+            for store, also in zip(kept_copies, ours_out):
+                store.wait()
+                also.wait()
+        else:
+            for value, source in ((1, a_ref), (0, b_ref)):
+
+                @pl.when(flag_ref[0] == value)
+                def _(source=source):
+                    parts = [source.at[pl.ds(at, out.shape[0])] for at, out in zip(begins, outs)]
+                    copy_through(parts, outs, *scratch)
 
     return pl.pallas_call(
         kernel,
@@ -322,7 +363,7 @@
         + [pl.BlockSpec(memory_space=pl.ANY)] * (2 + len(earlier)),
         out_specs=[pl.BlockSpec(memory_space=pl.ANY)] * (pieces + len(kept)),
         out_shape=[jax.ShapeDtypeStruct(shape, a.dtype) for shape in shapes + kept],
-        scratch_shapes=copy_scratch(rows, cols),
+        scratch_shapes=copy_scratch(rows, cols) * (1 + len(kept)),
         compiler_params=pltpu.CompilerParams(vmem_limit_bytes=VMEM),
         cost_estimate=pl.CostEstimate(flops=0, bytes_accessed=2 * a.size * a.dtype.itemsize, transcendentals=0),
     )(flag, a, b, *earlier)
@@ -342,10 +383,11 @@
 
 def density_call(terms, parts, out_dtype, aux, earlier, rows=None, copied=None):
     count = len(terms)
-    extra = [] if copied is None else [copied]
+    depth = terms[0][0].array.shape[1]
+    extra = list(copied or [])
+    whole = [jax.ShapeDtypeStruct((sum(x.shape[0] for x in extra), depth), jnp.bfloat16)] if extra else []
     pieces = [len(t[0].pieces) for t in terms]
     begins = [sum(pieces[:s]) for s in range(count)]
-    depth = terms[0][0].array.shape[1]
     cols = depth
     begin, length = rows or (0, aux)
     tile = 512
@@ -355,7 +397,8 @@
     spans = []
     for part in parts:
         ends = np.cumsum([piece.shape[0] // tile for piece in part])
-        spans.append([(int(end) - piece.shape[0] // tile, int(end)) for end, piece in zip(ends, part)])
+        shift = begin // tile if ends[-1] == aux // tile else 0
+        spans.append([(int(end) - piece.shape[0] // tile - shift, int(end) - shift) for end, piece in zip(ends, part)])
     parts = [p for part in parts for p in part]
 
     def kernel(*refs):
@@ -363,7 +406,7 @@
         amps, refs = refs[:count], refs[count + len(earlier) :]
         source, refs = refs[: len(extra)], refs[len(extra) :]
         part_refs, out, refs = refs[: len(parts)], refs[len(parts)], refs[len(parts) + 1 :]
-        target, refs = refs[: len(extra)], refs[len(extra) :]
+        target, refs = refs[: len(whole)], refs[len(whole) :]
         (left, right, left_sems, right_sems), scratch = refs[:4], refs[4:]
         step = pl.program_id(0)
         slot = step % 2
@@ -453,15 +496,15 @@
         in_specs=[pl.BlockSpec(memory_space=pl.ANY)] * (sum(pieces) + count + len(earlier) + len(extra))
         + [rows_of(*ends) for span in spans for ends in span],
         out_specs=[pl.BlockSpec((tile, cols), lambda i: (i, 0))]
-        + [pl.BlockSpec(memory_space=pl.ANY)] * len(extra),
+        + [pl.BlockSpec(memory_space=pl.ANY)] * len(whole),
         out_shape=[jax.ShapeDtypeStruct((length, cols), out_dtype)]
-        + [jax.ShapeDtypeStruct(x.shape, x.dtype) for x in extra],
+        + whole,
         scratch_shapes=[
             pltpu.VMEM((2, tile, count * depth), jnp.bfloat16),
             pltpu.VMEM((cols, count * depth), jnp.bfloat16),
             pltpu.SemaphoreType.DMA((2, count)),
             pltpu.SemaphoreType.DMA((count,)),
-            *(copy_scratch(*copied.shape) if extra else []),
+            *(copy_scratch(*whole[0].shape) if extra else []),
         ],
         compiler_params=pltpu.CompilerParams(vmem_limit_bytes=VMEM),
         cost_estimate=pl.CostEstimate(
@@ -503,11 +546,9 @@
     own = Slab(append_call(three_index[0], plan), list(range(blocks)))
 
     r1 = moved(own, routes.rounds[0])
-    own_far = Slab(sibling(own.array), own.ids, 1)
+    split = choice_call(flag, own.array, own.array, [], pieces=2)
+    own_far = Slab([sibling(piece) for piece in split], own.ids, 1)
     mate = swapped(own)
-    s1 = swapped(r1)
-    sent2 = chosen(own, r1, mate.array)
-    r2 = moved(sent2, routes.rounds[1])
 
     labels = jnp.arange(occ_energy.shape[0], dtype=jnp.int32)
     picked = orbital_map[:, None] == labels[None, :]
@@ -533,11 +574,19 @@
     )
     vir_rows, vir_cols = vir[:, :, None], vir[:, None, :]
 
-    r3_ids = routes.moved(routes.either(r2.ids, own.ids), routes.rounds[2])
+    def moved_ids(ids_lead, ids_other, pairs):
+        return routes.moved(routes.either(ids_lead, ids_other), pairs)
+
+    def swapped_ids(ids):
+        return routes.moved(ids, routes.swap)
+
+    r2_ids = moved_ids(own.ids, r1.ids, routes.rounds[1])
+    r3_ids = moved_ids(r2_ids, own.ids, routes.rounds[2])
     r4_ids = routes.moved(r3_ids, routes.rounds[3])
     r5_ids = routes.moved(own.ids, routes.rounds[4])
-    all_ids = [own.ids, mate.ids, r1.ids, s1.ids, r2.ids, routes.moved(r2.ids, routes.swap)]
-    all_ids += [r3_ids, routes.moved(r3_ids, routes.swap), r4_ids, r5_ids, routes.moved(r5_ids, routes.swap)]
+    all_ids = [own.ids, mate.ids]
+    for ids in (r1.ids, r2_ids, r3_ids, r4_ids, r5_ids):
+        all_ids += [ids, swapped_ids(ids)]
     table = table_of(all_ids)
     near, far = 0, 1
     rows_near = own.array[:aux].T
@@ -556,46 +605,55 @@
         return (out, *copy) if copy else out
 
     f32, bf16 = jnp.float32, jnp.bfloat16
-    done = amps([(s, near) for s in (own, mate, r1, s1)], [rows_near], sent2.array)
-
-    sent, kept = choice_call(flag, r2.array, own.array, [done], keep=True)
+    done = amps([(own, near), (mate, near)], [rows_near])
+
+    sent2 = chosen(own, r1, own_far.pieces[0], done)
+    r2 = moved(sent2, routes.rounds[1])
+    s1 = swapped(r1)
+    done = amps([(r1, near), (s1, near)], [rows_near], sent2.array)
+    part = density([own, mate, r1, s1], near, [], f32, done)
+
+    sent, kept = choice_call(flag, r2.array, own.array, [part, *own_far.pieces], keep=True)
     r2 = Slab(kept, r2.ids)
     sent3 = Slab(sent, routes.either(r2.ids, own.ids))
     r3 = moved(sent3, routes.rounds[2])
     s2 = swapped(r2)
-    rows_far = own_far.array[:aux].T
-    part, again = density([own, mate, r1, s1], near, [], f32, sent3.array, copied=own_far.array)
-    mate_far = swapped(Slab(again, own.ids, 1))
+    mate_far = swapped(own_far)
+    rows_far = jnp.concatenate(own_far.pieces)[:aux].T
     jobs = [(r1, far), (s1, far), (r2, near), (r2, far), (s2, far), (s2, near)]
-    done = amps(jobs, [rows_near, rows_far], part)
-
-    r3 = chosen(r3, r3, done)
+    jobs += [(own_far, near), (mate_far, near)]
+    done = amps(jobs, [rows_near, rows_far], sent3.array)
+    part = density([own_far, mate_far, r2, s2], near, [[part]], f32, done)
+
+    r3 = chosen(r3, r3, part)
     r4 = moved(r3, routes.rounds[3])
     s3 = swapped(r3)
-    jobs = [(own_far, near), (mate_far, near), (r3, near), (r3, far), (s3, far), (s3, near)]
-    done = amps(jobs, [rows_near, rows_far], done)
-    slabs = [own_far, mate_far, r2, s2, r3, s3]
-    part, again = density(slabs, near, [[part]], f32, done, copied=own.array)
+    out_part, again = density([r1, s1, r2, s2], far, [], f32, r3.array, copied=own.pieces)
     r5 = moved(Slab(again, own.ids), routes.rounds[4])
+    jobs = [(r3, near), (r3, far), (s3, far), (s3, near)]
+    done = amps(jobs, [rows_near, rows_far], out_part)
+    part = density([r3, s3], near, [[part]], f32, done)
 
     done = amps([(r4, far)], [rows_near, rows_far], part)
-    slabs = [r1, s1, r2, s2, r3, s3, r4]
     half = aux // 2
-    sent0, again = density(slabs, far, [], bf16, done, rows=(0, half), copied=own_far.array)
-    sent1 = density(slabs, far, [], bf16, sent0, rows=(half, half))
+    slabs = [r3, s3, r4]
+    sent0, again = density(
+        slabs, far, [[out_part]], bf16, done, rows=(0, half), copied=own_far.pieces
+    )
     r6 = moved(Slab(again, own.ids, 1), routes.rounds[4])
+    sent1 = density(slabs, far, [[out_part]], bf16, sent0, rows=(half, half))
     incoming = [sibling(sent0), sibling(sent1)]
     done = amps([(r4, near)], [rows_near], sent1)
 
-    r5 = chosen(r5, r5, done, pieces=3)
+    r5 = chosen(r5, r5, done, pieces=PIECES)
     s5 = swapped(r5)
-    done = amps([(r5, near)], [rows_near], r5.array)
+    done = amps([(r5, near)], [rows_near], *r5.pieces)
     done = join_call([incoming[0], done])
     done = amps([(s5, near)], [rows_near], done)
     part = density([r4, r5, s5], near, [[part]], f32, done)
-    r6 = chosen(r6, r6, part, pieces=3)
+    r6 = chosen(r6, r6, part, pieces=PIECES)
     s6 = swapped(r6)
-    done = amps([(r6, near)], [rows_near], r6.array)
+    done = amps([(r6, near)], [rows_near], *r6.pieces)
     done = join_call([incoming[1], done])
     done = amps([(s6, near)], [rows_near], done)
     return density([r6, s6], near, [[part], incoming], f32, done)[None]

time: 327 us -> 323 us (0.988)
  waiting for transfers between devices: 83.8 us -> 55.9 us
  Pallas kernels: 199 us -> 212 us
  local copies, waits for them, and re-layouts: 21.4 us -> 25.4 us
  other arithmetic: 1.94 us -> 5.68 us
    ppermute x17 -> x18, waiting for transfers between devices: 53.2 us -> 32.3 us  [moved(): sent = [lax.ppermute(piece, 'wide', pairs) for piece in slab.pieces]]
    pallas_call x6 -> x8, Pallas kernels: 86.2 us -> 97.8 us  [density_call(): pl.pallas_call(kernel, grid=(steps,), in_specs=[pl.BlockSpec(memory_space...]
    ppermute x3 -> x4, waiting for transfers between devices: 30.7 us -> 23.6 us  [sibling(): return lax.ppermute(array, 'narrow', [(0, 1), (1, 0)])]
    unnamed x23 -> x31, local copies, waits for them, and re-layouts: 10.7 us -> 15.3 us
    pallas_call x9 -> x10, Pallas kernels: 83.3 us -> 87.5 us  [amplitude_call(): pl.pallas_call(kernel, grid=(len(jobs),), in_specs=[pl.BlockSpec(memory_s...]
    transpose x0 -> x1, other arithmetic: none -> 3.74 us  [paired_plan(): rows_far = jnp.concatenate(own_far.pieces)[:aux].T]
    pallas_call x5 -> x6, Pallas kernels: 24.9 us -> 22.5 us  [choice_call(): pl.pallas_call(kernel, in_specs=[pl.BlockSpec(memory_space=pltpu.SMEM)] +...]
    ppermute x17 -> x18, starting transfers between devices: 13.2 us -> 13.4 us  [moved(): sent = [lax.ppermute(piece, 'wide', pairs) for piece in slab.pieces]]
  transfers between devices with their start and end apart: 20 -> 22, of which waited for: 6 -> 6; matrix products, arithmetic and copies ran while one was open for 5% -> 6% of each run, Pallas kernels for 55% -> 57%
where the time goes in v6:
time: 323 us; the launch traced here: 318 us
  Pallas kernels  212 us (66%)
  waiting for transfers between devices  55.9 us (17%)
  local copies, waits for them, and re-layouts  25.4 us (8%)
  starting transfers between devices  18.5 us (6%)
  other arithmetic  5.68 us (2%)
    pallas_call x8, Pallas kernels, density_call(): pl.pallas_call(kernel, grid=(steps,), in_specs=[pl.BlockSpec(memory_space...  97.8 us
    pallas_call x10, Pallas kernels, amplitude_call(): pl.pallas_call(kernel, grid=(len(jobs),), in_specs=[pl.BlockSpec(memory_s...  87.5 us
    ppermute x18, waiting for transfers between devices, moved(): sent = [lax.ppermute(piece, 'wide', pairs) for piece in slab.pieces]  32.3 us
    ppermute x4, waiting for transfers between devices, sibling(): return lax.ppermute(array, 'narrow', [(0, 1), (1, 0)])  23.6 us
    pallas_call x6, Pallas kernels, choice_call(): pl.pallas_call(kernel, in_specs=[pl.BlockSpec(memory_space=pltpu.SMEM)] +...  22.5 us
    unnamed x31, local copies, waits for them, and re-layouts  15.3 us
    ppermute x18, starting transfers between devices, moved(): sent = [lax.ppermute(piece, 'wide', pairs) for piece in slab.pieces]  13.4 us
  transfers between devices with their start and end apart: 22, of which 6 were waited for; matrix products, arithmetic and copies ran while one was open for 6% of the time, Pallas kernels for 57%

profile of v6, /device:TPU:3, one launch (start us, length us, event | category | flops | bytes accessed | tf_op | source)
XLA Modules:
  0.0 317.9 jit_solution(7289218976743538034)
XLA Ops:
  1.3 2.9 shard_map.73.a_ref.b_ref.refs_0_.refs_9_
  4.4 2.2 collective-permute-start.2
  7.2 3.9 %shard_map.74 = (bf16[1536,512]{1,0:T(8,128)(2,1)}, bf16[1552,512]{1,0:T(8,128)(2,1)}) custom-call(s32[1]{0:T(128)} %dynamic_slice.12.flag_ref, bf16[3088,512]{1,0:T(8,128)(2,1)} %shard_map.73.a_ref.b_ref.refs_0_.refs_9_, bf16[3088,512]{1,0:T(8,128)(2,1)} %shard_map.73.a_ref.b_ref.refs_0_.refs_9_), custom_call_target="tpu_custom_call" | custom-call | bytes 6324224 | tf_op jit(solution)/shard_map/pallas_call | solution.py:360
  11.1 1.3 collective-permute-start.1
  12.7 29.1 %collective-permute-done.b_ref.refs_0_.refs_2_ = bf16[3088,512]{1,0:T(8,128)(2,1)} collective-permute-done((bf16[3088,512]{1,0:T(8,128)(2,1)}, bf16[3088,512]{1,0:T(8,128)(2,1)}, u32[]{:S(2)}, u32[]{:S(2)}) %collective-permute-start) | collective-permute-done | bytes 3162144 | tf_op jit(solution)/shard_map/ppermute | solution.py:526
  41.8 2.8 collective-permute-start.4
  45.3 1.9 slice.27
  49.8 4.6 %copy.73 = bf16[3072,512]{0,1:T(8,128)(2,1)} copy(bf16[3072,512]{1,0:T(8,128)(2,1)} %slice.27) | data formatting | bytes 6291456
  54.4 8.3 %shard_map.75.refs_1_.refs_4_.refs_5_ = bf16[2,512,512]{2,1,0:T(8,128)(2,1)} custom-call(f32[12,3]{1,0:T(8,128)} %copy.50.scalars, bf16[3088,512]{1,0:T(8,128)(2,1)} %shard_map.73.a_ref.b_ref.refs_0_.refs_9_, bf16[3088,512]{1,0:T(8,128)(2,1)} %collective-permute-done.2.refs_1_, bf16[512,3072]{1,0:T(8,128)(2,1)} %bitcast.21, ...), custom_call_target="tpu_custom_call" | custom-call | flops 3221225472 | bytes 10485760 | tf_op jit(solution)/shard_map/pallas_call | solution.py:215
  62.7 3.6 %shard_map.76.refs_3_ = bf16[3088,512]{1,0:T(8,128)(2,1)} custom-call(s32[1]{0:T(128)} %dynamic_slice.12.flag_ref, bf16[3088,512]{1,0:T(8,128)(2,1)} %shard_map.73.a_ref.b_ref.refs_0_.refs_9_, bf16[3088,512]{1,0:T(8,128)(2,1)} %collective-permute-done.b_ref.refs_0_.refs_2_, bf16[1536,512]{1,0:T(8,128)(2,1)} %collective-permute-done.1.refs_0_.refs_1_.refs_4_.refs_7_, ...), custom_call_target="tpu_custom_call" | custom-call | bytes 6324224 | tf_op jit(solution)/shard_map/pallas_call | solution.py:360
  66.4 1.3 collective-permute-start.5
  67.7 8.3 %shard_map.77.refs_6_.refs_7_.refs_8_ = bf16[2,512,512]{2,1,0:T(8,128)(2,1)} custom-call(f32[12,3]{1,0:T(8,128)} %copy.50.scalars, bf16[3088,512]{1,0:T(8,128)(2,1)} %collective-permute-done.b_ref.refs_0_.refs_2_, bf16[3088,512]{1,0:T(8,128)(2,1)} %collective-permute-done.4.refs_1_.refs_3_, bf16[512,3072]{1,0:T(8,128)(2,1)} %bitcast.22, ...), custom_call_target="tpu_custom_call" | custom-call | flops 3221225472 | bytes 10485760 | tf_op jit(solution)/shard_map/pallas_call | solution.py:215
  76.0 13.0 %shard_map.78.refs_0_.refs_11_ = f32[3072,512]{1,0:T(8,128)} custom-call(bf16[3088,512]{1,0:T(8,128)(2,1)} %shard_map.73.a_ref.b_ref.refs_0_.refs_9_, bf16[3088,512]{1,0:T(8,128)(2,1)} %collective-permute-done.2.refs_1_, bf16[3088,512]{1,0:T(8,128)(2,1)} %collective-permute-done.b_ref.refs_0_.refs_2_, ...), custom_call_target="tpu_custom_call" | custom-call | flops 6442450944 | bytes 20971520 | tf_op jit(solution)/shard_map/pallas_call | solution.py:493
  89.0 13.8 %collective-permute-done.5.refs_2_.refs_5_.refs_1_.refs_8_ = bf16[1552,512]{1,0:T(8,128)(2,1)S(1)} collective-permute-done((bf16[1552,512]{1,0:T(8,128)(2,1)S(1)}, bf16[1552,512]{1,0:T(8,128)(2,1)S(1)}, u32[]{:S(2)}, u32[]{:S(2)}) %collective-permute-start.5) | collective-permute-done | bytes 1589280 | tf_op jit(solution)/shard_map/ppermute | solution.py:542
  102.8 1.9 collective-permute-done.3.a_ref
  104.7 1.7 copy-done.9
  106.4 4.6 %shard_map.79 = (bf16[3088,512]{1,0:T(8,128)(2,1)}, bf16[3088,512]{1,0:T(8,128)(2,1)}) custom-call(s32[1]{0:T(128)} %dynamic_slice.12.flag_ref, bf16[3088,512]{1,0:T(8,128)(2,1)} %copy-done.9, bf16[3088,512]{1,0:T(8,128)(2,1)} %shard_map.73.a_ref.b_ref.refs_0_.refs_9_, f32[3072,512]{1,0:T(8,128)} %shard_map.78.refs_0_.refs_11_, ...), custom_call_target="tpu_custom_call" | custom-call | bytes 6324224 | tf_op jit(solution)/shard_map/pallas_call | solution.py:360
  111.0 1.8 collective-permute-start.9
  113.3 3.7 %fusion = bf16[512,3072]{0,1:T(8,128)(2,1)} fusion(bf16[1552,512]{1,0:T(8,128)(2,1)} %copy-done.3, bf16[1536,512]{1,0:T(8,128)(2,1)} %collective-permute-done.1.refs_0_.refs_1_.refs_4_.refs_7_), kind=kLoop, calls=%fused_computation.1 | loop fusion | flops 6291456 | bytes 6307840 | tf_op jit(solution)/shard_map/transpose | solution.py:622
  117.1 4.7 %copy.55.refs_9_.refs_3_.refs_2_ = bf16[512,3072]{1,0:T(8,128)(2,1)} copy(bf16[512,3072]{0,1:T(8,128)(2,1)} %fusion) | data formatting | bytes 6291456 | tf_op jit(solution)/shard_map/transpose | solution.py:622
  121.7 1.2 collective-permute-done.7.refs_6_.refs_2_
  123.0 1.6 copy-done.4
  124.6 20.0 %shard_map.80.refs_6_.refs_7_.refs_8_.refs_9_.refs_10_.refs_4_.refs_5_ = bf16[8,512,512]{2,1,0:T(8,128)(2,1)} custom-call(f32[12,3]{1,0:T(8,128)} %copy.50.scalars, bf16[3088,512]{1,0:T(8,128)(2,1)} %collective-permute-done.b_ref.refs_0_.refs_2_, bf16[3088,512]{1,0:T(8,128)(2,1)} %collective-permute-done.4.refs_1_.refs_3_, ...), custom_call_target="tpu_custom_call" | custom-call | flops 12884901888 | bytes 29360128 | tf_op jit(solution)/shard_map/pallas_call | solution.py:215
  144.7 15.0 %shard_map.81.refs_0_.refs_5_ = f32[3072,512]{1,0:T(8,128)} custom-call(bf16[1536,512]{1,0:T(8,128)(2,1)} %collective-permute-done.1.refs_0_.refs_1_.refs_4_.refs_7_, bf16[1552,512]{1,0:T(8,128)(2,1)} %copy-done.3, bf16[1536,512]{1,0:T(8,128)(2,1)} %collective-permute-done.7.refs_6_.refs_2_, bf16[1552,512]{1,0:T(8,128)(2,1)} %collective-permute-done.8.refs_7_.refs_3_, ...), custom_call_target="tpu_custom_call" | custom-call | flops 6442450944 | bytes 27262976 | tf_op jit(solution)/shard_map/pallas_call | solution.py:493
  159.7 3.5 %shard_map.82.refs_8_.refs_0_ = bf16[3088,512]{1,0:T(8,128)(2,1)} custom-call(s32[1]{0:T(128)} %dynamic_slice.12.flag_ref, bf16[3088,512]{1,0:T(8,128)(2,1)} %collective-permute-done.6.a_ref.b_ref, bf16[3088,512]{1,0:T(8,128)(2,1)} %collective-permute-done.6.a_ref.b_ref, f32[3072,512]{1,0:T(8,128)} %shard_map.81.refs_0_.refs_5_), custom_call_target="tpu_custom_call" | custom-call | bytes 6324224 | tf_op jit(solution)/shard_map/pallas_call | solution.py:360
  164.4 1.3 collective-permute-start.11
  165.6 15.2 %shard_map.83 = (f32[3072,512]{1,0:T(8,128)}, bf16[3088,512]{1,0:T(8,128)(2,1)}) custom-call(bf16[3088,512]{1,0:T(8,128)(2,1)} %collective-permute-done.b_ref.refs_0_.refs_2_, bf16[3088,512]{1,0:T(8,128)(2,1)} %collective-permute-done.4.refs_1_.refs_3_, bf16[3088,512]{1,0:T(8,128)(2,1)} %get-tuple-element.34.refs_2_.refs_4_, bf16[3088,512]{1,0:T(8,128)(2,1)} %copy-done.4, ...), custom_call_target="tpu_custom_call" | custom-call | flops 6442450944 | bytes 20971520 | tf_op jit(solution)/shard_map/pallas_call | solution.py:493
  181.1 1.7 copy-done.2
  182.7 12.0 %shard_map.84.refs_2_.refs_3_.refs_4_ = bf16[4,512,512]{2,1,0:T(8,128)(2,1)} custom-call(f32[12,3]{1,0:T(8,128)} %copy.50.scalars, bf16[3088,512]{1,0:T(8,128)(2,1)} %shard_map.82.refs_8_.refs_0_, bf16[3088,512]{1,0:T(8,128)(2,1)} %copy-done.2, bf16[512,3072]{1,0:T(8,128)(2,1)} %bitcast.24, bf16[512,3072]{1,0:T(8,128)(2,1)} %copy.55.refs_9_.refs_3_.refs_2_, ...), custom_call_target="tpu_custom_call" | custom-call | flops 6442450944 | bytes 14680064 | tf_op jit(solution)/shard_map/pallas_call | solution.py:215
  194.8 11.5 %shard_map.85.refs_3_.refs_11_ = f32[3072,512]{1,0:T(8,128)} custom-call(bf16[3088,512]{1,0:T(8,128)(2,1)} %shard_map.82.refs_8_.refs_0_, bf16[3088,512]{1,0:T(8,128)(2,1)} %copy-done.2, bf16[4,512,512]{2,1,0:T(8,128)(2,1)} %shard_map.84.refs_2_.refs_3_.refs_4_, bf16[4,512,512]{2,1,0:T(8,128)(2,1)} %shard_map.84.refs_2_.refs_3_.refs_4_, ...), custom_call_target="tpu_custom_call" | custom-call | flops 3221225472 | bytes 19922944 | tf_op jit(solution)/shard_map/pallas_call | solution.py:493
  206.3 1.7 copy-done.1
  207.9 6.5 %shard_map.86.refs_5_.refs_6_ = bf16[1,512,512]{2,1,0:T(8,128)(2,1)} custom-call(f32[12,3]{1,0:T(8,128)} %copy.50.scalars, bf16[3088,512]{1,0:T(8,128)(2,1)} %copy-done.1, bf16[512,3072]{1,0:T(8,128)(2,1)} %bitcast.25, bf16[512,3072]{1,0:T(8,128)(2,1)} %copy.55.refs_9_.refs_3_.refs_2_, f32[3072,512]{1,0:T(8,128)} %shard_map.85.refs_3_.refs_11_, ...), custom_call_target="tpu_custom_call" | custom-call | flops 1610612736 | bytes 9961472 | tf_op jit(solution)/shard_map/pallas_call | solution.py:215
  214.4 9.3 %shard_map.87 = (bf16[1536,512]{1,0:T(8,128)(2,1)}, bf16[3088,512]{1,0:T(8,128)(2,1)}) custom-call(bf16[3088,512]{1,0:T(8,128)(2,1)} %shard_map.82.refs_8_.refs_0_, bf16[3088,512]{1,0:T(8,128)(2,1)} %copy-done.2, bf16[3088,512]{1,0:T(8,128)(2,1)} %copy-done.1, bf16[4,512,512]{2,1,0:T(8,128)(2,1)} %shard_map.84.refs_2_.refs_3_.refs_4_, ...), custom_call_target="tpu_custom_call" | custom-call | flops 2415919104 | bytes 11010048 | tf_op jit(solution)/shard_map/pallas_call | solution.py:493
  224.4 1.2 collective-permute-start.17
  225.6 8.2 %shard_map.88.refs_2_ = bf16[1536,512]{1,0:T(8,128)(2,1)} custom-call(bf16[3088,512]{1,0:T(8,128)(2,1)} %shard_map.82.refs_8_.refs_0_, bf16[3088,512]{1,0:T(8,128)(2,1)} %copy-done.2, bf16[3088,512]{1,0:T(8,128)(2,1)} %copy-done.1, bf16[4,512,512]{2,1,0:T(8,128)(2,1)} %shard_map.84.refs_2_.refs_3_.refs_4_, ...), custom_call_target="tpu_custom_call" | custom-call | flops 2415919104 | bytes 11010048 | tf_op jit(solution)/shard_map/pallas_call | solution.py:493
  233.8 6.5 %shard_map.89.refs_0_.refs_7_ = bf16[1,512,512]{2,1,0:T(8,128)(2,1)} custom-call(f32[12,3]{1,0:T(8,128)} %copy.50.scalars, bf16[3088,512]{1,0:T(8,128)(2,1)} %copy-done.1, bf16[512,3072]{1,0:T(8,128)(2,1)} %bitcast.26, bf16[1536,512]{1,0:T(8,128)(2,1)} %shard_map.88.refs_2_, f32[2,512,1]{2,1,0:T(8,128)} %copy.51.refs_3_.refs_4_.refs_11_.refs_5_.refs_7_, ...), custom_call_target="tpu_custom_call" | custom-call | flops 1610612736 | bytes 6815744 | tf_op jit(solution)/shard_map/pallas_call | solution.py:215
  240.3 3.5 %shard_map.90 = (bf16[1024,512]{1,0:T(8,128)(2,1)}, bf16[1024,512]{1,0:T(8,128)(2,1)}, bf16[1040,512]{1,0:T(8,128)(2,1)}) custom-call(s32[1]{0:T(128)} %dynamic_slice.12.flag_ref, bf16[3088,512]{1,0:T(8,128)(2,1)} %collective-permute-done.13.a_ref.b_ref, bf16[3088,512]{1,0:T(8,128)(2,1)} %collective-permute-done.13.a_ref.b_ref, ...), custom_call_target="tpu_custom_call" | custom-call | bytes 6324224 | tf_op jit(solution)/shard_map/pallas_call | solution.py:360
  244.7 6.5 %shard_map.91.refs_1_.refs_8_ = bf16[1,512,512]{2,1,0:T(8,128)(2,1)} custom-call(f32[12,3]{1,0:T(8,128)} %copy.50.scalars, bf16[1024,512]{1,0:T(8,128)(2,1)} %get-tuple-element.39.refs_0_.refs_4_.refs_1_, bf16[1024,512]{1,0:T(8,128)(2,1)} %get-tuple-element.40.refs_1_.refs_5_.refs_2_, bf16[1040,512]{1,0:T(8,128)(2,1)} %get-tuple-element.41.refs_2_.refs_6_.refs_3_, ...), custom_call_target="tpu_custom_call" | custom-call | flops 1610612736 | bytes 6815744 | tf_op jit(solution)/shard_map/pallas_call | solution.py:215
  251.2 9.5 %collective-permute-done.17.refs_0_.refs_10_ = bf16[1536,512]{1,0:T(8,128)(2,1)} collective-permute-done((bf16[1536,512]{1,0:T(8,128)(2,1)}, bf16[1536,512]{1,0:T(8,128)(2,1)}, u32[]{:S(2)}, u32[]{:S(2)}) %collective-permute-start.17) | collective-permute-done | bytes 1572896 | tf_op jit(solution)/shard_map/ppermute | solution.py:542
  260.7 1.2 collective-permute-start.21
  262.5 6.5 %shard_map.93.refs_9_.refs_10_ = bf16[1,512,512]{2,1,0:T(8,128)(2,1)} custom-call(f32[12,3]{1,0:T(8,128)} %copy.50.scalars, bf16[1024,512]{1,0:T(8,128)(2,1)} %collective-permute-done.14.refs_0_.refs_4_, bf16[1024,512]{1,0:T(8,128)(2,1)} %collective-permute-done.15.refs_1_.refs_5_, bf16[1040,512]{1,0:T(8,128)(2,1)} %collective-permute-done.16.refs_2_.refs_6_, ...), custom_call_target="tpu_custom_call" | custom-call | flops 1610612736 | bytes 6815744 | tf_op jit(solution)/shard_map/pallas_call | solution.py:215
  269.0 13.3 %shard_map.94.refs_0_.refs_9_ = f32[3072,512]{1,0:T(8,128)} custom-call(bf16[3088,512]{1,0:T(8,128)(2,1)} %copy-done.1, bf16[1024,512]{1,0:T(8,128)(2,1)} %get-tuple-element.39.refs_0_.refs_4_.refs_1_, bf16[1024,512]{1,0:T(8,128)(2,1)} %get-tuple-element.40.refs_1_.refs_5_.refs_2_, bf16[1040,512]{1,0:T(8,128)(2,1)} %get-tuple-element.41.refs_2_.refs_6_.refs_3_, ...), custom_call_target="tpu_custom_call" | custom-call | flops 4831838208 | bytes 23592960 | tf_op jit(solution)/shard_map/pallas_call | solution.py:493
  282.4 1.7 copy-done.5
  284.0 3.5 %shard_map.95 = (bf16[1024,512]{1,0:T(8,128)(2,1)}, bf16[1024,512]{1,0:T(8,128)(2,1)}, bf16[1040,512]{1,0:T(8,128)(2,1)}) custom-call(s32[1]{0:T(128)} %dynamic_slice.12.flag_ref, bf16[3088,512]{1,0:T(8,128)(2,1)} %copy-done.5, bf16[3088,512]{1,0:T(8,128)(2,1)} %copy-done.5, f32[3072,512]{1,0:T(8,128)} %shard_map.94.refs_0_.refs_9_), custom_call_target="tpu_custom_call" | custom-call | bytes 6324224 | tf_op jit(solution)/shard_map/pallas_call | solution.py:360
  287.5 1.2 collective-permute-start.20
  289.2 6.5 %shard_map.96.refs_1_.refs_6_ = bf16[1,512,512]{2,1,0:T(8,128)(2,1)} custom-call(f32[12,3]{1,0:T(8,128)} %copy.50.scalars, bf16[1024,512]{1,0:T(8,128)(2,1)} %get-tuple-element.42.refs_0_.refs_4_, bf16[1024,512]{1,0:T(8,128)(2,1)} %get-tuple-element.43.refs_1_.refs_5_, bf16[1040,512]{1,0:T(8,128)(2,1)} %get-tuple-element.44.refs_2_.refs_6_, ...), custom_call_target="tpu_custom_call" | custom-call | flops 1610612736 | bytes 6815744 | tf_op jit(solution)/shard_map/pallas_call | solution.py:215
  299.0 6.5 %shard_map.98.refs_7_.refs_8_ = bf16[1,512,512]{2,1,0:T(8,128)(2,1)} custom-call(f32[12,3]{1,0:T(8,128)} %copy.50.scalars, bf16[1024,512]{1,0:T(8,128)(2,1)} %copy-done.7, bf16[1024,512]{1,0:T(8,128)(2,1)} %copy-done.8, bf16[1040,512]{1,0:T(8,128)(2,1)} %copy-done.6, bf16[512,3072]{1,0:T(8,128)(2,1)} %bitcast.30, f32[8,128]{1,0:T(8,128)} %shard_map.97.refs_4_, ...), custom_call_target="tpu_custom_call" | custom-call | flops 1610612736 | bytes 6815744 | tf_op jit(solution)/shard_map/pallas_call | solution.py:215
  305.5 12.2 %shard_map.99 = f32[3072,512]{1,0:T(8,128)} custom-call(bf16[1024,512]{1,0:T(8,128)(2,1)} %get-tuple-element.42.refs_0_.refs_4_, bf16[1024,512]{1,0:T(8,128)(2,1)} %get-tuple-element.43.refs_1_.refs_5_, bf16[1040,512]{1,0:T(8,128)(2,1)} %get-tuple-element.44.refs_2_.refs_6_, bf16[1024,512]{1,0:T(8,128)(2,1)} %copy-done.7, bf16[1024,512]{1,0:T(8,128)(2,1)} %copy-done.8, ...), custom_call_target="tpu_custom_call" | custom-call | flops 3221225472 | bytes 26214400 | tf_op jit(solution)/shard_map/pallas_call | solution.py:493
  (71 shorter events, 13.5 us)
Async XLA Ops:
  1.3 5.2 %copy-start.14 = (s32[16]{0:T(128)S(1)}, s32[16]{0:T(128)}, u32[]{:S(2)}) copy-start(s32[16]{0:T(128)} %constant.51.clone) | copy-start | bytes 196
  4.3 37.5 %collective-permute-start = (bf16[3088,512]{1,0:T(8,128)(2,1)}, bf16[3088,512]{1,0:T(8,128)(2,1)}, u32[]{:S(2)}, u32[]{:S(2)}) collective-permute-start(bf16[3088,512]{1,0:T(8,128)(2,1)} %shard_map.73.a_ref.b_ref.refs_0_.refs_9_), channel_id=1, source_target_pairs={{0,6},{2,26},{4,12},{6,0},{8,14},{10,2},{12,20},{14,8},{16,22},{18... | collective-permute-start | bytes 9486344 | tf_op jit(solution)/shard_map/ppermute | solution.py:526
  4.4 50.1 %collective-permute-start.2 = (bf16[3088,512]{1,0:T(8,128)(2,1)}, bf16[3088,512]{1,0:T(8,128)(2,1)}, u32[]{:S(2)}, u32[]{:S(2)}) collective-permute-start(bf16[3088,512]{1,0:T(8,128)(2,1)} %shard_map.73.a_ref.b_ref.refs_0_.refs_9_), channel_id=1, source_target_pairs={{0,2},{2,0},{4,6},{6,4},{8,10},{10,8},{12,14},{14,12},{16,18},{18,... | collective-permute-start | bytes 9486344 | tf_op jit(solution)/shard_map/ppermute | solution.py:526
  7.2 5.2 %copy-start.10 = (f32[1024]{0:T(1024)S(1)}, f32[1024]{0:T(1024)}, u32[]{:S(2)}) copy-start(f32[1024]{0:T(1024)} %param.12) | copy-start | bytes 12292
  7.2 5.3 %copy-start.12 = (f32[16]{0:T(128)S(1)}, f32[16]{0:T(128)}, u32[]{:S(2)}) copy-start(f32[16]{0:T(128)} %param.11) | copy-start | bytes 196
  7.2 5.3 %copy-start.13 = (s32[16]{0:T(128)S(1)}, s32[16]{0:T(128)}, u32[]{:S(2)}) copy-start(s32[16]{0:T(128)} %param.10) | copy-start | bytes 196
  7.2 38.1 %copy-start = (bf16[3088,512]{1,0:T(8,128)(2,1)S(1)}, bf16[3088,512]{1,0:T(8,128)(2,1)}, u32[]{:S(2)}) copy-start(bf16[3088,512]{1,0:T(8,128)(2,1)} %shard_map.73.a_ref.b_ref.refs_0_.refs_9_) | copy-start | bytes 9486340
  11.1 51.6 %collective-permute-start.1 = (bf16[1536,512]{1,0:T(8,128)(2,1)}, bf16[1536,512]{1,0:T(8,128)(2,1)}, u32[]{:S(2)}, u32[]{:S(2)}) collective-permute-start(bf16[1536,512]{1,0:T(8,128)(2,1)} %get-tuple-element.31), channel_id=1, source_target_pairs={{0,1},{1,0},{2,3},{3,2},{4,5},{5,4},{6,7},{7,6},{8,9},{9,8},{10,11... | collective-permute-start | bytes 4718600 | tf_op jit(solution)/shard_map/ppermute | solution.py:542
  41.8 25.9 %collective-permute-start.4 = (bf16[3088,512]{1,0:T(8,128)(2,1)}, bf16[3088,512]{1,0:T(8,128)(2,1)}, u32[]{:S(2)}, u32[]{:S(2)}) collective-permute-start(bf16[3088,512]{1,0:T(8,128)(2,1)} %collective-permute-done.b_ref.refs_0_.refs_2_), channel_id=1, source_target_pairs={{0,2},{2,0},{4,6},{6,4},{8,10},{10,8},{12,14},{14,12},{16,18},{18,... | collective-permute-start | bytes 9486344 | tf_op jit(solution)/shard_map/ppermute | solution.py:526
  62.7 3.7 %copy-start.11 = (bf16[1552,512]{1,0:T(8,128)(2,1)S(1)}, bf16[1552,512]{1,0:T(8,128)(2,1)}, u32[]{:S(2)}) copy-start(bf16[1552,512]{1,0:T(8,128)(2,1)} %get-tuple-element.32) | copy-start | bytes 4767748
  66.3 38.4 %collective-permute-start.3 = (bf16[3088,512]{1,0:T(8,128)(2,1)}, bf16[3088,512]{1,0:T(8,128)(2,1)S(1)}, u32[]{:S(2)}, u32[]{:S(2)}) collective-permute-start(bf16[3088,512]{1,0:T(8,128)(2,1)} %shard_map.76.refs_3_), channel_id=1, source_target_pairs={{0,24},{2,4},{4,2},{6,14},{8,0},{10,12},{12,10},{14,22},{16,8},{18... | collective-permute-start | bytes 9486344 | tf_op jit(solution)/shard_map/ppermute | solution.py:526
  66.4 36.4 %collective-permute-start.5 = (bf16[1552,512]{1,0:T(8,128)(2,1)S(1)}, bf16[1552,512]{1,0:T(8,128)(2,1)S(1)}, u32[]{:S(2)}, u32[]{:S(2)}) collective-permute-start(bf16[1552,512]{1,0:T(8,128)(2,1)S(1)} %copy-done.11), channel_id=1, source_target_pairs={{0,1},{1,0},{2,3},{3,2},{4,5},{5,4},{6,7},{7,6},{8,9},{9,8},{10,11... | collective-permute-start | bytes 4767752 | tf_op jit(solution)/shard_map/ppermute | solution.py:542
  102.8 1.9 copy-start.3
  104.7 1.7 copy-start.9
  111.0 12.0 %collective-permute-start.9 = (bf16[3088,512]{1,0:T(8,128)(2,1)}, bf16[3088,512]{1,0:T(8,128)(2,1)S(1)}, u32[]{:S(2)}, u32[]{:S(2)}) collective-permute-start(bf16[3088,512]{1,0:T(8,128)(2,1)} %get-tuple-element.34.refs_2_.refs_4_), channel_id=1, source_target_pairs={{0,2},{2,0},{4,6},{6,4},{8,10},{10,8},{12,14},{14,12},{16,18},{18,... | collective-permute-start | bytes 9486344 | tf_op jit(solution)/shard_map/ppermute | solution.py:526
  112.8 10.2 %collective-permute-start.8 = (bf16[1552,512]{1,0:T(8,128)(2,1)}, bf16[1552,512]{1,0:T(8,128)(2,1)}, u32[]{:S(2)}, u32[]{:S(2)}) collective-permute-start(bf16[1552,512]{1,0:T(8,128)(2,1)} %copy-done.3), channel_id=1, source_target_pairs={{0,2},{2,0},{4,6},{6,4},{8,10},{10,8},{12,14},{14,12},{16,18},{18,... | collective-permute-start | bytes 4767752 | tf_op jit(solution)/shard_map/ppermute | solution.py:526
  112.9 10.1 %collective-permute-start.7 = (bf16[1536,512]{1,0:T(8,128)(2,1)}, bf16[1536,512]{1,0:T(8,128)(2,1)}, u32[]{:S(2)}, u32[]{:S(2)}) collective-permute-start(bf16[1536,512]{1,0:T(8,128)(2,1)} %collective-permute-done.1.refs_0_.refs_1_.refs_4_.refs_7_), channel_id=1, source_target_pairs={{0,2},{2,0},{4,6},{6,4},{8,10},{10,8},{12,14},{14,12},{16,18},{18,... | collective-permute-start | bytes 4718600 | tf_op jit(solution)/shard_map/ppermute | solution.py:526
  113.3 46.4 %collective-permute-start.6 = (bf16[3088,512]{1,0:T(8,128)(2,1)}, bf16[3088,512]{1,0:T(8,128)(2,1)}, u32[]{:S(2)}, u32[]{:S(2)}) collective-permute-start(bf16[3088,512]{1,0:T(8,128)(2,1)} %get-tuple-element.33.refs_10_), channel_id=1, source_target_pairs={{0,6},{2,10},{4,28},{6,0},{8,14},{10,18},{12,4},{14,8},{16,22},{18... | collective-permute-start | bytes 9486344 | tf_op jit(solution)/shard_map/ppermute | solution.py:526
  123.0 1.6 copy-start.4
  163.2 17.9 %collective-permute-start.10 = (bf16[3088,512]{1,0:T(8,128)(2,1)}, bf16[3088,512]{1,0:T(8,128)(2,1)S(1)}, u32[]{:S(2)}, u32[]{:S(2)}) collective-permute-start(bf16[3088,512]{1,0:T(8,128)(2,1)} %shard_map.82.refs_8_.refs_0_), channel_id=1, source_target_pairs={{0,2},{2,0},{4,6},{6,4},{8,10},{10,8},{12,14},{14,12},{16,18},{18,... | collective-permute-start | bytes 9486344 | tf_op jit(solution)/shard_map/ppermute | solution.py:526
  164.4 41.9 %collective-permute-start.11 = (bf16[3088,512]{1,0:T(8,128)(2,1)}, bf16[3088,512]{1,0:T(8,128)(2,1)S(1)}, u32[]{:S(2)}, u32[]{:S(2)}) collective-permute-start(bf16[3088,512]{1,0:T(8,128)(2,1)} %shard_map.82.refs_8_.refs_0_), channel_id=1, source_target_pairs={{0,8},{2,4},{4,2},{6,30},{8,16},{10,12},{12,10},{14,6},{16,24},{18... | collective-permute-start | bytes 9486344 | tf_op jit(solution)/shard_map/ppermute | solution.py:526
  180.8 59.5 %collective-permute-start.13 = (bf16[3088,512]{1,0:T(8,128)(2,1)}, bf16[3088,512]{1,0:T(8,128)(2,1)}, u32[]{:S(2)}, u32[]{:S(2)}) collective-permute-start(bf16[3088,512]{1,0:T(8,128)(2,1)} %get-tuple-element.37), channel_id=1, source_target_pairs={{0,8},{2,4},{4,2},{6,30},{8,16},{10,12},{12,10},{14,6},{16,24},{18... | collective-permute-start | bytes 9486344 | tf_op jit(solution)/shard_map/ppermute | solution.py:526
  181.1 1.7 copy-start.2
  206.3 1.7 copy-start.1
  223.8 58.6 %collective-permute-start.12 = (bf16[3088,512]{1,0:T(8,128)(2,1)}, bf16[3088,512]{1,0:T(8,128)(2,1)S(1)}, u32[]{:S(2)}, u32[]{:S(2)}) collective-permute-start(bf16[3088,512]{1,0:T(8,128)(2,1)} %get-tuple-element.36), channel_id=1, source_target_pairs={{0,8},{2,4},{4,2},{6,30},{8,16},{10,12},{12,10},{14,6},{16,24},{18... | collective-permute-start | bytes 9486344 | tf_op jit(solution)/shard_map/ppermute | solution.py:526
  224.4 36.3 %collective-permute-start.17 = (bf16[1536,512]{1,0:T(8,128)(2,1)}, bf16[1536,512]{1,0:T(8,128)(2,1)}, u32[]{:S(2)}, u32[]{:S(2)}) collective-permute-start(bf16[1536,512]{1,0:T(8,128)(2,1)} %get-tuple-element.38.refs_6_), channel_id=1, source_target_pairs={{0,1},{1,0},{2,3},{3,2},{4,5},{5,4},{6,7},{7,6},{8,9},{9,8},{10,11... | collective-permute-start | bytes 4718600 | tf_op jit(solution)/shard_map/ppermute | solution.py:542
  243.8 18.7 %collective-permute-start.16 = (bf16[1040,512]{1,0:T(8,128)(2,1)}, bf16[1040,512]{1,0:T(8,128)(2,1)}, u32[]{:S(2)}, u32[]{:S(2)}) collective-permute-start(bf16[1040,512]{1,0:T(8,128)(2,1)} %get-tuple-element.41.refs_2_.refs_6_.refs_3_), channel_id=1, source_target_pairs={{0,2},{2,0},{4,6},{6,4},{8,10},{10,8},{12,14},{14,12},{16,18},{18,... | collective-permute-start | bytes 3194888 | tf_op jit(solution)/shard_map/ppermute | solution.py:526
  244.2 18.3 %collective-permute-start.14 = (bf16[1024,512]{1,0:T(8,128)(2,1)}, bf16[1024,512]{1,0:T(8,128)(2,1)}, u32[]{:S(2)}, u32[]{:S(2)}) collective-permute-start(bf16[1024,512]{1,0:T(8,128)(2,1)} %get-tuple-element.39.refs_0_.refs_4_.refs_1_), channel_id=1, source_target_pairs={{0,2},{2,0},{4,6},{6,4},{8,10},{10,8},{12,14},{14,12},{16,18},{18,... | collective-permute-start | bytes 3145736 | tf_op jit(solution)/shard_map/ppermute | solution.py:526
  244.4 18.1 %collective-permute-start.15 = (bf16[1024,512]{1,0:T(8,128)(2,1)}, bf16[1024,512]{1,0:T(8,128)(2,1)}, u32[]{:S(2)}, u32[]{:S(2)}) collective-permute-start(bf16[1024,512]{1,0:T(8,128)(2,1)} %get-tuple-element.40.refs_1_.refs_5_.refs_2_), channel_id=1, source_target_pairs={{0,2},{2,0},{4,6},{6,4},{8,10},{10,8},{12,14},{14,12},{16,18},{18,... | collective-permute-start | bytes 3145736 | tf_op jit(solution)/shard_map/ppermute | solution.py:526
  260.7 35.4 %collective-permute-start.21 = (bf16[1536,512]{1,0:T(8,128)(2,1)}, bf16[1536,512]{1,0:T(8,128)(2,1)}, u32[]{:S(2)}, u32[]{:S(2)}) collective-permute-start(bf16[1536,512]{1,0:T(8,128)(2,1)} %shard_map.88.refs_2_), channel_id=1, source_target_pairs={{0,1},{1,0},{2,3},{3,2},{4,5},{5,4},{6,7},{7,6},{8,9},{9,8},{10,11... | collective-permute-start | bytes 4718600 | tf_op jit(solution)/shard_map/ppermute | solution.py:542
  282.4 1.7 copy-start.5
  287.5 9.2 %collective-permute-start.20 = (bf16[1040,512]{1,0:T(8,128)(2,1)}, bf16[1040,512]{1,0:T(8,128)(2,1)S(1)}, u32[]{:S(2)}, u32[]{:S(2)}) collective-permute-start(bf16[1040,512]{1,0:T(8,128)(2,1)} %get-tuple-element.44.refs_2_.refs_6_), channel_id=1, source_target_pairs={{0,2},{2,0},{4,6},{6,4},{8,10},{10,8},{12,14},{14,12},{16,18},{18,... | collective-permute-start | bytes 3194888 | tf_op jit(solution)/shard_map/ppermute | solution.py:526
  288.7 7.9 %collective-permute-start.18 = (bf16[1024,512]{1,0:T(8,128)(2,1)}, bf16[1024,512]{1,0:T(8,128)(2,1)S(1)}, u32[]{:S(2)}, u32[]{:S(2)}) collective-permute-start(bf16[1024,512]{1,0:T(8,128)(2,1)} %get-tuple-element.42.refs_0_.refs_4_), channel_id=1, source_target_pairs={{0,2},{2,0},{4,6},{6,4},{8,10},{10,8},{12,14},{14,12},{16,18},{18,... | collective-permute-start | bytes 3145736 | tf_op jit(solution)/shard_map/ppermute | solution.py:526
  288.8 7.9 %collective-permute-start.19 = (bf16[1024,512]{1,0:T(8,128)(2,1)}, bf16[1024,512]{1,0:T(8,128)(2,1)S(1)}, u32[]{:S(2)}, u32[]{:S(2)}) collective-permute-start(bf16[1024,512]{1,0:T(8,128)(2,1)} %get-tuple-element.43.refs_1_.refs_5_), channel_id=1, source_target_pairs={{0,2},{2,0},{4,6},{6,4},{8,10},{10,8},{12,14},{14,12},{16,18},{18,... | collective-permute-start | bytes 3145736 | tf_op jit(solution)/shard_map/ppermute | solution.py:526
  296.7 1.1 copy-start.7
  296.7 1.3 copy-start.8
  298.0 1.0 copy-start.6

commit v7 on v6

--- a/solution.py
+++ b/solution.py
@@ -147,7 +147,7 @@
         if slab not in slabs:
             slabs.append(slab)
     count, blocks = len(slabs), len(turned)
-    cols, aux = turned[0].shape
+    cols, aux = turned[0][0].shape[0], sum(piece.shape[1] for piece in turned[0])
     held_rows = aux + TAIL
     pieces = [len(slab.pieces) for slab in slabs]
     begins = [sum(pieces[:s]) for s in range(count)]
@@ -155,12 +155,14 @@
     block_of = [block for _, block in jobs]
     far_of = [slab.far for slab, _ in jobs]
     line_of = [lines[slab] for slab, _ in jobs]
+    row_pieces = [len(block) for block in turned]
+    chunks = aux // CHUNK
     opens = [t for t in range(len(jobs)) if t == 0 or of_job[t] != of_job[t - 1]]
     half = cols // 2
 
     def kernel(scalars, *refs):
         sources, refs = refs[: sum(pieces)], refs[sum(pieces) :]
-        row_sources, refs = refs[:blocks], refs[blocks + len(earlier) :]
+        row_sources, refs = refs[: sum(row_pieces)], refs[sum(row_pieces) + len(earlier) :]
         vir_row, vir_col, out, held, rows, held_sems, row_sems = refs
         step = pl.program_id(0)
 
@@ -168,55 +170,94 @@
             row = 0
             for index in range(pieces[s]):
                 source = sources[begins[s] + index]
-                target = held.at[s % 2, pl.ds(row, source.shape[0]), :]
-                yield pltpu.make_async_copy(source, target, held_sems.at[s % 2, index])
-                row += source.shape[0]
-
-        def row_copy(block):
-            return pltpu.make_async_copy(row_sources[block], rows.at[block], row_sems.at[block])
+                for begin, size in chunks_of(source.shape[0]):
+                    target = held.at[s % 2, pl.ds(row, size), :]
+                    yield pltpu.make_async_copy(
+                        source.at[pl.ds(begin, size)], target, held_sems.at[s % 2, row // CHUNK]
+                    )
+                    row += size
+
+        def row_copies(block):
+            column = 0
+            for source in row_sources[sum(row_pieces[:block]) : sum(row_pieces[: block + 1])]:
+                for begin, size in chunks_of(source.shape[1]):
+                    target = rows.at[block, :, pl.ds(column, size)]
+                    yield pltpu.make_async_copy(
+                        source.at[:, pl.ds(begin, size)], target, row_sems.at[block, column // CHUNK]
+                    )
+                    column += size
 
         @pl.when(step == 0)
         def _():
-            for copy in slab_copies(0):
+            for pair in zip(slab_copies(0), row_copies(block_of[0])):
+                for copy in pair:
+                    copy.start()
+            for copy in list(slab_copies(0))[chunks:]:
                 copy.start()
-            for block in dict.fromkeys(block_of):
-                row_copy(block).start()
+            for block in list(dict.fromkeys(block_of))[1:]:
+                for copy in row_copies(block):
+                    copy.start()
 
         for s, t in enumerate(opens):
 
             @pl.when(step == t)
             def _(s=s):
-                for copy in slab_copies(s):
-                    copy.wait()
+                if s:
+                    for copy in slab_copies(s):
+                        copy.wait()
                 if s + 1 < count:
                     for copy in slab_copies(s + 1):
                         copy.start()
 
-        for block in dict.fromkeys(block_of):
+        for block in list(dict.fromkeys(block_of))[1:]:
 
             @pl.when(step == block_of.index(block))
             def _(block=block):
-                row_copy(block).wait()
+                for copy in row_copies(block):
+                    copy.wait()
 
         slot = pick(step, [s % 2 for s in of_job])
         block = pick(step, block_of)
         line = pick(step, line_of)
+        @pl.when(step == 0)
+        def _():
+            for copy in list(slab_copies(0))[chunks:]:
+                copy.wait()
+
         plan = held[slot, aux:, :128].astype(jnp.float32)
         lane = lax.broadcasted_iota(jnp.int32, plan.shape, 1).astype(jnp.float32)
         row = lax.broadcasted_iota(jnp.int32, plan.shape, 0)
         told = jnp.where(jnp.logical_and(row == 0, lane == scalars[line, 2]), plan, 0.0)
         weight = scalars[line, 1] + jnp.sum(told, keepdims=True)
-        for begin in range(0, cols, half):
-            part = pl.ds(begin, half)
-            coulomb = jnp.dot(rows[block], held[slot, :aux, part], preferred_element_type=jnp.float32)
+
+        def finish(part, coulomb):
             denominator = (vir_row[0] + vir_col[0, :, part]) - scalars[line, 0]
             out[0, :, part] = (weight * coulomb / denominator).astype(out.dtype)
+
+        @pl.when(step == 0)
+        def _():
+            coulomb = None
+            for index, pair in enumerate(zip(row_copies(block_of[0]), slab_copies(0))):
+                for copy in pair:
+                    copy.wait()
+                chunk = pl.ds(index * CHUNK, CHUNK)
+                term = jnp.dot(
+                    rows[block_of[0], :, chunk], held[0, chunk, :], preferred_element_type=jnp.float32
+                )
+                coulomb = term if coulomb is None else coulomb + term
+            finish(pl.ds(0, cols), coulomb)
+
+        @pl.when(step > 0)
+        def _():
+            for begin in range(0, cols, half):
+                part = pl.ds(begin, half)
+                finish(part, jnp.dot(rows[block], held[slot, :aux, part], preferred_element_type=jnp.float32))
 
     return pl.pallas_call(
         kernel,
         grid=(len(jobs),),
         in_specs=[pl.BlockSpec(memory_space=pltpu.SMEM)]
-        + [pl.BlockSpec(memory_space=pl.ANY)] * (sum(pieces) + blocks + len(earlier))
+        + [pl.BlockSpec(memory_space=pl.ANY)] * (sum(pieces) + sum(row_pieces) + len(earlier))
         + [
             pl.BlockSpec((1, cols, 1), lambda t: (pick(t, block_of), 0, 0)),
             pl.BlockSpec((1, 1, cols), lambda t: (pick(t, far_of), 0, 0)),
@@ -226,8 +267,8 @@
         scratch_shapes=[
             pltpu.VMEM((2, held_rows, cols), jnp.bfloat16),
             pltpu.VMEM((blocks, cols, aux), jnp.bfloat16),
-            pltpu.SemaphoreType.DMA((2, max(pieces))),
-            pltpu.SemaphoreType.DMA((blocks,)),
+            pltpu.SemaphoreType.DMA((2, chunks + 1)),
+            pltpu.SemaphoreType.DMA((blocks, chunks)),
         ],
         compiler_params=pltpu.CompilerParams(vmem_limit_bytes=VMEM),
         cost_estimate=pl.CostEstimate(
@@ -235,7 +276,7 @@
             bytes_accessed=2 * cols * (blocks * aux + count * aux + len(jobs) * cols),
             transcendentals=0,
         ),
-    )(table, *[p for s in slabs for p in s.pieces], *turned, *earlier, vir_rows, vir_cols)
+    )(table, *[p for s in slabs for p in s.pieces], *[p for b in turned for p in b], *earlier, vir_rows, vir_cols)
 
 
 def chunks_of(rows):
@@ -417,8 +458,8 @@
                     amps[s].at[place], right.at[:, pl.ds(s * depth, depth)], right_sems.at[s]
                 )
 
-        def slab_copies(which, start):
-            for s in range(count):
+        def slab_copies(which, start, of=range(count)):
+            for s in of:
                 end = 0
                 for index in range(pieces[s]):
                     source = sources[begins[s] + index]
@@ -442,9 +483,9 @@
 
         @pl.when(step == 0)
         def _():
-            for copy in amp_copies():
+            for s, copy in enumerate(amp_copies()):
                 copy.start()
-            slab_copies(step, True)
+                slab_copies(step, True, [s])
             if extra:
                 for copy in copies_in(source, scratch[0], scratch[1]):
                     copy.start()
@@ -453,23 +494,34 @@
         def _():
             slab_copies(step + 1, True)
 
+        def finish(total):
+            at = 0
+            for span in spans:
+                part = part_refs[at][...]
+                for index in range(1, len(span)):
+                    part = jnp.where(step >= span[index][0], part_refs[at + index][...], part)
+                total = total + part.astype(jnp.float32)
+                at += len(span)
+            out[...] = total.astype(out.dtype)
+
+        def product(a, b):
+            return lax.dot_general(a, b, (((1,), (1,)), ((), ())), preferred_element_type=jnp.float32)
+
         @pl.when(step == 0)
         def _():
-            for copy in amp_copies():
+            total = None
+            for s, copy in enumerate(amp_copies()):
                 copy.wait()
-
-        slab_copies(step, False)
-        total = lax.dot_general(
-            left[slot], right[...], (((1,), (1,)), ((), ())), preferred_element_type=jnp.float32
-        )
-        at = 0
-        for span in spans:
-            part = part_refs[at][...]
-            for index in range(1, len(span)):
-                part = jnp.where(step >= span[index][0], part_refs[at + index][...], part)
-            total = total + part.astype(jnp.float32)
-            at += len(span)
-        out[...] = total.astype(out.dtype)
+                slab_copies(step, False, [s])
+                at = pl.ds(s * depth, depth)
+                term = product(left[0, :, at], right[:, at])
+                total = term if total is None else total + term
+            finish(total)
+
+        @pl.when(step > 0)
+        def _():
+            slab_copies(step, False)
+            finish(product(left[slot], right[...]))
 
         if extra:
 
@@ -589,7 +641,7 @@
         all_ids += [ids, swapped_ids(ids)]
     table = table_of(all_ids)
     near, far = 0, 1
-    rows_near = own.array[:aux].T
+    rows_near = [own.array[:aux].T]
     stacks = {}
 
     def amps(jobs, turned, *earlier):
@@ -607,7 +659,9 @@
     f32, bf16 = jnp.float32, jnp.bfloat16
     done = amps([(own, near), (mate, near)], [rows_near])
 
-    sent2 = chosen(own, r1, own_far.pieces[0], done)
+    sent, kept = choice_call(1 - flag, r1.array, own.array, [own_far.pieces[0], done], keep=True)
+    r1 = Slab(kept, r1.ids)
+    sent2 = Slab(sent, routes.either(own.ids, r1.ids))
     r2 = moved(sent2, routes.rounds[1])
     s1 = swapped(r1)
     done = amps([(r1, near), (s1, near)], [rows_near], sent2.array)
@@ -619,7 +673,8 @@
     r3 = moved(sent3, routes.rounds[2])
     s2 = swapped(r2)
     mate_far = swapped(own_far)
-    rows_far = jnp.concatenate(own_far.pieces)[:aux].T
+    cut = own_far.pieces[0].shape[0]
+    rows_far = [own_far.pieces[0].T, own_far.pieces[1][: aux - cut].T]
     jobs = [(r1, far), (s1, far), (r2, near), (r2, far), (s2, far), (s2, near)]
     jobs += [(own_far, near), (mate_far, near)]
     done = amps(jobs, [rows_near, rows_far], sent3.array)
@@ -632,9 +687,8 @@
     r5 = moved(Slab(again, own.ids), routes.rounds[4])
     jobs = [(r3, near), (r3, far), (s3, far), (s3, near)]
     done = amps(jobs, [rows_near, rows_far], out_part)
-    part = density([r3, s3], near, [[part]], f32, done)
-
-    done = amps([(r4, far)], [rows_near, rows_far], part)
+
+    done = amps([(r4, far)], [rows_near, rows_far], done)
     half = aux // 2
     slabs = [r3, s3, r4]
     sent0, again = density(
@@ -644,13 +698,14 @@
     sent1 = density(slabs, far, [[out_part]], bf16, sent0, rows=(half, half))
     incoming = [sibling(sent0), sibling(sent1)]
     done = amps([(r4, near)], [rows_near], sent1)
-
-    r5 = chosen(r5, r5, done, pieces=PIECES)
+    part = density([r3, s3, r4], near, [[part]], f32, done)
+
+    r5 = chosen(r5, r5, part, pieces=PIECES)
     s5 = swapped(r5)
     done = amps([(r5, near)], [rows_near], *r5.pieces)
     done = join_call([incoming[0], done])
     done = amps([(s5, near)], [rows_near], done)
-    part = density([r4, r5, s5], near, [[part]], f32, done)
+    part = density([r5, s5], near, [[part]], f32, done)
     r6 = chosen(r6, r6, part, pieces=PIECES)
     s6 = swapped(r6)
     done = amps([(r6, near)], [rows_near], *r6.pieces)

time: 323 us -> 306 us (0.947)
  waiting for transfers between devices: 55.9 us -> 38.4 us
  other arithmetic: 5.68 us -> 1.94 us
    ppermute x18, waiting for transfers between devices: 32.3 us -> 15.1 us  [moved(): sent = [lax.ppermute(piece, 'wide', pairs) for piece in slab.pieces]]
    pallas_call x10, Pallas kernels: 87.5 us -> 91.7 us  [amplitude_call(): pl.pallas_call(kernel, grid=(len(jobs),), in_specs=[pl.BlockSpec(memory_s...]
    transpose x1 -> x0, other arithmetic: 3.74 us -> none  [paired_plan(): rows_far = jnp.concatenate(own_far.pieces)[:aux].T]
  transfers between devices with their start and end apart: 22 -> 22, of which waited for: 6 -> 7; matrix products, arithmetic and copies ran while one was open for 6% -> 5% of each run, Pallas kernels for 57% -> 59%
where the time goes in v7:
time: 306 us; the launch traced here: 303 us
  Pallas kernels  215 us (70%)
  waiting for transfers between devices  38.4 us (13%)
  local copies, waits for them, and re-layouts  25.1 us (8%)
  starting transfers between devices  21.3 us (7%)
    pallas_call x8, Pallas kernels, density_call(): pl.pallas_call(kernel, grid=(steps,), in_specs=[pl.BlockSpec(memory_space...  94.8 us
    pallas_call x10, Pallas kernels, amplitude_call(): pl.pallas_call(kernel, grid=(len(jobs),), in_specs=[pl.BlockSpec(memory_s...  91.7 us
    pallas_call x6, Pallas kernels, choice_call(): pl.pallas_call(kernel, in_specs=[pl.BlockSpec(memory_space=pltpu.SMEM)] +...  24.4 us
    ppermute x4, waiting for transfers between devices, sibling(): return lax.ppermute(array, 'narrow', [(0, 1), (1, 0)])  23.4 us
    ppermute x18, starting transfers between devices, moved(): sent = [lax.ppermute(piece, 'wide', pairs) for piece in slab.pieces]  16 us
    unnamed x31, local copies, waits for them, and re-layouts  15.3 us
    ppermute x18, waiting for transfers between devices, moved(): sent = [lax.ppermute(piece, 'wide', pairs) for piece in slab.pieces]  15.1 us
  transfers between devices with their start and end apart: 22, of which 7 were waited for; matrix products, arithmetic and copies ran while one was open for 5% of the time, Pallas kernels for 59%

profile of v7, /device:TPU:3, one launch (start us, length us, event | category | flops | bytes accessed | tf_op | source)
XLA Modules:
  0.0 302.9 jit_solution(2205797124128076823)
XLA Ops:
  1.3 2.9 shard_map.73.a_ref.b_ref.refs_0_.refs_9_
  5.7 3.8 %shard_map.74 = (bf16[1536,512]{1,0:T(8,128)(2,1)}, bf16[1552,512]{1,0:T(8,128)(2,1)}) custom-call(s32[1]{0:T(128)} %dynamic_slice.12.flag_ref, bf16[3088,512]{1,0:T(8,128)(2,1)} %shard_map.73.a_ref.b_ref.refs_0_.refs_9_, bf16[3088,512]{1,0:T(8,128)(2,1)} %shard_map.73.a_ref.b_ref.refs_0_.refs_9_), custom_call_target="tpu_custom_call" | custom-call | bytes 6324224 | tf_op jit(solution)/shard_map/pallas_call | solution.py:401
  9.4 1.5 collective-permute-start.1
  11.0 1.9 slice.27
  17.1 4.6 %copy.82 = bf16[3072,512]{0,1:T(8,128)(2,1)} copy(bf16[3072,512]{1,0:T(8,128)(2,1)} %slice.27) | data formatting | bytes 6291456
  21.7 8.4 %shard_map.75.refs_1_.refs_4_.refs_5_ = bf16[2,512,512]{2,1,0:T(8,128)(2,1)} custom-call(f32[12,3]{1,0:T(8,128)} %copy.56.scalars, bf16[3088,512]{1,0:T(8,128)(2,1)} %shard_map.73.a_ref.b_ref.refs_0_.refs_9_, bf16[3088,512]{1,0:T(8,128)(2,1)} %collective-permute-done.2.refs_1_, bf16[512,3072]{1,0:T(8,128)(2,1)} %bitcast.22, ...), custom_call_target="tpu_custom_call" | custom-call | flops 3221225472 | bytes 10485760 | tf_op jit(solution)/shard_map/pallas_call | solution.py:256
  30.1 13.9 %collective-permute-done.1.refs_0_.refs_1_.refs_4_.refs_7_ = bf16[1536,512]{1,0:T(8,128)(2,1)} collective-permute-done((bf16[1536,512]{1,0:T(8,128)(2,1)}, bf16[1536,512]{1,0:T(8,128)(2,1)}, u32[]{:S(2)}, u32[]{:S(2)}) %collective-permute-start.1) | collective-permute-done | bytes 1572896 | tf_op jit(solution)/shard_map/ppermute | solution.py:594
  44.0 5.5 %shard_map.76 = (bf16[3088,512]{1,0:T(8,128)(2,1)}, bf16[3088,512]{1,0:T(8,128)(2,1)}) custom-call(s32[1]{0:T(128)S(6)} %sub.6.flag_ref, bf16[3088,512]{1,0:T(8,128)(2,1)} %collective-permute-done.a_ref, bf16[3088,512]{1,0:T(8,128)(2,1)} %shard_map.73.a_ref.b_ref.refs_0_.refs_9_, bf16[1536,512]{1,0:T(8,128)(2,1)} %collective-permute-done.1.refs_0_.refs_1_.refs_4_.refs_7_, ...), custom_call_target="tpu_custom_call" | custom-call | bytes 6324224 | tf_op jit(solution)/shard_map/pallas_call | solution.py:401
  50.8 1.5 collective-permute-start.3
  52.3 1.2 collective-permute-start.5
  53.5 2.8 collective-permute-done.4.refs_1_.refs_3_
  56.3 1.7 copy-done.3
  57.9 8.5 %shard_map.77.refs_6_.refs_7_.refs_8_ = bf16[2,512,512]{2,1,0:T(8,128)(2,1)} custom-call(f32[12,3]{1,0:T(8,128)} %copy.56.scalars, bf16[3088,512]{1,0:T(8,128)(2,1)} %get-tuple-element.35.refs_0_.refs_2_, bf16[3088,512]{1,0:T(8,128)(2,1)} %copy-done.3, bf16[512,3072]{1,0:T(8,128)(2,1)} %bitcast.23, bf16[3088,512]{1,0:T(8,128)(2,1)} %get-tuple-element.34.refs_3_, ...), custom_call_target="tpu_custom_call" | custom-call | flops 3221225472 | bytes 10485760 | tf_op jit(solution)/shard_map/pallas_call | solution.py:256
  66.4 12.3 %shard_map.78.refs_0_.refs_11_ = f32[3072,512]{1,0:T(8,128)} custom-call(bf16[3088,512]{1,0:T(8,128)(2,1)} %shard_map.73.a_ref.b_ref.refs_0_.refs_9_, bf16[3088,512]{1,0:T(8,128)(2,1)} %collective-permute-done.2.refs_1_, bf16[3088,512]{1,0:T(8,128)(2,1)} %get-tuple-element.35.refs_0_.refs_2_, bf16[3088,512]{1,0:T(8,128)(2,1)} %copy-done.3, ...), custom_call_target="tpu_custom_call" | custom-call | flops 6442450944 | bytes 20971520 | tf_op jit(solution)/shard_map/pallas_call | solution.py:545
  78.8 8.6 %collective-permute-done.5.refs_2_.refs_5_.refs_1_.refs_8_ = bf16[1552,512]{1,0:T(8,128)(2,1)S(1)} collective-permute-done((bf16[1552,512]{1,0:T(8,128)(2,1)}, bf16[1552,512]{1,0:T(8,128)(2,1)S(1)}, u32[]{:S(2)}, u32[]{:S(2)}) %collective-permute-start.5) | collective-permute-done | bytes 1589280 | tf_op jit(solution)/shard_map/ppermute | solution.py:594
  87.4 2.5 collective-permute-done.3.a_ref
  89.9 1.7 copy-done.10
  91.6 4.7 %shard_map.79 = (bf16[3088,512]{1,0:T(8,128)(2,1)}, bf16[3088,512]{1,0:T(8,128)(2,1)}) custom-call(s32[1]{0:T(128)} %dynamic_slice.12.flag_ref, bf16[3088,512]{1,0:T(8,128)(2,1)} %copy-done.10, bf16[3088,512]{1,0:T(8,128)(2,1)} %shard_map.73.a_ref.b_ref.refs_0_.refs_9_, f32[3072,512]{1,0:T(8,128)} %shard_map.78.refs_0_.refs_11_, ...), custom_call_target="tpu_custom_call" | custom-call | bytes 6324224 | tf_op jit(solution)/shard_map/pallas_call | solution.py:401
  96.3 2.4 collective-permute-start.9
  99.3 2.6 copy.61.refs_9_.refs_3_.refs_2_
  102.1 1.6 copy.62.refs_10_.refs_4_.refs_3_
  103.7 5.2 %collective-permute-done.7.refs_6_.refs_2_ = bf16[1536,512]{1,0:T(8,128)(2,1)} collective-permute-done((bf16[1536,512]{1,0:T(8,128)(2,1)}, bf16[1536,512]{1,0:T(8,128)(2,1)}, u32[]{:S(2)}, u32[]{:S(2)}) %collective-permute-start.7) | collective-permute-done | bytes 1572896 | tf_op jit(solution)/shard_map/ppermute | solution.py:578
  108.9 21.4 %shard_map.80.refs_6_.refs_7_.refs_8_.refs_9_.refs_10_.refs_4_.refs_5_ = bf16[8,512,512]{2,1,0:T(8,128)(2,1)} custom-call(f32[12,3]{1,0:T(8,128)} %copy.56.scalars, bf16[3088,512]{1,0:T(8,128)(2,1)} %get-tuple-element.35.refs_0_.refs_2_, bf16[3088,512]{1,0:T(8,128)(2,1)} %copy-done.3, bf16[3088,512]{1,0:T(8,128)(2,1)} %get-tuple-element.38.refs_2_.refs_4_, ...), custom_call_target="tpu_custom_call" | custom-call | flops 12884901888 | bytes 29360128 | tf_op jit(solution)/shard_map/pallas_call | solution.py:256
  130.2 14.7 %shard_map.81.refs_0_.refs_7_ = f32[3072,512]{1,0:T(8,128)} custom-call(bf16[1536,512]{1,0:T(8,128)(2,1)} %collective-permute-done.1.refs_0_.refs_1_.refs_4_.refs_7_, bf16[1552,512]{1,0:T(8,128)(2,1)} %copy-done.4, bf16[1536,512]{1,0:T(8,128)(2,1)} %collective-permute-done.7.refs_6_.refs_2_, bf16[1552,512]{1,0:T(8,128)(2,1)} %collective-permute-done.8.refs_7_.refs_3_, ...), custom_call_target="tpu_custom_call" | custom-call | flops 6442450944 | bytes 27262976 | tf_op jit(solution)/shard_map/pallas_call | solution.py:545
  145.0 3.5 %shard_map.82.refs_8_.refs_0_ = bf16[3088,512]{1,0:T(8,128)(2,1)} custom-call(s32[1]{0:T(128)} %dynamic_slice.12.flag_ref, bf16[3088,512]{1,0:T(8,128)(2,1)} %collective-permute-done.6.a_ref.b_ref, bf16[3088,512]{1,0:T(8,128)(2,1)} %collective-permute-done.6.a_ref.b_ref, f32[3072,512]{1,0:T(8,128)} %shard_map.81.refs_0_.refs_7_), custom_call_target="tpu_custom_call" | custom-call | bytes 6324224 | tf_op jit(solution)/shard_map/pallas_call | solution.py:401
  149.0 2.7 collective-permute-start.11
  151.6 14.4 %shard_map.83 = (f32[3072,512]{1,0:T(8,128)}, bf16[3088,512]{1,0:T(8,128)(2,1)}) custom-call(bf16[3088,512]{1,0:T(8,128)(2,1)} %get-tuple-element.35.refs_0_.refs_2_, bf16[3088,512]{1,0:T(8,128)(2,1)} %copy-done.3, bf16[3088,512]{1,0:T(8,128)(2,1)} %get-tuple-element.38.refs_2_.refs_4_, bf16[3088,512]{1,0:T(8,128)(2,1)} %collective-permute-done.9.refs_3_.refs_5_, ...), custom_call_target="tpu_custom_call" | custom-call | flops 6442450944 | bytes 20971520 | tf_op jit(solution)/shard_map/pallas_call | solution.py:545
  166.0 1.5 collective-permute-start.13
  167.5 1.6 copy-done.2
  169.1 12.7 %shard_map.84.refs_4_.refs_3_ = bf16[4,512,512]{2,1,0:T(8,128)(2,1)} custom-call(f32[12,3]{1,0:T(8,128)} %copy.56.scalars, bf16[3088,512]{1,0:T(8,128)(2,1)} %shard_map.82.refs_8_.refs_0_, bf16[3088,512]{1,0:T(8,128)(2,1)} %copy-done.2, bf16[512,3072]{1,0:T(8,128)(2,1)} %bitcast.25, bf16[512,1536]{1,0:T(8,128)(2,1)} %copy.61.refs_9_.refs_3_.refs_2_, ...), custom_call_target="tpu_custom_call" | custom-call | flops 6442450944 | bytes 14680064 | tf_op jit(solution)/shard_map/pallas_call | solution.py:256
  181.8 4.5 %collective-permute-done.11.refs_0_.refs_2_ = bf16[3088,512]{1,0:T(8,128)(2,1)S(1)} collective-permute-done((bf16[3088,512]{1,0:T(8,128)(2,1)}, bf16[3088,512]{1,0:T(8,128)(2,1)S(1)}, u32[]{:S(2)}, u32[]{:S(2)}) %collective-permute-start.11) | collective-permute-done | bytes 3162144 | tf_op jit(solution)/shard_map/ppermute | solution.py:578
  186.3 1.7 copy-done.1
  188.0 6.8 %shard_map.85.refs_5_.refs_6_ = bf16[1,512,512]{2,1,0:T(8,128)(2,1)} custom-call(f32[12,3]{1,0:T(8,128)} %copy.56.scalars, bf16[3088,512]{1,0:T(8,128)(2,1)} %copy-done.1, bf16[512,3072]{1,0:T(8,128)(2,1)} %bitcast.26, bf16[512,1536]{1,0:T(8,128)(2,1)} %copy.61.refs_9_.refs_3_.refs_2_, bf16[512,1536]{1,0:T(8,128)(2,1)} %copy.62.refs_10_.refs_4_.refs_3_, ...), custom_call_target="tpu_custom_call" | custom-call | flops 1610612736 | bytes 9961472 | tf_op jit(solution)/shard_map/pallas_call | solution.py:256
  194.9 8.9 %shard_map.86 = (bf16[1536,512]{1,0:T(8,128)(2,1)}, bf16[3088,512]{1,0:T(8,128)(2,1)}) custom-call(bf16[3088,512]{1,0:T(8,128)(2,1)} %shard_map.82.refs_8_.refs_0_, bf16[3088,512]{1,0:T(8,128)(2,1)} %copy-done.2, bf16[3088,512]{1,0:T(8,128)(2,1)} %copy-done.1, bf16[4,512,512]{2,1,0:T(8,128)(2,1)} %shard_map.84.refs_4_.refs_3_, ...), custom_call_target="tpu_custom_call" | custom-call | flops 2415919104 | bytes 11010048 | tf_op jit(solution)/shard_map/pallas_call | solution.py:545
  203.7 3.6 %collective-permute-start.12 = (bf16[3088,512]{1,0:T(8,128)(2,1)}, bf16[3088,512]{1,0:T(8,128)(2,1)S(1)}, u32[]{:S(2)}, u32[]{:S(2)}) collective-permute-start(bf16[3088,512]{1,0:T(8,128)(2,1)} %get-tuple-element.40), channel_id=1, source_target_pairs={{0,8},{2,4},{4,2},{6,30},{8,16},{10,12},{12,10},{14,6},{16,24},{18... | collective-permute-start | bytes 9486344 | tf_op jit(solution)/shard_map/ppermute | solution.py:578
  207.4 1.2 collective-permute-start.17
  208.6 7.8 %shard_map.87.refs_2_ = bf16[1536,512]{1,0:T(8,128)(2,1)} custom-call(bf16[3088,512]{1,0:T(8,128)(2,1)} %shard_map.82.refs_8_.refs_0_, bf16[3088,512]{1,0:T(8,128)(2,1)} %copy-done.2, bf16[3088,512]{1,0:T(8,128)(2,1)} %copy-done.1, bf16[4,512,512]{2,1,0:T(8,128)(2,1)} %shard_map.84.refs_4_.refs_3_, bf16[4,512,512]{2,1,0:T(8,128)(2,1)} %shard_map.84.refs_4_.refs_3_, ...), custom_call_target="tpu_custom_call" | custom-call | flops 2415919104 | bytes 11010048 | tf_op jit(solution)/shard_map/pallas_call | solution.py:545
  216.4 6.8 %shard_map.88.refs_5_.refs_6_ = bf16[1,512,512]{2,1,0:T(8,128)(2,1)} custom-call(f32[12,3]{1,0:T(8,128)} %copy.56.scalars, bf16[3088,512]{1,0:T(8,128)(2,1)} %copy-done.1, bf16[512,3072]{1,0:T(8,128)(2,1)} %bitcast.27, bf16[1536,512]{1,0:T(8,128)(2,1)} %shard_map.87.refs_2_, f32[2,512,1]{2,1,0:T(8,128)} %copy.57.refs_3_.refs_4_.refs_12_.refs_6_.refs_5_.refs_7_, ...), custom_call_target="tpu_custom_call" | custom-call | flops 1610612736 | bytes 6815744 | tf_op jit(solution)/shard_map/pallas_call | solution.py:256
  223.2 12.8 %shard_map.89.refs_0_.refs_9_ = f32[3072,512]{1,0:T(8,128)} custom-call(bf16[3088,512]{1,0:T(8,128)(2,1)} %shard_map.82.refs_8_.refs_0_, bf16[3088,512]{1,0:T(8,128)(2,1)} %copy-done.2, bf16[3088,512]{1,0:T(8,128)(2,1)} %copy-done.1, bf16[4,512,512]{2,1,0:T(8,128)(2,1)} %shard_map.84.refs_4_.refs_3_, bf16[4,512,512]{2,1,0:T(8,128)(2,1)} %shard_map.84.refs_4_.refs_3_, ...), custom_call_target="tpu_custom_call" | custom-call | flops 4831838208 | bytes 23592960 | tf_op jit(solution)/shard_map/pallas_call | solution.py:545
  236.1 3.5 %shard_map.90 = (bf16[1024,512]{1,0:T(8,128)(2,1)}, bf16[1024,512]{1,0:T(8,128)(2,1)}, bf16[1040,512]{1,0:T(8,128)(2,1)}) custom-call(s32[1]{0:T(128)} %dynamic_slice.12.flag_ref, bf16[3088,512]{1,0:T(8,128)(2,1)} %collective-permute-done.13.a_ref.b_ref, bf16[3088,512]{1,0:T(8,128)(2,1)} %collective-permute-done.13.a_ref.b_ref, ...), custom_call_target="tpu_custom_call" | custom-call | bytes 6324224 | tf_op jit(solution)/shard_map/pallas_call | solution.py:401
  242.3 6.8 %shard_map.91.refs_1_.refs_6_ = bf16[1,512,512]{2,1,0:T(8,128)(2,1)} custom-call(f32[12,3]{1,0:T(8,128)} %copy.56.scalars, bf16[1024,512]{1,0:T(8,128)(2,1)} %get-tuple-element.43.refs_0_.refs_4_, bf16[1024,512]{1,0:T(8,128)(2,1)} %get-tuple-element.44.refs_1_.refs_5_, bf16[1040,512]{1,0:T(8,128)(2,1)} %get-tuple-element.45.refs_2_.refs_6_, ...), custom_call_target="tpu_custom_call" | custom-call | flops 1610612736 | bytes 6815744 | tf_op jit(solution)/shard_map/pallas_call | solution.py:256
  249.7 6.8 %shard_map.93.refs_7_.refs_8_ = bf16[1,512,512]{2,1,0:T(8,128)(2,1)} custom-call(f32[12,3]{1,0:T(8,128)} %copy.56.scalars, bf16[1024,512]{1,0:T(8,128)(2,1)} %collective-permute-done.14.refs_0_.refs_3_, bf16[1024,512]{1,0:T(8,128)(2,1)} %collective-permute-done.15.refs_1_.refs_4_, bf16[1040,512]{1,0:T(8,128)(2,1)} %collective-permute-done.16.refs_2_.refs_5_, ...), custom_call_target="tpu_custom_call" | custom-call | flops 1610612736 | bytes 6815744 | tf_op jit(solution)/shard_map/pallas_call | solution.py:256
  256.5 11.5 %shard_map.94.refs_0_.refs_9_ = f32[3072,512]{1,0:T(8,128)} custom-call(bf16[1024,512]{1,0:T(8,128)(2,1)} %get-tuple-element.43.refs_0_.refs_4_, bf16[1024,512]{1,0:T(8,128)(2,1)} %get-tuple-element.44.refs_1_.refs_5_, bf16[1040,512]{1,0:T(8,128)(2,1)} %get-tuple-element.45.refs_2_.refs_6_, bf16[1024,512]{1,0:T(8,128)(2,1)} %collective-permute-done.14.refs_0_.refs_3_, ...), custom_call_target="tpu_custom_call" | custom-call | flops 3221225472 | bytes 19922944 | tf_op jit(solution)/shard_map/pallas_call | solution.py:545
  268.1 1.7 copy-done.6
  269.7 3.5 %shard_map.95 = (bf16[1024,512]{1,0:T(8,128)(2,1)}, bf16[1024,512]{1,0:T(8,128)(2,1)}, bf16[1040,512]{1,0:T(8,128)(2,1)}) custom-call(s32[1]{0:T(128)} %dynamic_slice.12.flag_ref, bf16[3088,512]{1,0:T(8,128)(2,1)} %copy-done.6, bf16[3088,512]{1,0:T(8,128)(2,1)} %copy-done.6, f32[3072,512]{1,0:T(8,128)} %shard_map.94.refs_0_.refs_9_), custom_call_target="tpu_custom_call" | custom-call | bytes 6324224 | tf_op jit(solution)/shard_map/pallas_call | solution.py:401
  273.9 6.8 %shard_map.96.refs_1_.refs_6_ = bf16[1,512,512]{2,1,0:T(8,128)(2,1)} custom-call(f32[12,3]{1,0:T(8,128)} %copy.56.scalars, bf16[1024,512]{1,0:T(8,128)(2,1)} %get-tuple-element.46.refs_0_.refs_4_, bf16[1024,512]{1,0:T(8,128)(2,1)} %get-tuple-element.47.refs_1_.refs_5_, bf16[1040,512]{1,0:T(8,128)(2,1)} %get-tuple-element.48.refs_2_.refs_6_, ...), custom_call_target="tpu_custom_call" | custom-call | flops 1610612736 | bytes 6815744 | tf_op jit(solution)/shard_map/pallas_call | solution.py:256
  283.7 6.8 %shard_map.98.refs_7_.refs_8_ = bf16[1,512,512]{2,1,0:T(8,128)(2,1)} custom-call(f32[12,3]{1,0:T(8,128)} %copy.56.scalars, bf16[1024,512]{1,0:T(8,128)(2,1)} %copy-done.8, bf16[1024,512]{1,0:T(8,128)(2,1)} %copy-done.9, bf16[1040,512]{1,0:T(8,128)(2,1)} %copy-done.7, bf16[512,3072]{1,0:T(8,128)(2,1)} %bitcast.31, f32[8,128]{1,0:T(8,128)} %shard_map.97.refs_4_, ...), custom_call_target="tpu_custom_call" | custom-call | flops 1610612736 | bytes 6815744 | tf_op jit(solution)/shard_map/pallas_call | solution.py:256
  290.4 12.2 %shard_map.99 = f32[3072,512]{1,0:T(8,128)} custom-call(bf16[1024,512]{1,0:T(8,128)(2,1)} %get-tuple-element.46.refs_0_.refs_4_, bf16[1024,512]{1,0:T(8,128)(2,1)} %get-tuple-element.47.refs_1_.refs_5_, bf16[1040,512]{1,0:T(8,128)(2,1)} %get-tuple-element.48.refs_2_.refs_6_, bf16[1024,512]{1,0:T(8,128)(2,1)} %copy-done.8, bf16[1024,512]{1,0:T(8,128)(2,1)} %copy-done.9, ...), custom_call_target="tpu_custom_call" | custom-call | flops 3221225472 | bytes 26214400 | tf_op jit(solution)/shard_map/pallas_call | solution.py:545
  (72 shorter events, 15.7 us)
Async XLA Ops:
  1.3 3.7 %copy-start.14 = (s32[16]{0:T(128)S(1)}, s32[16]{0:T(128)}, u32[]{:S(2)}) copy-start(s32[16]{0:T(128)} %constant.53.clone) | copy-start | bytes 196
  4.3 17.4 %collective-permute-start.2 = (bf16[3088,512]{1,0:T(8,128)(2,1)}, bf16[3088,512]{1,0:T(8,128)(2,1)}, u32[]{:S(2)}, u32[]{:S(2)}) collective-permute-start(bf16[3088,512]{1,0:T(8,128)(2,1)} %shard_map.73.a_ref.b_ref.refs_0_.refs_9_), channel_id=1, source_target_pairs={{0,2},{2,0},{4,6},{6,4},{8,10},{10,8},{12,14},{14,12},{16,18},{18,... | collective-permute-start | bytes 9486344 | tf_op jit(solution)/shard_map/ppermute | solution.py:578
  5.0 39.0 %collective-permute-start = (bf16[3088,512]{1,0:T(8,128)(2,1)}, bf16[3088,512]{1,0:T(8,128)(2,1)}, u32[]{:S(2)}, u32[]{:S(2)}) collective-permute-start(bf16[3088,512]{1,0:T(8,128)(2,1)} %shard_map.73.a_ref.b_ref.refs_0_.refs_9_), channel_id=1, source_target_pairs={{0,6},{2,26},{4,12},{6,0},{8,14},{10,2},{12,20},{14,8},{16,22},{18... | collective-permute-start | bytes 9486344 | tf_op jit(solution)/shard_map/ppermute | solution.py:578
  5.7 5.3 %copy-start = (bf16[3088,512]{1,0:T(8,128)(2,1)S(1)}, bf16[3088,512]{1,0:T(8,128)(2,1)}, u32[]{:S(2)}) copy-start(bf16[3088,512]{1,0:T(8,128)(2,1)} %shard_map.73.a_ref.b_ref.refs_0_.refs_9_) | copy-start | bytes 9486340
  9.4 34.6 %collective-permute-start.1 = (bf16[1536,512]{1,0:T(8,128)(2,1)}, bf16[1536,512]{1,0:T(8,128)(2,1)}, u32[]{:S(2)}, u32[]{:S(2)}) collective-permute-start(bf16[1536,512]{1,0:T(8,128)(2,1)} %get-tuple-element.33), channel_id=1, source_target_pairs={{0,1},{1,0},{2,3},{3,2},{4,5},{5,4},{6,7},{7,6},{8,9},{9,8},{10,11... | collective-permute-start | bytes 4718600 | tf_op jit(solution)/shard_map/ppermute | solution.py:594
  10.9 2.5 copy-start.11
  10.9 3.9 %copy-start.12 = (f32[16]{0:T(128)S(1)}, f32[16]{0:T(128)}, u32[]{:S(2)}) copy-start(f32[16]{0:T(128)} %param.11) | copy-start | bytes 196
  11.0 3.9 %copy-start.13 = (s32[16]{0:T(128)S(1)}, s32[16]{0:T(128)}, u32[]{:S(2)}) copy-start(s32[16]{0:T(128)} %param.10) | copy-start | bytes 196
  49.6 6.7 %collective-permute-start.4 = (bf16[3088,512]{1,0:T(8,128)(2,1)}, bf16[3088,512]{1,0:T(8,128)(2,1)S(1)}, u32[]{:S(2)}, u32[]{:S(2)}) collective-permute-start(bf16[3088,512]{1,0:T(8,128)(2,1)} %get-tuple-element.35.refs_0_.refs_2_), channel_id=1, source_target_pairs={{0,2},{2,0},{4,6},{6,4},{8,10},{10,8},{12,14},{14,12},{16,18},{18,... | collective-permute-start | bytes 9486344 | tf_op jit(solution)/shard_map/ppermute | solution.py:578
  50.8 39.1 %collective-permute-start.3 = (bf16[3088,512]{1,0:T(8,128)(2,1)}, bf16[3088,512]{1,0:T(8,128)(2,1)S(1)}, u32[]{:S(2)}, u32[]{:S(2)}) collective-permute-start(bf16[3088,512]{1,0:T(8,128)(2,1)} %get-tuple-element.34.refs_3_), channel_id=1, source_target_pairs={{0,24},{2,4},{4,2},{6,14},{8,0},{10,12},{12,10},{14,22},{16,8},{18... | collective-permute-start | bytes 9486344 | tf_op jit(solution)/shard_map/ppermute | solution.py:578
  52.3 35.1 %collective-permute-start.5 = (bf16[1552,512]{1,0:T(8,128)(2,1)}, bf16[1552,512]{1,0:T(8,128)(2,1)S(1)}, u32[]{:S(2)}, u32[]{:S(2)}) collective-permute-start(bf16[1552,512]{1,0:T(8,128)(2,1)} %get-tuple-element.36), channel_id=1, source_target_pairs={{0,1},{1,0},{2,3},{3,2},{4,5},{5,4},{6,7},{7,6},{8,9},{9,8},{10,11... | collective-permute-start | bytes 4767752 | tf_op jit(solution)/shard_map/ppermute | solution.py:594
  56.3 1.7 copy-start.3
  87.4 2.5 copy-start.4
  89.9 1.7 copy-start.10
  96.3 5.7 %copy-start.5 = (bf16[1552,512]{1,0:T(8,128)(2,1)S(1)}, bf16[1552,512]{1,0:T(8,128)(2,1)}, u32[]{:S(2)}) copy-start(bf16[1552,512]{1,0:T(8,128)(2,1)} %copy-done.4) | copy-start | bytes 4767748
  96.3 12.6 %collective-permute-start.9 = (bf16[3088,512]{1,0:T(8,128)(2,1)}, bf16[3088,512]{1,0:T(8,128)(2,1)}, u32[]{:S(2)}, u32[]{:S(2)}) collective-permute-start(bf16[3088,512]{1,0:T(8,128)(2,1)} %get-tuple-element.38.refs_2_.refs_4_), channel_id=1, source_target_pairs={{0,2},{2,0},{4,6},{6,4},{8,10},{10,8},{12,14},{14,12},{16,18},{18,... | collective-permute-start | bytes 9486344 | tf_op jit(solution)/shard_map/ppermute | solution.py:578
  98.7 10.2 %collective-permute-start.8 = (bf16[1552,512]{1,0:T(8,128)(2,1)}, bf16[1552,512]{1,0:T(8,128)(2,1)}, u32[]{:S(2)}, u32[]{:S(2)}) collective-permute-start(bf16[1552,512]{1,0:T(8,128)(2,1)} %copy-done.4), channel_id=1, source_target_pairs={{0,2},{2,0},{4,6},{6,4},{8,10},{10,8},{12,14},{14,12},{16,18},{18,... | collective-permute-start | bytes 4767752 | tf_op jit(solution)/shard_map/ppermute | solution.py:578
  98.8 10.1 %collective-permute-start.7 = (bf16[1536,512]{1,0:T(8,128)(2,1)}, bf16[1536,512]{1,0:T(8,128)(2,1)}, u32[]{:S(2)}, u32[]{:S(2)}) collective-permute-start(bf16[1536,512]{1,0:T(8,128)(2,1)} %collective-permute-done.1.refs_0_.refs_1_.refs_4_.refs_7_), channel_id=1, source_target_pairs={{0,2},{2,0},{4,6},{6,4},{8,10},{10,8},{12,14},{14,12},{16,18},{18,... | collective-permute-start | bytes 4718600 | tf_op jit(solution)/shard_map/ppermute | solution.py:578
  99.2 45.8 %collective-permute-start.6 = (bf16[3088,512]{1,0:T(8,128)(2,1)}, bf16[3088,512]{1,0:T(8,128)(2,1)}, u32[]{:S(2)}, u32[]{:S(2)}) collective-permute-start(bf16[3088,512]{1,0:T(8,128)(2,1)} %get-tuple-element.37.refs_11_), channel_id=1, source_target_pairs={{0,6},{2,10},{4,28},{6,0},{8,14},{10,18},{12,4},{14,8},{16,22},{18... | collective-permute-start | bytes 9486344 | tf_op jit(solution)/shard_map/ppermute | solution.py:578
  148.5 19.0 %collective-permute-start.10 = (bf16[3088,512]{1,0:T(8,128)(2,1)}, bf16[3088,512]{1,0:T(8,128)(2,1)S(1)}, u32[]{:S(2)}, u32[]{:S(2)}) collective-permute-start(bf16[3088,512]{1,0:T(8,128)(2,1)} %shard_map.82.refs_8_.refs_0_), channel_id=1, source_target_pairs={{0,2},{2,0},{4,6},{6,4},{8,10},{10,8},{12,14},{14,12},{16,18},{18,... | collective-permute-start | bytes 9486344 | tf_op jit(solution)/shard_map/ppermute | solution.py:578
  149.0 37.4 %collective-permute-start.11 = (bf16[3088,512]{1,0:T(8,128)(2,1)}, bf16[3088,512]{1,0:T(8,128)(2,1)S(1)}, u32[]{:S(2)}, u32[]{:S(2)}) collective-permute-start(bf16[3088,512]{1,0:T(8,128)(2,1)} %shard_map.82.refs_8_.refs_0_), channel_id=1, source_target_pairs={{0,8},{2,4},{4,2},{6,30},{8,16},{10,12},{12,10},{14,6},{16,24},{18... | collective-permute-start | bytes 9486344 | tf_op jit(solution)/shard_map/ppermute | solution.py:578
  166.0 70.1 %collective-permute-start.13 = (bf16[3088,512]{1,0:T(8,128)(2,1)}, bf16[3088,512]{1,0:T(8,128)(2,1)}, u32[]{:S(2)}, u32[]{:S(2)}) collective-permute-start(bf16[3088,512]{1,0:T(8,128)(2,1)} %get-tuple-element.41), channel_id=1, source_target_pairs={{0,8},{2,4},{4,2},{6,30},{8,16},{10,12},{12,10},{14,6},{16,24},{18... | collective-permute-start | bytes 9486344 | tf_op jit(solution)/shard_map/ppermute | solution.py:578
  167.5 1.6 copy-start.2
  186.3 1.7 copy-start.1
  203.7 64.3 %collective-permute-start.12 = (bf16[3088,512]{1,0:T(8,128)(2,1)}, bf16[3088,512]{1,0:T(8,128)(2,1)S(1)}, u32[]{:S(2)}, u32[]{:S(2)}) collective-permute-start(bf16[3088,512]{1,0:T(8,128)(2,1)} %get-tuple-element.40), channel_id=1, source_target_pairs={{0,8},{2,4},{4,2},{6,30},{8,16},{10,12},{12,10},{14,6},{16,24},{18... | collective-permute-start | bytes 9486344 | tf_op jit(solution)/shard_map/ppermute | solution.py:578
  207.4 33.7 %collective-permute-start.17 = (bf16[1536,512]{1,0:T(8,128)(2,1)}, bf16[1536,512]{1,0:T(8,128)(2,1)}, u32[]{:S(2)}, u32[]{:S(2)}) collective-permute-start(bf16[1536,512]{1,0:T(8,128)(2,1)} %get-tuple-element.42.refs_6_), channel_id=1, source_target_pairs={{0,1},{1,0},{2,3},{3,2},{4,5},{5,4},{6,7},{7,6},{8,9},{9,8},{10,11... | collective-permute-start | bytes 4718600 | tf_op jit(solution)/shard_map/ppermute | solution.py:594
  239.6 10.1 %collective-permute-start.16 = (bf16[1040,512]{1,0:T(8,128)(2,1)}, bf16[1040,512]{1,0:T(8,128)(2,1)}, u32[]{:S(2)}, u32[]{:S(2)}) collective-permute-start(bf16[1040,512]{1,0:T(8,128)(2,1)} %get-tuple-element.45.refs_2_.refs_6_), channel_id=1, source_target_pairs={{0,2},{2,0},{4,6},{6,4},{8,10},{10,8},{12,14},{14,12},{16,18},{18,... | collective-permute-start | bytes 3194888 | tf_op jit(solution)/shard_map/ppermute | solution.py:578
  239.7 10.0 %collective-permute-start.14 = (bf16[1024,512]{1,0:T(8,128)(2,1)}, bf16[1024,512]{1,0:T(8,128)(2,1)}, u32[]{:S(2)}, u32[]{:S(2)}) collective-permute-start(bf16[1024,512]{1,0:T(8,128)(2,1)} %get-tuple-element.43.refs_0_.refs_4_), channel_id=1, source_target_pairs={{0,2},{2,0},{4,6},{6,4},{8,10},{10,8},{12,14},{14,12},{16,18},{18,... | collective-permute-start | bytes 3145736 | tf_op jit(solution)/shard_map/ppermute | solution.py:578
  240.2 9.6 %collective-permute-start.15 = (bf16[1024,512]{1,0:T(8,128)(2,1)}, bf16[1024,512]{1,0:T(8,128)(2,1)}, u32[]{:S(2)}, u32[]{:S(2)}) collective-permute-start(bf16[1024,512]{1,0:T(8,128)(2,1)} %get-tuple-element.44.refs_1_.refs_5_), channel_id=1, source_target_pairs={{0,2},{2,0},{4,6},{6,4},{8,10},{10,8},{12,14},{14,12},{16,18},{18,... | collective-permute-start | bytes 3145736 | tf_op jit(solution)/shard_map/ppermute | solution.py:578
  241.1 39.6 %collective-permute-start.21 = (bf16[1536,512]{1,0:T(8,128)(2,1)}, bf16[1536,512]{1,0:T(8,128)(2,1)}, u32[]{:S(2)}, u32[]{:S(2)}) collective-permute-start(bf16[1536,512]{1,0:T(8,128)(2,1)} %shard_map.87.refs_2_), channel_id=1, source_target_pairs={{0,1},{1,0},{2,3},{3,2},{4,5},{5,4},{6,7},{7,6},{8,9},{9,8},{10,11... | collective-permute-start | bytes 4718600 | tf_op jit(solution)/shard_map/ppermute | solution.py:594
  268.1 1.7 copy-start.6
  273.2 8.1 %collective-permute-start.20 = (bf16[1040,512]{1,0:T(8,128)(2,1)}, bf16[1040,512]{1,0:T(8,128)(2,1)S(1)}, u32[]{:S(2)}, u32[]{:S(2)}) collective-permute-start(bf16[1040,512]{1,0:T(8,128)(2,1)} %get-tuple-element.48.refs_2_.refs_6_), channel_id=1, source_target_pairs={{0,2},{2,0},{4,6},{6,4},{8,10},{10,8},{12,14},{14,12},{16,18},{18,... | collective-permute-start | bytes 3194888 | tf_op jit(solution)/shard_map/ppermute | solution.py:578
  273.3 8.0 %collective-permute-start.18 = (bf16[1024,512]{1,0:T(8,128)(2,1)}, bf16[1024,512]{1,0:T(8,128)(2,1)S(1)}, u32[]{:S(2)}, u32[]{:S(2)}) collective-permute-start(bf16[1024,512]{1,0:T(8,128)(2,1)} %get-tuple-element.46.refs_0_.refs_4_), channel_id=1, source_target_pairs={{0,2},{2,0},{4,6},{6,4},{8,10},{10,8},{12,14},{14,12},{16,18},{18,... | collective-permute-start | bytes 3145736 | tf_op jit(solution)/shard_map/ppermute | solution.py:578
  273.8 7.5 %collective-permute-start.19 = (bf16[1024,512]{1,0:T(8,128)(2,1)}, bf16[1024,512]{1,0:T(8,128)(2,1)S(1)}, u32[]{:S(2)}, u32[]{:S(2)}) collective-permute-start(bf16[1024,512]{1,0:T(8,128)(2,1)} %get-tuple-element.47.refs_1_.refs_5_), channel_id=1, source_target_pairs={{0,2},{2,0},{4,6},{6,4},{8,10},{10,8},{12,14},{14,12},{16,18},{18,... | collective-permute-start | bytes 3145736 | tf_op jit(solution)/shard_map/ppermute | solution.py:578
  281.3 1.1 copy-start.8
  281.3 1.4 copy-start.9
  282.7 1.0 copy-start.7
